TPU v7x, 32 devices: a whole 2x2x4 slice. The times are simulated.
32 devices in a mesh: dp: 4 (over y, x), fsdp: 8 (over z, core).
Axes of the slice: x: 2, y: 2, z: 4, core: 2. Of those that a mesh axis runs over, the one named last changes fastest.
Arguments:
- latents: float32 [32, 256, 1024], P(('dp', 'fsdp'))
- pixels: bfloat16 [32, 512, 1024], P(('dp', 'fsdp')), may hold values from -6 to 6
- slot_index: int32 [32], P(('dp', 'fsdp')), may hold values from 0 to 31, as said below
- counts: int32 [32], P(('dp', 'fsdp')), may hold values from 128 to 512, as said below
- cotangent: float32 [32, 256, 1024], P(('dp', 'fsdp')), may hold values from -6 to 6
- gain_q: bfloat16 [1024], P(('dp', 'fsdp')), may hold values from 0.5 to 1.5
- gain_kv: bfloat16 [1024], P(('dp', 'fsdp')), may hold values from 0.5 to 1.5
- w_query: bfloat16 [1024, 1024], P(('dp', 'fsdp')), may hold values from -0.1875 to 0.1875
- w_key: bfloat16 [1024, 1024], P(('dp', 'fsdp')), may hold values from -0.1875 to 0.1875
- w_value: bfloat16 [1024, 1024], P(('dp', 'fsdp')), may hold values from -0.1875 to 0.1875
- w_out: bfloat16 [1024, 1024], P(('dp', 'fsdp')), may hold values from -3.5 to 3.5
- gain_self: bfloat16 [1024], P(('dp', 'fsdp')), may hold values from 0.5 to 1.5
- w_qkv: bfloat16 [1024, 3072], P(('dp', 'fsdp')), may hold values from -0.1875 to 0.1875
- w_self_out: bfloat16 [1024, 1024], P(('dp', 'fsdp')), may hold values from -3 to 3
- gain_mlp: bfloat16 [1024], P(('dp', 'fsdp')), may hold values from 0.5 to 1.5
- w_up: bfloat16 [1024, 4096], P(('dp', 'fsdp')), may hold values from -0.1875 to 0.1875
- w_down: bfloat16 [4096, 1024], P(('dp', 'fsdp')), may hold values from -0.09375 to 0.09375
Outputs:
- latents_out: float32 [32, 256, 1024], P(('dp', 'fsdp'))
- latents_grad: float32 [32, 256, 1024], P(('dp', 'fsdp'))
- pixels_grad: float32 [32, 512, 1024], P(('dp', 'fsdp'))
- gain_q_grad: float32 [1024], P(('dp', 'fsdp'))
- gain_kv_grad: float32 [1024], P(('dp', 'fsdp'))
- w_query_grad: float32 [1024, 1024], P(('dp', 'fsdp'))
- w_key_grad: float32 [1024, 1024], P(('dp', 'fsdp'))
- w_value_grad: float32 [1024, 1024], P(('dp', 'fsdp'))
- w_out_grad: float32 [1024, 1024], P(('dp', 'fsdp'))
- gain_self_grad: float32 [1024], P(('dp', 'fsdp'))
- w_qkv_grad: float32 [1024, 3072], P(('dp', 'fsdp'))
- w_self_out_grad: float32 [1024, 1024], P(('dp', 'fsdp'))
- gain_mlp_grad: float32 [1024], P(('dp', 'fsdp'))
- w_up_grad: float32 [1024, 4096], P(('dp', 'fsdp'))
- w_down_grad: float32 [4096, 1024], P(('dp', 'fsdp'))
- norms: float32 [32], P(('dp', 'fsdp'))
Inputs may be any that keep to these rules, and one draw needn't show every extreme that they name: Group i reads pixel block i (slot_index[i] = i), which lies on the same device. The first counts[b] slots of pixel block b are visible, the rest are padding; some block has all 512 slots visible.
All inputs are finite; a program needn't handle non-finite values.
Results may differ from a plain program's by a relative error of at most 0.018.
Values may be sent and summed in bfloat16 or wider, within the bound.
A program may use at most 256 MiB of HBM per device.

v0:
```python
import jax
import jax.numpy as jnp
from jax import lax
from jax.sharding import PartitionSpec as P

HEADS = 8


EPS = 1e-05


def layer_norm(inputs, gain):
    center = inputs - jnp.mean(inputs, axis=-1, keepdims=True)
    spread = jnp.mean(center * center, axis=-1, keepdims=True)
    return center * lax.rsqrt(spread + EPS) * gain


def project(inputs, matrix):
    return jnp.einsum("gld,de->gle", inputs, matrix, preferred_element_type=jnp.float32)


def project_back(grad_rows, matrix):
    return jnp.einsum("gle,de->gld", grad_rows, matrix, preferred_element_type=jnp.float32)


def weight_grad(inputs, grad_rows):
    return jnp.einsum("gld,gle->de", inputs, grad_rows, preferred_element_type=jnp.float32)


def split_heads(tensor):
    return tensor.reshape(tensor.shape[0], tensor.shape[1], HEADS, -1)


def merge_heads(tensor):
    return tensor.reshape(tensor.shape[0], tensor.shape[1], -1)


def scores_of(queries, key_rows, visible):
    scores = jnp.einsum("glhd,gshd->ghls", queries, key_rows, preferred_element_type=jnp.float32)
    scores = scores * queries.shape[-1] ** (-0.5)
    if visible is not None:
        scores = jnp.where(visible[:, None, None, :], scores, -1e30)
    return scores


def attend_forward(queries, key_rows, value_rows, visible):
    scores = scores_of(queries, key_rows, visible)
    largest = jnp.max(scores, axis=-1, keepdims=True)
    exp_scores = jnp.exp(scores - largest)
    totals = jnp.sum(exp_scores, axis=-1, keepdims=True)
    attn_probs = exp_scores / totals
    log_total = largest + jnp.log(totals)
    mixed = jnp.einsum(
        "ghls,gshd->glhd",
        attn_probs.astype(jnp.bfloat16),
        value_rows,
        preferred_element_type=jnp.float32,
    ).astype(jnp.bfloat16)
    return (mixed, log_total)


def attend_backward(queries, key_rows, value_rows, visible, log_total, mixed_grad):
    scale = queries.shape[-1] ** (-0.5)
    attn_probs = jnp.exp(scores_of(queries, key_rows, visible) - log_total)
    probs_grad = jnp.einsum(
        "glhd,gshd->ghls", mixed_grad, value_rows, preferred_element_type=jnp.float32
    )
    value_grad = jnp.einsum(
        "ghls,glhd->gshd",
        attn_probs.astype(jnp.bfloat16),
        mixed_grad,
        preferred_element_type=jnp.float32,
    ).astype(jnp.bfloat16)
    score_grad = attn_probs * (
        probs_grad - jnp.sum(probs_grad * attn_probs, axis=-1, keepdims=True)
    )
    score_grad = score_grad.astype(jnp.bfloat16)
    query_grad = (
        jnp.einsum("ghls,gshd->glhd", score_grad, key_rows, preferred_element_type=jnp.float32)
        * scale
    ).astype(jnp.bfloat16)
    key_grad = (
        jnp.einsum("ghls,glhd->gshd", score_grad, queries, preferred_element_type=jnp.float32)
        * scale
    ).astype(jnp.bfloat16)
    return (query_grad, key_grad, value_grad)


def local(
    latents,
    pixels,
    slot_index,
    counts,
    cotangent,
    gain_q,
    gain_kv,
    w_query,
    w_key,
    w_value,
    w_out,
    gain_self,
    w_qkv,
    w_self_out,
    gain_mlp,
    w_up,
    w_down,
):
    groups = latents.shape[0]
    slots = pixels.shape[1]
    width = latents.shape[2]
    local_slot = slot_index % groups
    chosen = jnp.take(pixels, local_slot, axis=0).astype(jnp.float32)
    visible_count = jnp.take(counts, local_slot, axis=0)
    visible = lax.broadcasted_iota(jnp.int32, (groups, slots), 1) < visible_count[:, None]
    cross_all = (
        lax.all_gather(gain_q, ("dp", "fsdp"), axis=0, tiled=True),
        lax.all_gather(gain_kv, ("dp", "fsdp"), axis=0, tiled=True),
        lax.all_gather(w_query, ("dp", "fsdp"), axis=0, tiled=True),
        lax.all_gather(w_key, ("dp", "fsdp"), axis=0, tiled=True),
        lax.all_gather(w_value, ("dp", "fsdp"), axis=0, tiled=True),
        lax.all_gather(w_out, ("dp", "fsdp"), axis=0, tiled=True),
    )
    normed = layer_norm(latents, cross_all[0].astype(jnp.float32)).astype(jnp.bfloat16)
    pix_normed = layer_norm(chosen, cross_all[1].astype(jnp.float32)).astype(jnp.bfloat16)
    queries = split_heads(project(normed, cross_all[2]).astype(jnp.bfloat16))
    key_rows = split_heads(project(pix_normed, cross_all[3]).astype(jnp.bfloat16))
    value_rows = split_heads(project(pix_normed, cross_all[4]).astype(jnp.bfloat16))
    cross_mixed, cross_total = attend_forward(queries, key_rows, value_rows, visible)
    cross_flat = merge_heads(cross_mixed)
    after_cross = latents + project(cross_flat, cross_all[5])
    self_all = (
        lax.all_gather(gain_self, ("dp", "fsdp"), axis=0, tiled=True),
        lax.all_gather(w_qkv, ("dp", "fsdp"), axis=0, tiled=True),
        lax.all_gather(w_self_out, ("dp", "fsdp"), axis=0, tiled=True),
    )
    normed_self = layer_norm(after_cross, self_all[0].astype(jnp.float32)).astype(jnp.bfloat16)
    packed = project(normed_self, self_all[1]).astype(jnp.bfloat16)
    self_queries = split_heads(packed[..., :width])
    self_keys = split_heads(packed[..., width : 2 * width])
    self_values = split_heads(packed[..., 2 * width :])
    self_mixed, self_total = attend_forward(self_queries, self_keys, self_values, None)
    self_flat = merge_heads(self_mixed)
    after_self = after_cross + project(self_flat, self_all[2])
    mlp_all = (
        lax.all_gather(gain_mlp, ("dp", "fsdp"), axis=0, tiled=True),
        lax.all_gather(w_up, ("dp", "fsdp"), axis=0, tiled=True),
        lax.all_gather(w_down, ("dp", "fsdp"), axis=0, tiled=True),
    )
    normed_mlp = layer_norm(after_self, mlp_all[0].astype(jnp.float32)).astype(jnp.bfloat16)
    hidden = project(normed_mlp, mlp_all[1])
    activated = jax.nn.gelu(hidden).astype(jnp.bfloat16)
    latents_out = after_self + project(activated, mlp_all[2])
    root_mean = jnp.sqrt(jnp.mean(latents_out * latents_out, axis=(1, 2)))
    total_norm = lax.psum(jnp.sum(root_mean), ("dp", "fsdp"))
    norms = root_mean * (groups * lax.axis_size(("dp", "fsdp"))) / total_norm
    mlp_back = (
        lax.all_gather(gain_mlp, ("dp", "fsdp"), axis=0, tiled=True),
        lax.all_gather(w_up, ("dp", "fsdp"), axis=0, tiled=True),
        lax.all_gather(w_down, ("dp", "fsdp"), axis=0, tiled=True),
    )
    out_grad = cotangent.astype(jnp.bfloat16)
    down_grad = weight_grad(activated, out_grad)
    act_grad = project_back(out_grad, mlp_back[2])
    hidden_grad = jax.vjp(jax.nn.gelu, hidden)[1](act_grad)[0].astype(jnp.bfloat16)
    up_grad = weight_grad(normed_mlp, hidden_grad)
    mlp_in_grad = project_back(hidden_grad, mlp_back[1])
    after_self_ln, mlp_gain_grad = jax.vjp(layer_norm, after_self, mlp_back[0].astype(jnp.float32))[
        1
    ](mlp_in_grad)
    after_self_grad = cotangent + after_self_ln
    mlp_grads = (
        lax.psum_scatter(mlp_gain_grad, ("dp", "fsdp"), scatter_dimension=0, tiled=True),
        lax.psum_scatter(up_grad, ("dp", "fsdp"), scatter_dimension=0, tiled=True),
        lax.psum_scatter(down_grad, ("dp", "fsdp"), scatter_dimension=0, tiled=True),
    )
    self_back = (
        lax.all_gather(gain_self, ("dp", "fsdp"), axis=0, tiled=True),
        lax.all_gather(w_qkv, ("dp", "fsdp"), axis=0, tiled=True),
        lax.all_gather(w_self_out, ("dp", "fsdp"), axis=0, tiled=True),
    )
    self_branch = after_self_grad.astype(jnp.bfloat16)
    self_out_grad = weight_grad(self_flat, self_branch)
    self_mixed_grad = split_heads(project_back(self_branch, self_back[2]).astype(jnp.bfloat16))
    self_q_grad, self_k_grad, self_v_grad = attend_backward(
        self_queries, self_keys, self_values, None, self_total, self_mixed_grad
    )
    packed_grad = jnp.concatenate(
        [merge_heads(self_q_grad), merge_heads(self_k_grad), merge_heads(self_v_grad)], axis=-1
    )
    qkv_grad = weight_grad(normed_self, packed_grad)
    self_in_grad = project_back(packed_grad, self_back[1])
    after_cross_ln, self_gain_grad = jax.vjp(
        layer_norm, after_cross, self_back[0].astype(jnp.float32)
    )[1](self_in_grad)
    after_cross_grad = after_self_grad + after_cross_ln
    self_grads = (
        lax.psum_scatter(self_gain_grad, ("dp", "fsdp"), scatter_dimension=0, tiled=True),
        lax.psum_scatter(qkv_grad, ("dp", "fsdp"), scatter_dimension=0, tiled=True),
        lax.psum_scatter(self_out_grad, ("dp", "fsdp"), scatter_dimension=0, tiled=True),
    )
    cross_back = (
        lax.all_gather(gain_q, ("dp", "fsdp"), axis=0, tiled=True),
        lax.all_gather(gain_kv, ("dp", "fsdp"), axis=0, tiled=True),
        lax.all_gather(w_query, ("dp", "fsdp"), axis=0, tiled=True),
        lax.all_gather(w_key, ("dp", "fsdp"), axis=0, tiled=True),
        lax.all_gather(w_value, ("dp", "fsdp"), axis=0, tiled=True),
        lax.all_gather(w_out, ("dp", "fsdp"), axis=0, tiled=True),
    )
    cross_branch = after_cross_grad.astype(jnp.bfloat16)
    out_w_grad = weight_grad(cross_flat, cross_branch)
    cross_mixed_grad = split_heads(project_back(cross_branch, cross_back[5]).astype(jnp.bfloat16))
    query_grad, key_grad, value_grad = attend_backward(
        queries, key_rows, value_rows, visible, cross_total, cross_mixed_grad
    )
    query_flat = merge_heads(query_grad)
    key_flat = merge_heads(key_grad)
    value_flat = merge_heads(value_grad)
    query_w_grad = weight_grad(normed, query_flat)
    key_w_grad = weight_grad(pix_normed, key_flat)
    value_w_grad = weight_grad(pix_normed, value_flat)
    normed_grad = project_back(query_flat, cross_back[2])
    pix_normed_grad = project_back(key_flat, cross_back[3]) + project_back(
        value_flat, cross_back[4]
    )
    latents_ln, query_gain_grad = jax.vjp(layer_norm, latents, cross_back[0].astype(jnp.float32))[
        1
    ](normed_grad)
    latents_grad = after_cross_grad + latents_ln
    chosen_grad, pixel_gain_grad = jax.vjp(layer_norm, chosen, cross_back[1].astype(jnp.float32))[
        1
    ](pix_normed_grad)
    pixels_grad = jnp.zeros(pixels.shape, jnp.float32).at[local_slot].add(chosen_grad)
    cross_grads = (
        lax.psum_scatter(query_gain_grad, ("dp", "fsdp"), scatter_dimension=0, tiled=True),
        lax.psum_scatter(pixel_gain_grad, ("dp", "fsdp"), scatter_dimension=0, tiled=True),
        lax.psum_scatter(query_w_grad, ("dp", "fsdp"), scatter_dimension=0, tiled=True),
        lax.psum_scatter(key_w_grad, ("dp", "fsdp"), scatter_dimension=0, tiled=True),
        lax.psum_scatter(value_w_grad, ("dp", "fsdp"), scatter_dimension=0, tiled=True),
        lax.psum_scatter(out_w_grad, ("dp", "fsdp"), scatter_dimension=0, tiled=True),
    )
    return (
        latents_out,
        latents_grad,
        pixels_grad,
        cross_grads[0],
        cross_grads[1],
        cross_grads[2],
        cross_grads[3],
        cross_grads[4],
        cross_grads[5],
        self_grads[0],
        self_grads[1],
        self_grads[2],
        mlp_grads[0],
        mlp_grads[1],
        mlp_grads[2],
        norms,
    )


def solution(mesh):
    in_specs = (
        P(("dp", "fsdp"), None, None),
        P(("dp", "fsdp"), None, None),
        P(("dp", "fsdp")),
        P(("dp", "fsdp")),
        P(("dp", "fsdp"), None, None),
        P(("dp", "fsdp")),
        P(("dp", "fsdp")),
        P(("dp", "fsdp"), None),
        P(("dp", "fsdp"), None),
        P(("dp", "fsdp"), None),
        P(("dp", "fsdp"), None),
        P(("dp", "fsdp")),
        P(("dp", "fsdp"), None),
        P(("dp", "fsdp"), None),
        P(("dp", "fsdp")),
        P(("dp", "fsdp"), None),
        P(("dp", "fsdp"), None),
    )
    out_specs = (
        P(("dp", "fsdp"), None, None),
        P(("dp", "fsdp"), None, None),
        P(("dp", "fsdp"), None, None),
        P(("dp", "fsdp")),
        P(("dp", "fsdp")),
        P(("dp", "fsdp"), None),
        P(("dp", "fsdp"), None),
        P(("dp", "fsdp"), None),
        P(("dp", "fsdp"), None),
        P(("dp", "fsdp")),
        P(("dp", "fsdp"), None),
        P(("dp", "fsdp"), None),
        P(("dp", "fsdp")),
        P(("dp", "fsdp"), None),
        P(("dp", "fsdp"), None),
        P(("dp", "fsdp")),
    )
    return jax.shard_map(local, mesh=mesh, in_specs=in_specs, out_specs=out_specs, check_vma=False)
```

profile of v0, /device:TPU:0, one launch (start us, length us, event | category | flops | bytes accessed | tf_op | source)
XLA Modules:
  0.0 1804.5 jit_solution(9631545740991180329)
XLA Ops:
  16.7 42.1 %all-reduce.9 = (bf16[1024]{0:T(1024)(128)(2,1)S(1)}, bf16[1024]{0:T(1024)(128)(2,1)S(1)}, bf16[1024]{0:T(1024)(128)(2,1)S(1)}, bf16[1024]{0:T(1024)(128)(2,1)S(1)}) all-reduce(bf16[1024]{0:T(1024)(128)(2,1)S(1)} %dynamic-update-slice.3, bf16[1024]{0:T(1024)(128)(2,1)S(1)} %dynamic-update-slice.2, ...), channel_id=1, replica_groups=mesh['dp'=4,'fsdp'=8] {'dp','fsdp'}, use_global_device_ids=true, to_apply=%add.1 | all-reduce | flops 4096 | bytes 16384
  61.2 9.2 all-gather.11.cloned.1.call-done
  73.7 55.1 %all-gather.13.cloned.1.call-done = bf16[1024,1024]{1,0:T(8,128)(2,1)} async-done(((bf16[32,1024]{1,0:T(8,128)(2,1)}), bf16[1024,1024]{1,0:T(8,128)(2,1)}) %all-gather.13.cloned.1.call-update) | async-done | bytes 2097168 | tf_op jit(solution)/shard_map/all_gather | solution.py:119
  128.8 3.9 convolution_convert_fusion.1
  139.6 47.5 %all-gather.9.cloned.1.call-done = bf16[1024,1024]{1,0:T(8,128)(2,1)} async-done(((bf16[32,1024]{1,0:T(8,128)(2,1)}), bf16[1024,1024]{1,0:T(8,128)(2,1)}) %all-gather.9.cloned.1.call-update) | async-done | bytes 2097168 | tf_op jit(solution)/shard_map/all_gather | solution.py:120
  193.2 52.1 %all-gather.15.cloned.1.call-done = bf16[1024,1024]{1,0:T(8,128)(2,1)} async-done(((bf16[32,1024]{1,0:T(8,128)(2,1)}), bf16[1024,1024]{1,0:T(8,128)(2,1)}) %all-gather.15.cloned.1.call-update) | async-done | bytes 2097168 | tf_op jit(solution)/shard_map/all_gather | solution.py:121
  248.1 68.5 %all-gather.17.cloned.1.call-done = bf16[1024,3072]{1,0:T(8,128)(2,1)} async-done(((bf16[32,3072]{1,0:T(8,128)(2,1)}), bf16[1024,3072]{1,0:T(8,128)(2,1)}) %all-gather.17.cloned.1.call-update) | async-done | bytes 6291472 | tf_op jit(solution)/shard_map/all_gather | solution.py:133
  316.5 4.7 fusion.7
  327.8 46.5 %all-gather.19.cloned.1.call-done = bf16[1024,1024]{1,0:T(8,128)(2,1)} async-done(((bf16[32,1024]{1,0:T(8,128)(2,1)}), bf16[1024,1024]{1,0:T(8,128)(2,1)}) %all-gather.19.cloned.1.call-update) | async-done | bytes 2097168 | tf_op jit(solution)/shard_map/all_gather | solution.py:134
  378.2 75.4 %all-gather.21.cloned.1.call-done = bf16[1024,4096]{1,0:T(8,128)(2,1)} async-done(((bf16[32,4096]{1,0:T(8,128)(2,1)}), bf16[1024,4096]{1,0:T(8,128)(2,1)}) %all-gather.21.cloned.1.call-update) | async-done | bytes 8388624 | tf_op jit(solution)/shard_map/all_gather | solution.py:146
  453.6 8.1 fusion.98
  461.7 70.9 %all-gather.23.cloned.1.call-done = bf16[4096,1024]{1,0:T(8,128)(2,1)} async-done(((bf16[128,1024]{1,0:T(8,128)(2,1)}), bf16[4096,1024]{1,0:T(8,128)(2,1)}) %all-gather.23.cloned.1.call-update) | async-done | bytes 8388624 | tf_op jit(solution)/shard_map/all_gather | solution.py:147
  532.7 9.4 fusion.6
  551.4 3.4 convolution_convert_fusion.5
  561.7 5.1 fusion.47
  573.9 3.2 fusion.29
  578.2 3.5 fusion.90
  581.8 4.1 multiply_reduce_fusion
  589.7 3.5 fusion.92
  599.8 7.9 fusion.56
  608.9 10.7 fusion.67
  620.8 9.8 fusion.96
  630.6 9.0 multiply_reduce_fusion.3
  640.4 3.4 fusion.112
  649.8 40.0 %all-reduce.8 = (f32[1024]{0:T(1024)S(1)}, f32[1024]{0:T(1024)S(1)}, f32[1024]{0:T(1024)S(1)}, f32[1024]{0:T(1024)S(1)}, f32[]{:T(128)}) all-reduce(f32[1024]{0:T(1024)S(1)} %get-tuple-element.34, f32[1024]{0:T(1024)S(1)} %get-tuple-element.28, ...), channel_id=2, replica_groups=mesh['dp'=4,'fsdp'=8] {'dp','fsdp'}, use_global_device_ids=true, to_apply=%region_23.24.clone | all-reduce | flops 4097 | bytes 32776
  698.4 136.3 %reduce-scatter.15.cloned.1.call-done = f32[32,1024]{1,0:T(8,128)} async-done(((f32[1024,1024]{1,0:T(8,128)}), f32[32,1024]{1,0:T(8,128)}) %reduce-scatter.15.cloned.1.call-update) | async-done | bytes 131088 | tf_op jit(solution)/shard_map/reduce_scatter | solution.py:239
  834.7 142.3 %reduce-scatter.13.cloned.1.call-done = f32[32,1024]{1,0:T(8,128)} async-done(((f32[1024,1024]{1,0:T(8,128)}), f32[32,1024]{1,0:T(8,128)}) %reduce-scatter.13.cloned.1.call-update) | async-done | bytes 131088 | tf_op jit(solution)/shard_map/reduce_scatter | solution.py:238
  977.1 142.3 %reduce-scatter.11.cloned.1.call-done = f32[32,1024]{1,0:T(8,128)} async-done(((f32[1024,1024]{1,0:T(8,128)}), f32[32,1024]{1,0:T(8,128)}) %reduce-scatter.11.cloned.1.call-update) | async-done | bytes 131088 | tf_op jit(solution)/shard_map/reduce_scatter | solution.py:237
  1119.3 143.0 %reduce-scatter.9.cloned.1.call-done = f32[32,1024]{1,0:T(8,128)} async-done(((f32[1024,1024]{1,0:T(8,128)}), f32[32,1024]{1,0:T(8,128)}) %reduce-scatter.9.cloned.1.call-update) | async-done | bytes 131088 | tf_op jit(solution)/shard_map/reduce_scatter | solution.py:236
  1262.3 158.2 %reduce-scatter.17.cloned.1.call-done = f32[32,3072]{1,0:T(8,128)} async-done(((f32[1024,3072]{1,0:T(8,128)}), f32[32,3072]{1,0:T(8,128)}) %reduce-scatter.17.cloned.1.call-update) | async-done | bytes 393232 | tf_op jit(solution)/shard_map/reduce_scatter | solution.py:198
  1420.5 188.6 %reduce-scatter.23.cloned.1.call-done = f32[128,1024]{1,0:T(8,128)} async-done(((f32[4096,1024]{1,0:T(8,128)}), f32[128,1024]{1,0:T(8,128)}) %reduce-scatter.23.cloned.1.call-update) | async-done | bytes 524304 | tf_op jit(solution)/shard_map/reduce_scatter | solution.py:174
  1609.2 187.2 %reduce-scatter.21.cloned.1.call-done = f32[32,4096]{1,0:T(8,128)} async-done(((f32[1024,4096]{1,0:T(8,128)}), f32[32,4096]{1,0:T(8,128)}) %reduce-scatter.21.cloned.1.call-update) | async-done | bytes 524304 | tf_op jit(solution)/shard_map/reduce_scatter | solution.py:173
  (197 shorter events, 91.1 us)
Async XLA Ops:
  7.2 53.1 %copy-start.3 = (f32[1,256,1024]{2,1,0:T(8,128)S(1)}, f32[1,256,1024]{2,1,0:T(8,128)}, u32[]{:S(2)}) copy-start(f32[1,256,1024]{2,1,0:T(8,128)} %param.19) | copy-start | bytes 3145732
  7.2 53.3 %copy-start.9 = (bf16[1,512,1024]{2,1,0:T(8,128)(2,1)S(1)}, bf16[1,512,1024]{2,1,0:T(8,128)(2,1)}, u32[]{:S(2)}) copy-start(bf16[1,512,1024]{2,1,0:T(8,128)(2,1)} %param.20) | copy-start | bytes 3145732
  7.2 63.2 %all-gather.11.cloned.1.call-start = ((), (), s32[]{:S(2)}) async-start(), calls=%async_computation.9 | async-start | bytes 2162688 | tf_op jit(solution)/shard_map/all_gather | solution.py:118
  7.9 120.9 %all-gather.13.cloned.1.call-start = ((), (), s32[]{:S(2)}) async-start(), calls=%async_computation.10 | async-start | bytes 2162688 | tf_op jit(solution)/shard_map/all_gather | solution.py:119
  8.7 178.5 %all-gather.9.cloned.1.call-start = ((), (), s32[]{:S(2)}) async-start(), calls=%async_computation.8 | async-start | bytes 2162688 | tf_op jit(solution)/shard_map/all_gather | solution.py:120
  9.4 235.9 %all-gather.15.cloned.1.call-start = ((), (), s32[]{:S(2)}) async-start(), calls=%async_computation.11 | async-start | bytes 2162688 | tf_op jit(solution)/shard_map/all_gather | solution.py:121
  10.0 306.5 %all-gather.17.cloned.1.call-start = ((), (), s32[]{:S(2)}) async-start(), calls=%async_computation.12 | async-start | bytes 6488064 | tf_op jit(solution)/shard_map/all_gather | solution.py:133
  10.6 363.8 %all-gather.19.cloned.1.call-start = ((), (), s32[]{:S(2)}) async-start(), calls=%async_computation.13 | async-start | bytes 2162688 | tf_op jit(solution)/shard_map/all_gather | solution.py:134
  11.2 442.5 %all-gather.21.cloned.1.call-start = ((), (), s32[]{:S(2)}) async-start(), calls=%async_computation.14 | async-start | bytes 8650752 | tf_op jit(solution)/shard_map/all_gather | solution.py:146
  11.9 520.7 %all-gather.23.cloned.1.call-start = ((), (), s32[]{:S(2)}) async-start(), calls=%async_computation.15 | async-start | bytes 8650752 | tf_op jit(solution)/shard_map/all_gather | solution.py:147
  12.7 685.8 %reduce-scatter.19.cloned.1.call-start = ((), (), s32[]{:S(2)}) async-start(), calls=%async_computation.21 | async-start | bytes 4325376 | tf_op jit(solution)/shard_map/reduce_scatter | solution.py:199
  187.2 4.0 copy-start.1
  193.2 54.5 %copy-start.28 = (bf16[8,128,256]{2,1,0:T(8,128)(2,1)}, bf16[8,128,256]{2,1,0:T(8,128)(2,1)S(1)}, u32[]{:S(2)}) copy-start(bf16[8,128,256]{2,1,0:T(8,128)(2,1)S(1)} %fusion.40) | copy-start | bytes 1572868
  532.7 10.8 copy-start.7
  532.7 10.8 copy-start.38
  551.3 283.4 %reduce-scatter.15.cloned.1.call-start = ((), (), s32[]{:S(2)}) async-start(), calls=%async_computation.19 | async-start | bytes 4325376 | tf_op jit(solution)/shard_map/reduce_scatter | solution.py:239
  561.1 5.7 copy-start.32
  561.7 5.2 copy-start.33
  568.4 3.0 copy-start.11
  571.1 406.0 %reduce-scatter.13.cloned.1.call-start = ((), (), s32[]{:S(2)}) async-start(), calls=%async_computation.18 | async-start | bytes 4325376 | tf_op jit(solution)/shard_map/reduce_scatter | solution.py:238
  573.9 4.3 copy-start.10
  581.7 537.6 %reduce-scatter.11.cloned.1.call-start = ((), (), s32[]{:S(2)}) async-start(), calls=%async_computation.17 | async-start | bytes 4325376 | tf_op jit(solution)/shard_map/reduce_scatter | solution.py:237
  581.7 4.2 copy-start.2
  593.2 3.7 copy-start.4
  593.2 669.2 %reduce-scatter.9.cloned.1.call-start = ((), (), s32[]{:S(2)}) async-start(), calls=%async_computation.16 | async-start | bytes 4325376 | tf_op jit(solution)/shard_map/reduce_scatter | solution.py:236
  599.7 820.8 %reduce-scatter.17.cloned.1.call-start = ((), (), s32[]{:S(2)}) async-start(), calls=%async_computation.20 | async-start | bytes 12976128 | tf_op jit(solution)/shard_map/reduce_scatter | solution.py:198
  607.6 1001.5 %reduce-scatter.23.cloned.1.call-start = ((), (), s32[]{:S(2)}) async-start(), calls=%async_computation.23 | async-start | bytes 17301504 | tf_op jit(solution)/shard_map/reduce_scatter | solution.py:174
  619.6 1176.8 %reduce-scatter.21.cloned.1.call-start = ((), (), s32[]{:S(2)}) async-start(), calls=%async_computation.22 | async-start | bytes 17301504 | tf_op jit(solution)/shard_map/reduce_scatter | solution.py:173
  640.4 3.4 copy-start.37
  640.4 3.4 copy-start.40
  645.5 4.4 copy-start.16
  649.8 44.7 %copy-start.12 = (f32[1,256,1024]{2,1,0:T(8,128)S(1)}, f32[1,256,1024]{2,1,0:T(8,128)}, u32[]{:S(2)}) copy-start(f32[1,256,1024]{2,1,0:T(8,128)} %copy-done.11) | copy-start | bytes 3145732
  (25 other events, 35.4 us)
Sparse Core Ops, SparseCore 0:
  11.0 59.3 all-gather.10
  73.3 55.3 all-gather.12
  131.8 55.3 all-gather.8
  190.0 55.3 all-gather.14
  248.2 68.2 all-gather.16
  319.4 54.9 all-gather.18
  377.4 76.2 all-gather.20
  456.6 75.9 all-gather.22
  551.5 141.2 reduce-scatter.18
  695.4 139.2 reduce-scatter.14
  837.6 139.4 reduce-scatter.12
  979.8 139.5 reduce-scatter.10
  1122.2 140.0 reduce-scatter.8
  1268.8 151.6 reduce-scatter.16
  1423.3 185.7 reduce-scatter.22
  1612.0 184.3 reduce-scatter.20
where the time goes:
time: 1810 us; the launch traced here: 1800 us
  waiting for transfers between devices  1530 us (85%)
  matrix products  131 us (7%)
  blocking collectives  82.2 us (5%)
  local copies, waits for them, and re-layouts  30.9 us (2%)
  between operations  18.3 us (1%)
    reduce_scatter x1, waiting for transfers between devices, local(): lax.psum_scatter(down_grad, ('dp', 'fsdp'), scatter_dimension=0, tiled=True)  189 us
    reduce_scatter x1, waiting for transfers between devices, local(): lax.psum_scatter(up_grad, ('dp', 'fsdp'), scatter_dimension=0, tiled=True)  187 us
    reduce_scatter x1, waiting for transfers between devices, local(): lax.psum_scatter(qkv_grad, ('dp', 'fsdp'), scatter_dimension=0, tiled=True)  158 us
    reduce_scatter x1, waiting for transfers between devices, local(): lax.psum_scatter(query_w_grad, ('dp', 'fsdp'), scatter_dimension=0, tiled...  143 us
    reduce_scatter x1, waiting for transfers between devices, local(): lax.psum_scatter(value_w_grad, ('dp', 'fsdp'), scatter_dimension=0, tiled...  142 us
    reduce_scatter x1, waiting for transfers between devices, local(): lax.psum_scatter(key_w_grad, ('dp', 'fsdp'), scatter_dimension=0, tiled=T...  142 us
    reduce_scatter x1, waiting for transfers between devices, local(): lax.psum_scatter(out_w_grad, ('dp', 'fsdp'), scatter_dimension=0, tiled=T...  136 us
    unnamed x2, blocking collectives  82.2 us
  transfers between devices with their start and end apart: 16, of which 15 were waited for; matrix products, arithmetic and copies ran while one was open for 8% of the time, Pallas kernels for 0%

commit v1 on v0

--- a/solution.py
+++ b/solution.py
@@ -1,7 +1,526 @@
+import functools
+
 import jax
 import jax.numpy as jnp
 from jax import lax
+from jax.experimental import pallas as pl
+from jax.experimental.pallas import tpu as pltpu
 from jax.sharding import PartitionSpec as P
+
+MESH = pl.DeviceIdType.MESH
+DMA = pltpu.SemaphoreType.DMA
+UNIT_COLS = 1024
+UNIT_ROWS = 32
+WIDTHS = ((256, 256, 256, 256), (128, 128, 384, 384), (128, 128, 384, 384))
+
+
+class Place:
+    def __init__(self):
+        dp, f = lax.axis_index("dp"), lax.axis_index("fsdp")
+        self.y, self.x, self.z, self.c = dp // 2, dp % 2, f // 2, f % 2
+        step = jnp.where(self.z < 2, 1, -1)
+        self.is_end = (self.z == 0) | (self.z == 3)
+        self.z1 = jnp.where(self.is_end, self.z + step, self.z - step)
+        self.z2 = jnp.where(self.is_end, self.z + 2 * step, self.z + step)
+        self.z3 = jnp.where(self.is_end, self.z + 3 * step, self.z + 2 * step)
+
+    def dev(self, y=None, x=None, z=None, c=None):
+        y = self.y if y is None else y
+        x = self.x if x is None else x
+        z = self.z if z is None else z
+        c = self.c if c is None else c
+        return (y * 2 + x, z * 2 + c)
+
+    def barrier(self):
+        bar = pltpu.get_barrier_semaphore()
+        peers = [
+            self.dev(c=1 - self.c),
+            self.dev(x=1 - self.x),
+            self.dev(y=1 - self.y),
+            self.dev(z=self.z1),
+            self.dev(z=self.z2),
+            self.dev(z=self.z3),
+        ]
+        for peer in peers:
+            pl.semaphore_signal(bar, inc=1, device_id=peer, device_id_type=MESH)
+        pl.semaphore_wait(bar, len(peers))
+
+
+def remote(src, dst, send_sem, recv_sem, dev):
+    return pltpu.make_async_remote_copy(
+        src_ref=src, dst_ref=dst, send_sem=send_sem, recv_sem=recv_sem, device_id=dev, device_id_type=MESH
+    )
+
+
+def part_cols(u, p, base):
+    widths = WIDTHS[u % 3]
+    return pl.ds(base + sum(widths[:p]), widths[p])
+
+
+class Gather:
+    STAGES = 7
+
+    def __init__(self, me, units, sems):
+        self.me, self.units = me, units
+        self.loc, self.sib_s, self.sib_r, self.zs, self.zr, self.xs, self.xr, self.ys, self.yr = sems
+
+    @staticmethod
+    def sems(n):
+        return [DMA((n,))] * 3 + [DMA((n, 4, 4))] * 2 + [DMA((n, 4))] * 4
+
+    def at(self, u, y, x, z, c, p=None):
+        _, full, row, col = self.units[u]
+        cols = pl.ds(col, UNIT_COLS) if p is None else part_cols(u, p, col)
+        return full.at[y, x, z, c, pl.ds(row, UNIT_ROWS), cols]
+
+    def own(self, u):
+        me, (shard, _, row, col) = self.me, self.units[u]
+        src = shard.at[pl.ds(row, UNIT_ROWS), pl.ds(col, UNIT_COLS)]
+        return pltpu.make_async_copy(src, self.at(u, me.y, me.x, me.z, me.c), self.loc.at[u])
+
+    def zblk(self, u, p, z):
+        me, s = self.me, slice(None)
+        return self.at(u, me.y if p != 3 else s, me.x if p != 2 else s, z, me.c, p)
+
+    def zcopy(self, u, p, z_to, z_block=None):
+        me = self.me
+        if z_block is None:
+            b = self.zblk(u, p, me.z)
+            return remote(b, b, self.zs.at[u, p, z_to], self.zr.at[u, p, me.z], me.dev(z=z_to))
+        b = self.zblk(u, p, z_block)
+        return remote(b, b, self.zs.at[u, p, me.z], self.zr.at[u, p, z_block], me.dev(z=z_to))
+
+    def zin(self, u, p, z_block):
+        b = self.zblk(u, p, z_block)
+        return remote(b, b, self.zs.at[u, p, z_block], self.zr.at[u, p, z_block], self.me.dev(z=z_block))
+
+    def z_a(self, u, p):
+        me = self.me
+        self.zcopy(u, p, me.z1).start()
+        self.zcopy(u, p, me.z2).start()
+
+        @pl.when(~me.is_end)
+        def _():
+            self.zcopy(u, p, me.z3).start()
+
+    def z_b(self, u, p):
+        me = self.me
+
+        @pl.when(~me.is_end)
+        def _():
+            self.zin(u, p, me.z3).wait_recv()
+            self.zcopy(u, p, me.z1, me.z3).start()
+
+    def z_wait(self, u, p):
+        me = self.me
+        self.zin(u, p, me.z1).wait_recv()
+        self.zin(u, p, me.z2).wait_recv()
+
+        @pl.when(me.is_end)
+        def _():
+            self.zin(u, p, me.z3).wait_recv()
+
+    def z_sent(self, u, p):
+        me = self.me
+        self.zcopy(u, p, me.z1).wait_send()
+        self.zcopy(u, p, me.z2).wait_send()
+
+        @pl.when(~me.is_end)
+        def _():
+            self.zcopy(u, p, me.z3).wait_send()
+            self.zcopy(u, p, me.z1, me.z3).wait_send()
+
+    def xcopy(self, u, p, out=True):
+        me, s = self.me, slice(None)
+        b = self.at(u, me.y if p != 3 and p != 1 else s, me.x if out else 1 - me.x, me.z if p == 2 else s, me.c, p)
+        return remote(b, b, self.xs.at[u, p], self.xr.at[u, p], me.dev(x=1 - me.x))
+
+    def ycopy(self, u, p, out=True):
+        me, s = self.me, slice(None)
+        b = self.at(u, me.y if out else 1 - me.y, me.x if p != 2 and p != 0 else s, me.z if p == 3 else s, me.c, p)
+        return remote(b, b, self.ys.at[u, p], self.yr.at[u, p], me.dev(y=1 - me.y))
+
+    def final(self, u, out=True):
+        me, s = self.me, slice(None)
+        b = self.at(u, s, s, s, me.c if out else 1 - me.c)
+        return remote(b, b, self.sib_s.at[u], self.sib_r.at[u], me.dev(c=1 - me.c))
+
+    def stage(self, s, u):
+        if s == 0:
+            self.own(u).start()
+        elif s == 1:
+            self.own(u).wait()
+            self.xcopy(u, 2).start()
+            self.ycopy(u, 3).start()
+            self.z_a(u, 0)
+            self.z_a(u, 1)
+        elif s == 2:
+            self.z_b(u, 0)
+            self.z_b(u, 1)
+            self.xcopy(u, 2, False).wait_recv()
+            self.z_a(u, 2)
+            self.ycopy(u, 3, False).wait_recv()
+            self.z_a(u, 3)
+        elif s == 3:
+            self.z_wait(u, 0)
+            self.xcopy(u, 0).start()
+            self.z_wait(u, 1)
+            self.ycopy(u, 1).start()
+            self.z_b(u, 2)
+            self.z_b(u, 3)
+        elif s == 4:
+            self.z_wait(u, 2)
+            self.ycopy(u, 2).start()
+            self.z_wait(u, 3)
+            self.xcopy(u, 3).start()
+            self.xcopy(u, 0, False).wait_recv()
+            self.ycopy(u, 0).start()
+            self.ycopy(u, 1, False).wait_recv()
+            self.xcopy(u, 1).start()
+        elif s == 5:
+            self.ycopy(u, 2, False).wait_recv()
+            self.xcopy(u, 3, False).wait_recv()
+            self.ycopy(u, 0, False).wait_recv()
+            self.xcopy(u, 1, False).wait_recv()
+            self.final(u).start()
+        elif s == 6:
+            self.final(u, False).wait_recv()
+
+    def sent(self, u):
+        for p in range(4):
+            self.z_sent(u, p)
+            self.xcopy(u, p).wait_send()
+            self.ycopy(u, p).wait_send()
+        self.final(u).wait_send()
+
+    def tick(self, t, wide):
+        for u in range(len(self.units)):
+            s = t - max(0, u - wide + 1)
+            if 0 <= s < self.STAGES:
+                self.stage(s, u)
+
+    def ticks(self, wide):
+        return self.STAGES + max(0, len(self.units) - wide)
+
+
+class Scatter:
+    STAGES = 5
+
+    def __init__(self, me, units, refs, sems):
+        self.me, self.units = me, units
+        self.part, self.r1, self.r2, self.rz = refs
+        self.s1, self.q1, self.s2, self.q2, self.zs, self.zr = sems
+
+    @staticmethod
+    def scratch(n):
+        return [
+            pltpu.VMEM((n, 2, 2, 4, UNIT_ROWS, UNIT_COLS), jnp.bfloat16),
+            pltpu.VMEM((n, 2, 4, UNIT_ROWS, UNIT_COLS), jnp.bfloat16),
+            pltpu.VMEM((n, 4, UNIT_ROWS, UNIT_COLS), jnp.bfloat16),
+            pltpu.VMEM((n, 4, 2, UNIT_ROWS, UNIT_COLS), jnp.bfloat16),
+        ]
+
+    @staticmethod
+    def sems(n):
+        return [DMA((n, 4))] * 4 + [DMA((n, 4, 4))] * 2
+
+    def pt(self, u, p, y, x, z):
+        return self.part.at[u, y, x, z, :, part_cols(u, p, 0)]
+
+    def first(self, u, p):
+        me, s = self.me, slice(None)
+        dst = self.r1.at[u, :, :, :, part_cols(u, p, 0)]
+        if p in (0, 2):
+            return remote(self.pt(u, p, 1 - me.y, s, s), dst, self.s1.at[u, p], self.q1.at[u, p], me.dev(y=1 - me.y))
+        return remote(self.pt(u, p, s, 1 - me.x, s), dst, self.s1.at[u, p], self.q1.at[u, p], me.dev(x=1 - me.x))
+
+    def add(self, count, dst, srcs):
+        def body(i, carry):
+            total = dst(i)[...].astype(jnp.float32)
+            for src in srcs:
+                total = total + src(i)[...].astype(jnp.float32)
+            dst(i)[...] = total.astype(jnp.bfloat16)
+            return carry
+
+        if count == 1:
+            body(0, 0)
+        else:
+            lax.fori_loop(0, count, body, 0)
+
+    def first_in(self, u, p):
+        me = self.me
+        self.first(u, p).wait_recv()
+        if p in (0, 2):
+            dst = lambda i: self.pt(u, p, me.y, i // 4, i % 4)
+        else:
+            dst = lambda i: self.pt(u, p, i // 4, me.x, i % 4)
+        self.add(8, dst, [lambda i: self.r1.at[u, i // 4, i % 4, :, part_cols(u, p, 0)]])
+
+    def second(self, u, p):
+        me, s = self.me, slice(None)
+        cols = part_cols(u, p, 0)
+        z = s if p < 2 else me.z
+        dst = self.r2.at[u, :, :, cols] if p < 2 else self.r2.at[u, 0, :, cols]
+        if p in (0, 2):
+            return remote(self.pt(u, p, me.y, 1 - me.x, z), dst, self.s2.at[u, p], self.q2.at[u, p], me.dev(x=1 - me.x))
+        return remote(self.pt(u, p, 1 - me.y, me.x, z), dst, self.s2.at[u, p], self.q2.at[u, p], me.dev(y=1 - me.y))
+
+    def second_in(self, u, p):
+        me = self.me
+        self.second(u, p).wait_recv()
+        self.add(
+            4,
+            lambda i: self.pt(u, p, me.y, me.x, i),
+            [lambda i: self.r2.at[u, i, :, part_cols(u, p, 0)]],
+        )
+
+    def zblk(self, u, p, z):
+        me, s = self.me, slice(None)
+        return self.pt(u, p, me.y if p != 3 else s, me.x if p != 2 else s, z)
+
+    def zslot(self, u, p, slot):
+        cols = part_cols(u, p, 0)
+        return self.rz.at[u, slot, 0, :, cols] if p < 2 else self.rz.at[u, slot, :, :, cols]
+
+    def zcopy(self, u, p, which, block, slot, z_to):
+        return remote(
+            self.zblk(u, p, block), self.zslot(u, p, slot), self.zs.at[u, p, which], self.zr.at[u, p, slot], self.me.dev(z=z_to)
+        )
+
+    def z_ends(self, u, p):
+        me = self.me
+        return [
+            self.zcopy(u, p, 2, me.z3, 3, me.z1),
+            self.zcopy(u, p, 1, me.z2, 2, me.z2),
+            self.zcopy(u, p, 0, me.z1, 0, me.z1),
+        ]
+
+    def z_mids(self, u, p):
+        me = self.me
+        return [self.zcopy(u, p, 0, me.z1, 0, me.z1), self.zcopy(u, p, 1, me.z2, 1, me.z2)]
+
+    def z_gone(self, u, p):
+        return self.zcopy(u, p, 2, self.me.z3, 1, self.me.z3)
+
+    def z_a(self, u, p):
+        me = self.me
+
+        @pl.when(me.is_end)
+        def _():
+            for c in self.z_ends(u, p):
+                c.start()
+
+        @pl.when(~me.is_end)
+        def _():
+            for c in self.z_mids(u, p):
+                c.start()
+
+    def zget(self, u, p, slot):
+        return self.zcopy(u, p, 0, self.me.z, slot, self.me.z1)
+
+    def z_b(self, u, p):
+        me = self.me
+
+        @pl.when(~me.is_end)
+        def _():
+            self.zget(u, p, 3).wait_recv()
+            self.z_add(u, p, me.z3, (3,))
+            self.z_gone(u, p).start()
+
+    def z_add(self, u, p, block, slots):
+        cols = part_cols(u, p, 0)
+        me = self.me
+        if p < 2:
+            dst, count = (lambda i: self.pt(u, p, me.y, me.x, block)), 1
+        elif p == 2:
+            dst, count = (lambda i: self.pt(u, p, me.y, i, block)), 2
+        else:
+            dst, count = (lambda i: self.pt(u, p, i, me.x, block)), 2
+        self.add(count, dst, [functools.partial(lambda slot, i: self.rz.at[u, slot, i, :, cols], k) for k in slots])
+
+    def z_in(self, u, p):
+        me = self.me
+        self.zget(u, p, 0).wait_recv()
+        self.zget(u, p, 1).wait_recv()
+
+        @pl.when(~me.is_end)
+        def _():
+            self.zget(u, p, 2).wait_recv()
+
+    def out(self, u, p):
+        out, row, col = self.units[u]
+        return out.at[pl.ds(row, UNIT_ROWS), part_cols(u, p, col)]
+
+    def finish_z(self, u, p):
+        me, cols = self.me, part_cols(u, p, 0)
+        self.z_in(u, p)
+        f32 = lambda ref: ref[...].astype(jnp.float32)
+        total = f32(self.pt(u, p, me.y, me.x, me.z)) + f32(self.rz.at[u, 0, 0, :, cols]) + f32(self.rz.at[u, 1, 0, :, cols])
+
+        @pl.when(me.is_end)
+        def _():
+            self.out(u, p)[...] = total
+
+        @pl.when(~me.is_end)
+        def _():
+            self.out(u, p)[...] = total + f32(self.rz.at[u, 2, 0, :, cols])
+
+    def pass_z(self, u, p):
+        me = self.me
+        self.z_in(u, p)
+
+        @pl.when(me.is_end)
+        def _():
+            self.z_add(u, p, me.z, (0, 1))
+
+        @pl.when(~me.is_end)
+        def _():
+            self.z_add(u, p, me.z, (0, 1, 2))
+
+        self.second(u, p).start()
+
+    def finish_last(self, u, p):
+        me, cols = self.me, part_cols(u, p, 0)
+        self.second(u, p).wait_recv()
+        total = self.pt(u, p, me.y, me.x, me.z)[...].astype(jnp.float32) + self.r2.at[u, 0, :, cols][...].astype(jnp.float32)
+        self.out(u, p)[...] = total
+
+    def stage(self, s, u):
+        if s == 0:
+            for p in (2, 3, 0, 1):
+                self.first(u, p).start()
+        elif s == 1:
+            for p in (2, 3):
+                self.first_in(u, p)
+                self.z_a(u, p)
+            for p in (0, 1):
+                self.first_in(u, p)
+                self.second(u, p).start()
+        elif s == 2:
+            for p in (2, 3):
+                self.z_b(u, p)
+            for p in (0, 1):
+                self.second_in(u, p)
+                self.z_a(u, p)
+        elif s == 3:
+            for p in (2, 3):
+                self.pass_z(u, p)
+            for p in (0, 1):
+                self.z_b(u, p)
+        elif s == 4:
+            for p in (0, 1):
+                self.finish_z(u, p)
+            for p in (2, 3):
+                self.finish_last(u, p)
+
+    def sent(self, u):
+        me = self.me
+        for p in range(4):
+            self.first(u, p).wait_send()
+            self.second(u, p).wait_send()
+
+            @pl.when(me.is_end)
+            def _():
+                for c in self.z_ends(u, p):
+                    c.wait_send()
+
+            @pl.when(~me.is_end)
+            def _():
+                for c in self.z_mids(u, p) + [self.z_gone(u, p)]:
+                    c.wait_send()
+
+
+def gather_units(shards, fulls):
+    units = [(shards[i], fulls[i], 0, 0) for i in (1, 2, 0, 3)]
+    units += [(shards[4], fulls[4], 0, k * UNIT_COLS) for k in range(3)]
+    units += [(shards[5], fulls[5], 0, 0)]
+    units += [(shards[6], fulls[6], 0, k * UNIT_COLS) for k in range(4)]
+    units += [(shards[7], fulls[7], k * UNIT_ROWS, 0) for k in range(4)]
+    return units
+
+
+def gather_kernel(wide, *refs):
+    shards, fulls, sems = refs[:8], refs[8:16], refs[16:]
+    me = Place()
+    me.barrier()
+    gather = Gather(me, gather_units(shards, fulls), sems)
+    for t in range(gather.ticks(wide)):
+        gather.tick(t, wide)
+    for u in range(len(gather.units)):
+        gather.sent(u)
+
+
+def gather_all(shards, wide=4):
+    outs = [jax.ShapeDtypeStruct((2, 2, 4, 2) + s.shape, s.dtype) for s in shards]
+    return pl.pallas_call(
+        functools.partial(gather_kernel, wide),
+        out_shape=outs,
+        in_specs=[pl.BlockSpec(memory_space=pl.ANY)] * 8,
+        out_specs=[pl.BlockSpec(memory_space=pl.ANY)] * 8,
+        scratch_shapes=Gather.sems(16),
+        compiler_params=pltpu.CompilerParams(collective_id=0, has_side_effects=True, vmem_limit_bytes=60 * 2**20),
+    )(*shards)
+
+
+def scatter_kernel(*refs):
+    grads, outs = refs[:8], refs[8:16]
+    part, r1, r2, rz, r0 = refs[16:21]
+    sems, (la, lb, ls, lr) = refs[21:27], refs[27:]
+    me = Place()
+    me.barrier()
+    units = [(outs[7], k * UNIT_ROWS, 0) for k in range(4)]
+    units += [(outs[6], 0, k * UNIT_COLS) for k in range(4)]
+    units += [(outs[4], 0, k * UNIT_COLS) for k in range(3)]
+    units += [(outs[i], 0, 0) for i in (5, 3, 0, 1, 2)]
+    which = [7] * 4 + [6] * 4 + [4] * 3 + [5, 3, 0, 1, 2]
+    sc = Scatter(me, units, (part, r1, r2, rz), sems)
+    n = len(units)
+
+    def mine(u):
+        _, row, col = units[u]
+        src = grads[which[u]].at[:, :, :, me.c, pl.ds(row, UNIT_ROWS), pl.ds(col, UNIT_COLS)]
+        return pltpu.make_async_copy(src, part.at[u], la.at[u])
+
+    def give(u):
+        _, row, col = units[u]
+        src = grads[which[u]].at[:, :, :, 1 - me.c, pl.ds(row, UNIT_ROWS), pl.ds(col, UNIT_COLS)]
+        return remote(src, r0.at[u], ls.at[u], lr.at[u], me.dev(c=1 - me.c))
+
+    for t in range(n + 6):
+        for s in (4, 3, 2, 1, 0, -1, -2):
+            u = t - (s + 2)
+            if not 0 <= u < n:
+                continue
+            if s == -2:
+                mine(u).start()
+                give(u).start()
+            elif s == -1:
+                mine(u).wait()
+                give(u).wait_recv()
+                idx = lambda i: (i // 8, (i // 4) % 2, i % 4)
+                sc.add(16, lambda i: part.at[(u,) + idx(i)], [lambda i: r0.at[(u,) + idx(i)]])
+                give(u).wait_send()
+            else:
+                sc.stage(s, u)
+    for u in range(n):
+        sc.sent(u)
+
+
+def scatter_all(grads):
+    outs = [jax.ShapeDtypeStruct(g.shape[4:], jnp.float32) for g in grads]
+    n = 16
+    return pl.pallas_call(
+        scatter_kernel,
+        out_shape=outs,
+        in_specs=[pl.BlockSpec(memory_space=pl.ANY)] * 8,
+        out_specs=[pl.BlockSpec(memory_space=pltpu.VMEM)] * 8,
+        scratch_shapes=Scatter.scratch(n)
+        + [pltpu.VMEM((n, 2, 2, 4, UNIT_ROWS, UNIT_COLS), jnp.bfloat16)]
+        + Scatter.sems(n)
+        + [DMA((n,))] * 4,
+        compiler_params=pltpu.CompilerParams(collective_id=1, has_side_effects=True, vmem_limit_bytes=62 * 2**20),
+    )(*grads)
+
 
 HEADS = 8
 
@@ -86,7 +605,7 @@
     return (query_grad, key_grad, value_grad)
 
 
-def local(
+def local_plain(
     latents,
     pixels,
     slot_index,
@@ -258,6 +777,142 @@
     )
 
 
+def local_fast(
+    latents,
+    pixels,
+    slot_index,
+    counts,
+    cotangent,
+    gain_q,
+    gain_kv,
+    w_query,
+    w_key,
+    w_value,
+    w_out,
+    gain_self,
+    w_qkv,
+    w_self_out,
+    gain_mlp,
+    w_up,
+    w_down,
+):
+    groups = latents.shape[0]
+    slots = pixels.shape[1]
+    width = latents.shape[2]
+    local_slot = slot_index % groups
+    chosen = jnp.take(pixels, local_slot, axis=0).astype(jnp.float32)
+    visible_count = jnp.take(counts, local_slot, axis=0)
+    visible = lax.broadcasted_iota(jnp.int32, (groups, slots), 1) < visible_count[:, None]
+    gains = lax.all_gather(jnp.stack([gain_q, gain_kv, gain_self, gain_mlp]), ("dp", "fsdp"), axis=1, tiled=True)
+    shards = (w_query, w_key, w_value, w_out, w_qkv, w_self_out, w_up, w_down)
+    fulls = [f.reshape(-1, f.shape[-1]) for f in gather_all(shards)]
+    cross_all = (gains[0], gains[1], fulls[0], fulls[1], fulls[2], fulls[3])
+    self_all = (gains[2], fulls[4], fulls[5])
+    mlp_all = (gains[3], fulls[6], fulls[7])
+    cross_back, self_back, mlp_back = cross_all, self_all, mlp_all
+    normed = layer_norm(latents, cross_all[0].astype(jnp.float32)).astype(jnp.bfloat16)
+    pix_normed = layer_norm(chosen, cross_all[1].astype(jnp.float32)).astype(jnp.bfloat16)
+    queries = split_heads(project(normed, cross_all[2]).astype(jnp.bfloat16))
+    key_rows = split_heads(project(pix_normed, cross_all[3]).astype(jnp.bfloat16))
+    value_rows = split_heads(project(pix_normed, cross_all[4]).astype(jnp.bfloat16))
+    cross_mixed, cross_total = attend_forward(queries, key_rows, value_rows, visible)
+    cross_flat = merge_heads(cross_mixed)
+    after_cross = latents + project(cross_flat, cross_all[5])
+    normed_self = layer_norm(after_cross, self_all[0].astype(jnp.float32)).astype(jnp.bfloat16)
+    packed = project(normed_self, self_all[1]).astype(jnp.bfloat16)
+    self_queries = split_heads(packed[..., :width])
+    self_keys = split_heads(packed[..., width : 2 * width])
+    self_values = split_heads(packed[..., 2 * width :])
+    self_mixed, self_total = attend_forward(self_queries, self_keys, self_values, None)
+    self_flat = merge_heads(self_mixed)
+    after_self = after_cross + project(self_flat, self_all[2])
+    normed_mlp = layer_norm(after_self, mlp_all[0].astype(jnp.float32)).astype(jnp.bfloat16)
+    hidden = project(normed_mlp, mlp_all[1])
+    activated = jax.nn.gelu(hidden).astype(jnp.bfloat16)
+    latents_out = after_self + project(activated, mlp_all[2])
+    root_mean = jnp.sqrt(jnp.mean(latents_out * latents_out, axis=(1, 2)))
+    out_grad = cotangent.astype(jnp.bfloat16)
+    down_grad = weight_grad(activated, out_grad)
+    act_grad = project_back(out_grad, mlp_back[2])
+    hidden_grad = jax.vjp(jax.nn.gelu, hidden)[1](act_grad)[0].astype(jnp.bfloat16)
+    up_grad = weight_grad(normed_mlp, hidden_grad)
+    mlp_in_grad = project_back(hidden_grad, mlp_back[1])
+    after_self_ln, mlp_gain_grad = jax.vjp(layer_norm, after_self, mlp_back[0].astype(jnp.float32))[
+        1
+    ](mlp_in_grad)
+    after_self_grad = cotangent + after_self_ln
+    self_branch = after_self_grad.astype(jnp.bfloat16)
+    self_out_grad = weight_grad(self_flat, self_branch)
+    self_mixed_grad = split_heads(project_back(self_branch, self_back[2]).astype(jnp.bfloat16))
+    self_q_grad, self_k_grad, self_v_grad = attend_backward(
+        self_queries, self_keys, self_values, None, self_total, self_mixed_grad
+    )
+    packed_grad = jnp.concatenate(
+        [merge_heads(self_q_grad), merge_heads(self_k_grad), merge_heads(self_v_grad)], axis=-1
+    )
+    qkv_grad = weight_grad(normed_self, packed_grad)
+    self_in_grad = project_back(packed_grad, self_back[1])
+    after_cross_ln, self_gain_grad = jax.vjp(
+        layer_norm, after_cross, self_back[0].astype(jnp.float32)
+    )[1](self_in_grad)
+    after_cross_grad = after_self_grad + after_cross_ln
+    cross_branch = after_cross_grad.astype(jnp.bfloat16)
+    out_w_grad = weight_grad(cross_flat, cross_branch)
+    cross_mixed_grad = split_heads(project_back(cross_branch, cross_back[5]).astype(jnp.bfloat16))
+    query_grad, key_grad, value_grad = attend_backward(
+        queries, key_rows, value_rows, visible, cross_total, cross_mixed_grad
+    )
+    query_flat = merge_heads(query_grad)
+    key_flat = merge_heads(key_grad)
+    value_flat = merge_heads(value_grad)
+    query_w_grad = weight_grad(normed, query_flat)
+    key_w_grad = weight_grad(pix_normed, key_flat)
+    value_w_grad = weight_grad(pix_normed, value_flat)
+    normed_grad = project_back(query_flat, cross_back[2])
+    pix_normed_grad = project_back(key_flat, cross_back[3]) + project_back(
+        value_flat, cross_back[4]
+    )
+    latents_ln, query_gain_grad = jax.vjp(layer_norm, latents, cross_back[0].astype(jnp.float32))[
+        1
+    ](normed_grad)
+    latents_grad = after_cross_grad + latents_ln
+    chosen_grad, pixel_gain_grad = jax.vjp(layer_norm, chosen, cross_back[1].astype(jnp.float32))[
+        1
+    ](pix_normed_grad)
+    pixels_grad = jnp.zeros(pixels.shape, jnp.float32).at[local_slot].add(chosen_grad)
+    grads = (query_w_grad, key_w_grad, value_w_grad, out_w_grad, qkv_grad, self_out_grad, up_grad, down_grad)
+    blocks = [g.astype(jnp.bfloat16).reshape(2, 2, 4, 2, -1, g.shape[-1]) for g in grads]
+    g_query, g_key, g_value, g_out, g_qkv, g_self_out, g_up, g_down = scatter_all(blocks)
+    small = jnp.concatenate([query_gain_grad, pixel_gain_grad, self_gain_grad, mlp_gain_grad, root_mean])
+    small = lax.psum(small, ("dp", "fsdp"))
+    rows = gain_q.shape[0]
+    mine = lax.axis_index(("dp", "fsdp")) * rows
+    gain_grads = [lax.dynamic_slice(small, (k * width + mine,), (rows,)) for k in range(4)]
+    norms = root_mean * (groups * lax.axis_size(("dp", "fsdp"))) / jnp.sum(small[4 * width :])
+    return (
+        latents_out,
+        latents_grad,
+        pixels_grad,
+        gain_grads[0],
+        gain_grads[1],
+        g_query,
+        g_key,
+        g_value,
+        g_out,
+        gain_grads[2],
+        g_qkv,
+        g_self_out,
+        gain_grads[3],
+        g_up,
+        g_down,
+        norms,
+    )
+
+
+def fits(mesh):
+    return mesh.shape["dp"] == 4 and mesh.shape["fsdp"] == 8
+
+
 def solution(mesh):
     in_specs = (
         P(("dp", "fsdp"), None, None),
@@ -296,4 +951,4 @@
         P(("dp", "fsdp"), None),
         P(("dp", "fsdp")),
     )
-    return jax.shard_map(local, mesh=mesh, in_specs=in_specs, out_specs=out_specs, check_vma=False)
+    return jax.shard_map(local_fast if fits(mesh) else local_plain, mesh=mesh, in_specs=in_specs, out_specs=out_specs, check_vma=False)

time: 1810 us -> 539 us (0.30)
  waiting for transfers between devices: 1530 us -> 0 us
  Pallas kernels: 0 us -> 304 us
  matrix products: 131 us -> 91.7 us
    reduce_scatter x8 -> x0, waiting for transfers between devices: 1100 us -> none  [the longest x1 189 us: local(): lax.psum_scatter(down_grad, ('dp', 'fsdp'), scatter_dimension=0, tiled=True)]
    all_gather x8 -> x0, waiting for transfers between devices: 425 us -> none  [the longest x1 75.4 us: local(): lax.all_gather(w_up, ('dp', 'fsdp'), axis=0, tiled=True)]
    pallas_call x0 -> x2, Pallas kernels: none -> 304 us  [the longest x1 155 us: scatter_all(): pl.pallas_call(scatter_kernel, out_shape=outs, in_specs=[pl.BlockSpec(mem...]
    unnamed x2 -> x0, blocking collectives: 82.2 us -> none
    all_gather x0 -> x1, blocking collectives: none -> 43.3 us  [local_fast(): lax.all_gather(jnp.stack([gain_q, gain_kv, gain_self, gain_mlp]), ('dp',...]
    psum x0 -> x1, blocking collectives: none -> 38 us  [local_fast(): small = lax.psum(small, ('dp', 'fsdp'))]
  transfers between devices with their start and end apart: 16 -> 0, of which waited for: 15 -> 0; matrix products, arithmetic and copies ran while one was open for 8% -> 0% of each run, Pallas kernels for 0% -> 0%
where the time goes in v1:
time: 539 us; the launch traced here: 530 us
  Pallas kernels  304 us (56%)
  matrix products  91.7 us (17%)
  blocking collectives  81.3 us (15%)
  local copies, waits for them, and re-layouts  34 us (6%)
  other arithmetic  13.6 us (3%)
    pallas_call x1, Pallas kernels, scatter_all(): pl.pallas_call(scatter_kernel, out_shape=outs, in_specs=[pl.BlockSpec(mem...  155 us
    pallas_call x1, Pallas kernels, gather_all(): pl.pallas_call(functools.partial(gather_kernel, wide), out_shape=outs, in...  150 us
    all_gather x1, blocking collectives, local_fast(): lax.all_gather(jnp.stack([gain_q, gain_kv, gain_self, gain_mlp]), ('dp',...  43.3 us
    psum x1, blocking collectives, local_fast(): small = lax.psum(small, ('dp', 'fsdp'))  38 us
    dot_general x8, matrix products, weight_grad(): jnp.einsum('gld,gle->de', inputs, grad_rows, preferred_element_type=jnp.f...  30.1 us
    dot_general x8, matrix products, project_back(): jnp.einsum('gle,de->gld', grad_rows, matrix, preferred_element_type=jnp.f...  28.5 us
    unnamed x131, local copies, waits for them, and re-layouts  24.6 us
    dot_general x8, matrix products, project(): jnp.einsum('gld,de->gle', inputs, matrix, preferred_element_type=jnp.floa...  19 us

profile of v1, /device:TPU:0, one launch (start us, length us, event | category | flops | bytes accessed | tf_op | source)
XLA Modules:
  0.0 529.7 jit_solution(9060387408845275956)
XLA Ops:
  5.7 43.3 %all-gather = bf16[32,32,4]{1,2,0:T(4,128)(2,1)S(1)} all-gather(bf16[1,32,4]{1,2,0:T(4,128)(2,1)S(1)} %maximum_bitcast_fusion.3), channel_id=1, replica_groups=mesh['dp'=4,'fsdp'=8] {'dp','fsdp'}, dimensions={0}, use_global_device_ids=true | all-gather | bytes 8448 | tf_op jit(solution)/shard_map/all_gather | solution.py:806
  49.2 149.6 %shard_map.284 = (bf16[2,2,4,2,32,1024]{5,4,3,2,1,0:T(8,128)(2,1)}, bf16[2,2,4,2,32,1024]{5,4,3,2,1,0:T(8,128)(2,1)}, bf16[2,2,4,2,32,1024]{5,4,3,2,1,0:T(8,128)...) custom-call(bf16[32,1024]{1,0:T(8,128)(2,1)} %refs_0_.1, ...), custom_call_target="tpu_custom_call" | custom-call | tf_op jit(solution)/shard_map/pallas_call | solution.py:455
  198.8 2.4 convolution_convert_fusion.15
  201.4 4.1 fusion.30
  205.5 2.3 convolution_convert_fusion.9
  207.8 1.9 copy.103
  216.3 1.9 fusion.7
  221.3 1.8 multiply_reduce_fusion.2
  227.4 2.4 fusion.82
  230.2 4.3 multiply_reduce_fusion.3
  235.2 9.5 %fusion.6 = bf16[256,4096]{1,0:T(8,128)(2,1)S(1)} fusion(f32[256,4096]{1,0:T(8,128)} %copy-done.50, bf16[4096,1024]{1,0:T(8,128)(2,1)} %bitcast.321, f32[1,256,1024]{2,1,0:T(8,128)} %param.22), kind=kOutput, calls=%fused_computation.12 | convolution fusion | flops 2168717312 | bytes 15728640 | tf_op jit(solution)/shard_map/gle,de->gld/dot_general | solution.py:542
  244.8 6.7 %fusion.44 = (f32[1024]{0:T(1024)S(1)}, f32[256]{0:T(256)S(1)}, f32[256,1024]{1,0:T(8,128)S(1)}) fusion(f32[1,256,1024]{2,1,0:T(8,128)S(1)} %copy-done.5, f32[256]{0:T(256)S(1)} %fusion.76, f32[256]{0:T(256)S(1)} %broadcast_multiply_fusion.1, f32[1024]{0:T(1024)S(1)} %bitcast.294, bf16[256,4096]{1,0:T(8,128)(2,1)S(1)} %fusion.6, ...), kind=kOutput, calls=%fused_computation.90 | convolution fusion | flops 2149317376 | bytes 12594176 | tf_op jit(solution)/shard_map/gle,de->gld/dot_general | solution.py:542
  255.5 2.1 copy.106
  257.6 1.7 convolution_convert_fusion.12
  262.3 5.1 fusion.45
  271.1 2.0 copy.107
  273.1 3.1 convolution_convert_fusion.4
  276.2 3.4 fusion.27
  279.6 2.1 convolution_convert_fusion.5
  281.7 2.9 convolution_convert_fusion.6
  284.6 1.6 multiply_reduce_fusion
  294.1 1.7 fusion.19
  298.4 1.9 add_bitcast_fusion
  300.4 38.0 %psum.7 = f32[4097]{0:T(1024)S(1)} all-reduce(f32[4097]{0:T(1024)S(1)} %constant_dynamic-update-slice_fusion), channel_id=1, replica_groups=mesh['dp'=4,'fsdp'=8] {'dp','fsdp'}, use_global_device_ids=true, to_apply=%region_27.28 | all-reduce | flops 4097 | bytes 32776 | tf_op jit(solution)/shard_map/psum | solution.py:887
  340.2 4.1 convolution_convert_fusion.7
  344.3 2.2 convolution_convert_fusion.8
  346.6 4.7 convolution_convert_fusion.2
  351.3 5.3 convolution_convert_fusion
  356.6 5.7 %convolution_convert_fusion.1 = bf16[1024,4096]{1,0:T(8,128)(2,1)} fusion(bf16[256,4096]{1,0:T(8,128)(2,1)S(1)} %copy-done.25, f32[1,256,1024]{2,1,0:T(8,128)S(1)} %copy-done.6, f32[1024]{0:T(1024)S(1)} %bitcast.296, f32[256]{0:T(256)S(1)} %fusion.76, f32[256]{0:T(256)S(1)} %broadcast_multiply_fusion.1), kind=kOutput, calls=%fused_computation.1 | convolution fusion | flops 2152726528 | bytes 11540480 | tf_op jit(solution)/shard_map/gld,gle->de/dot_general | solution.py:546
  362.3 154.8 %shard_map.285 = (f32[32,1024]{1,0:T(8,128)}, f32[32,1024]{1,0:T(8,128)}, f32[32,1024]{1,0:T(8,128)}, f32[32,1024]{1,0:T(8,128)}, f32[32,3072]{1,0:T(8,128)}, /*...) custom-call(bf16[2,2,4,2,32,1024]{5,4,3,2,1,0:T(8,128)(2,1)} %bitcast.261, ...), custom_call_target="tpu_custom_call" | custom-call | tf_op jit(solution)/shard_map/pallas_call | solution.py:512
  517.1 1.7 copy.139
  523.5 1.8 copy.143
  (191 shorter events, 49.0 us)
Async XLA Ops:
  0.6 4.4 copy-start.9
  3.5 195.3 %copy-start.2 = (f32[1,256,1024]{2,1,0:T(8,128)S(1)}, f32[1,256,1024]{2,1,0:T(8,128)}, u32[]{:S(2)}) copy-start(f32[1,256,1024]{2,1,0:T(8,128)} %param.19) | copy-start | bytes 3145732
  201.3 8.4 %copy-start.18 = (bf16[256,1024]{0,1:T(8,128)(2,1)}, bf16[256,1024]{0,1:T(8,128)(2,1)S(1)}, u32[]{:S(2)}) copy-start(bf16[256,1024]{0,1:T(8,128)(2,1)S(1)} %copy.102) | copy-start | bytes 1572868
  201.4 4.1 copy-start.47
  210.7 5.6 %slice-start.4 = ((s8[6291456]{0:T(1024)(128)(4,1)}), s8[4194304]{0:T(1024)(128)(4,1)S(1)}, s32[]{:S(2)}) async-start(s8[6291456]{0:T(1024)(128)(4,1)} %bitcast.326), calls=%async_computation.4 | async-start | bytes 8388608
  212.8 3.5 slice-start.5
  223.0 3.5 slice-start
  223.5 4.0 slice-start.1
  225.4 4.4 slice-start.2
  226.3 3.6 copy-start.4
  227.4 2.8 slice-start.3
  230.2 4.3 copy-start.50
  235.2 9.6 %copy-start.5 = (f32[1,256,1024]{2,1,0:T(8,128)S(1)}, f32[1,256,1024]{2,1,0:T(8,128)}, u32[]{:S(2)}) copy-start(f32[1,256,1024]{2,1,0:T(8,128)} %copy-done.4) | copy-start | bytes 3145732
  244.8 6.7 %copy-start.24 = (bf16[256,4096]{1,0:T(8,128)(2,1)}, bf16[256,4096]{1,0:T(8,128)(2,1)S(1)}, u32[]{:S(2)}) copy-start(bf16[256,4096]{1,0:T(8,128)(2,1)S(1)} %fusion.6) | copy-start | bytes 6291460
  259.2 3.0 copy-start.31
  262.0 5.4 %copy-start.33 = (bf16[8,128,256]{2,1,0:T(8,128)(2,1)}, bf16[8,128,256]{2,1,0:T(8,128)(2,1)S(1)}, u32[]{:S(2)}) copy-start(bf16[8,128,256]{2,1,0:T(8,128)(2,1)S(1)} %fusion.36) | copy-start | bytes 1572868
  262.3 5.1 copy-start.35
  273.1 3.1 copy-start.23
  276.2 3.4 copy-start.27
  281.7 2.9 copy-start.1
  281.7 2.9 copy-start.40
  288.4 3.5 copy-start.37
  288.4 2.5 copy-start.49
  288.9 3.1 copy-start.41
  298.4 41.8 %copy-start.11 = (bf16[1,512,1024]{2,1,0:T(8,128)(2,1)S(1)}, bf16[1,512,1024]{2,1,0:T(8,128)(2,1)}, u32[]{:S(2)}) copy-start(bf16[1,512,1024]{2,1,0:T(8,128)(2,1)} %param.20) | copy-start | bytes 3145732
  340.2 4.1 copy-start.38
  346.6 4.7 copy-start.43
  346.6 4.7 copy-start.51
  351.3 5.3 copy-start.6
  351.3 5.3 copy-start.25
  517.1 9.7 %copy-start.45 = (f32[32,4096]{1,0:T(8,128)S(1)}, f32[32,4096]{1,0:T(8,128)}, u32[]{:S(2)}) copy-start(f32[32,4096]{1,0:T(8,128)} %get-tuple-element.133) | copy-start | bytes 1572868
  517.1 10.5 %copy-start.44 = (f32[128,1024]{1,0:T(8,128)S(1)}, f32[128,1024]{1,0:T(8,128)}, u32[]{:S(2)}) copy-start(f32[128,1024]{1,0:T(8,128)} %get-tuple-element.134) | copy-start | bytes 1572868
  (26 other events, 43.9 us)

commit v2 on v1

--- a/solution.py
+++ b/solution.py
@@ -11,7 +11,9 @@
 DMA = pltpu.SemaphoreType.DMA
 UNIT_COLS = 1024
 UNIT_ROWS = 32
-WIDTHS = ((256, 256, 256, 256), (128, 128, 384, 384), (128, 128, 384, 384))
+RING = 4
+PARTIALS = 5
+WIDTHS = ((256, 256, 256, 256), (128, 128, 384, 384), (128, 128, 384, 384), (128, 128, 384, 384))
 
 
 class Place:
@@ -53,7 +55,7 @@
 
 
 def part_cols(u, p, base):
-    widths = WIDTHS[u % 3]
+    widths = WIDTHS[u % RING]
     return pl.ds(base + sum(widths[:p]), widths[p])
 
 
@@ -212,24 +214,15 @@
         self.s1, self.q1, self.s2, self.q2, self.zs, self.zr = sems
 
     @staticmethod
-    def scratch(n):
-        return [
-            pltpu.VMEM((n, 2, 2, 4, UNIT_ROWS, UNIT_COLS), jnp.bfloat16),
-            pltpu.VMEM((n, 2, 4, UNIT_ROWS, UNIT_COLS), jnp.bfloat16),
-            pltpu.VMEM((n, 4, UNIT_ROWS, UNIT_COLS), jnp.bfloat16),
-            pltpu.VMEM((n, 4, 2, UNIT_ROWS, UNIT_COLS), jnp.bfloat16),
-        ]
-
-    @staticmethod
     def sems(n):
         return [DMA((n, 4))] * 4 + [DMA((n, 4, 4))] * 2
 
     def pt(self, u, p, y, x, z):
-        return self.part.at[u, y, x, z, :, part_cols(u, p, 0)]
+        return self.part.at[u % PARTIALS, y, x, z, :, part_cols(u, p, 0)]
 
     def first(self, u, p):
         me, s = self.me, slice(None)
-        dst = self.r1.at[u, :, :, :, part_cols(u, p, 0)]
+        dst = self.r1.at[u % RING, :, :, :, part_cols(u, p, 0)]
         if p in (0, 2):
             return remote(self.pt(u, p, 1 - me.y, s, s), dst, self.s1.at[u, p], self.q1.at[u, p], me.dev(y=1 - me.y))
         return remote(self.pt(u, p, s, 1 - me.x, s), dst, self.s1.at[u, p], self.q1.at[u, p], me.dev(x=1 - me.x))
@@ -254,13 +247,13 @@
             dst = lambda i: self.pt(u, p, me.y, i // 4, i % 4)
         else:
             dst = lambda i: self.pt(u, p, i // 4, me.x, i % 4)
-        self.add(8, dst, [lambda i: self.r1.at[u, i // 4, i % 4, :, part_cols(u, p, 0)]])
+        self.add(8, dst, [lambda i: self.r1.at[u % RING, i // 4, i % 4, :, part_cols(u, p, 0)]])
 
     def second(self, u, p):
         me, s = self.me, slice(None)
         cols = part_cols(u, p, 0)
         z = s if p < 2 else me.z
-        dst = self.r2.at[u, :, :, cols] if p < 2 else self.r2.at[u, 0, :, cols]
+        dst = self.r2.at[u % RING, :, :, cols] if p < 2 else self.r2.at[u % RING, 0, :, cols]
         if p in (0, 2):
             return remote(self.pt(u, p, me.y, 1 - me.x, z), dst, self.s2.at[u, p], self.q2.at[u, p], me.dev(x=1 - me.x))
         return remote(self.pt(u, p, 1 - me.y, me.x, z), dst, self.s2.at[u, p], self.q2.at[u, p], me.dev(y=1 - me.y))
@@ -271,7 +264,7 @@
         self.add(
             4,
             lambda i: self.pt(u, p, me.y, me.x, i),
-            [lambda i: self.r2.at[u, i, :, part_cols(u, p, 0)]],
+            [lambda i: self.r2.at[u % RING, i, :, part_cols(u, p, 0)]],
         )
 
     def zblk(self, u, p, z):
@@ -280,7 +273,7 @@
 
     def zslot(self, u, p, slot):
         cols = part_cols(u, p, 0)
-        return self.rz.at[u, slot, 0, :, cols] if p < 2 else self.rz.at[u, slot, :, :, cols]
+        return self.rz.at[u % RING, slot, 0, :, cols] if p < 2 else self.rz.at[u % RING, slot, :, :, cols]
 
     def zcopy(self, u, p, which, block, slot, z_to):
         return remote(
@@ -336,7 +329,7 @@
             dst, count = (lambda i: self.pt(u, p, me.y, i, block)), 2
         else:
             dst, count = (lambda i: self.pt(u, p, i, me.x, block)), 2
-        self.add(count, dst, [functools.partial(lambda slot, i: self.rz.at[u, slot, i, :, cols], k) for k in slots])
+        self.add(count, dst, [functools.partial(lambda slot, i: self.rz.at[u % RING, slot, i, :, cols], k) for k in slots])
 
     def z_in(self, u, p):
         me = self.me
@@ -355,7 +348,7 @@
         me, cols = self.me, part_cols(u, p, 0)
         self.z_in(u, p)
         f32 = lambda ref: ref[...].astype(jnp.float32)
-        total = f32(self.pt(u, p, me.y, me.x, me.z)) + f32(self.rz.at[u, 0, 0, :, cols]) + f32(self.rz.at[u, 1, 0, :, cols])
+        total = f32(self.pt(u, p, me.y, me.x, me.z)) + f32(self.rz.at[u % RING, 0, 0, :, cols]) + f32(self.rz.at[u % RING, 1, 0, :, cols])
 
         @pl.when(me.is_end)
         def _():
@@ -363,7 +356,7 @@
 
         @pl.when(~me.is_end)
         def _():
-            self.out(u, p)[...] = total + f32(self.rz.at[u, 2, 0, :, cols])
+            self.out(u, p)[...] = total + f32(self.rz.at[u % RING, 2, 0, :, cols])
 
     def pass_z(self, u, p):
         me = self.me
@@ -382,7 +375,7 @@
     def finish_last(self, u, p):
         me, cols = self.me, part_cols(u, p, 0)
         self.second(u, p).wait_recv()
-        total = self.pt(u, p, me.y, me.x, me.z)[...].astype(jnp.float32) + self.r2.at[u, 0, :, cols][...].astype(jnp.float32)
+        total = self.pt(u, p, me.y, me.x, me.z)[...].astype(jnp.float32) + self.r2.at[u % RING, 0, :, cols][...].astype(jnp.float32)
         self.out(u, p)[...] = total
 
     def stage(self, s, u):
@@ -430,102 +423,694 @@
                     c.wait_send()
 
 
-def gather_units(shards, fulls):
-    units = [(shards[i], fulls[i], 0, 0) for i in (1, 2, 0, 3)]
-    units += [(shards[4], fulls[4], 0, k * UNIT_COLS) for k in range(3)]
-    units += [(shards[5], fulls[5], 0, 0)]
-    units += [(shards[6], fulls[6], 0, k * UNIT_COLS) for k in range(4)]
-    units += [(shards[7], fulls[7], k * UNIT_ROWS, 0) for k in range(4)]
-    return units
-
-
-def gather_kernel(wide, *refs):
-    shards, fulls, sems = refs[:8], refs[8:16], refs[16:]
+EPS = 1e-05
+HEADS = 8
+GELU_A = 0.7978845608028654
+GELU_B = 0.044715
+NT = (((1,), (1,)), ((), ()))
+F32, BF16 = jnp.float32, jnp.bfloat16
+
+
+def matmul(a, b):
+    return jnp.dot(a, b, preferred_element_type=F32)
+
+
+def matmul_nt(a, b):
+    return lax.dot_general(a, b, NT, preferred_element_type=F32)
+
+
+def block(i, size):
+    return pl.ds(pl.multiple_of(i * size, size), size)
+
+
+def for_each(count, body):
+    def step(i, carry):
+        body(i)
+        return carry
+
+    lax.fori_loop(0, count, step, 0)
+
+
+def normalise(v):
+    center = v - jnp.mean(v, axis=-1, keepdims=True)
+    inv = lax.rsqrt(jnp.mean(center * center, axis=-1, keepdims=True) + EPS)
+    return center * inv, inv
+
+
+def ln_forward(src, gain, dst):
+    def body(i):
+        rows = block(i, 32)
+        n, _ = normalise(src[rows, :].astype(F32))
+        dst[rows, :] = (n * gain[...]).astype(BF16)
+
+    for_each(src.shape[0] // 32, body)
+
+
+def ln_backward(src, row0, gain, incoming, base, gain_grad):
+    def body(i):
+        rows = block(i, 32)
+        n, inv = normalise(src[pl.ds(pl.multiple_of(row0 + i * 32, 32), 32), :].astype(F32))
+        g = incoming[rows, :]
+        e = g * gain[...]
+        grad = inv * (e - jnp.mean(e, axis=-1, keepdims=True) - n * jnp.mean(e * n, axis=-1, keepdims=True))
+        prod = g * n
+        gain_grad[...] += prod[0:8] + prod[8:16] + prod[16:24] + prod[24:32]
+        if base is None:
+            incoming[rows, :] = grad
+        else:
+            base[rows, :] = base[rows, :] + grad
+
+    for_each(incoming.shape[0] // 32, body)
+
+
+def attend_forward_heads(q, q0, k, k0, v, v0, out, count):
+    def body(h):
+        def head(ref, at):
+            return ref[:, pl.ds(pl.multiple_of(at + h * 128, 128), 128)]
+
+        s = matmul_nt(head(q, q0), head(k, k0)) * 128 ** (-0.5)
+        if count is not None:
+            s = jnp.where(lax.broadcasted_iota(jnp.int32, s.shape, 1) < count, s, -1e30)
+        e = jnp.exp(s - jnp.max(s, axis=-1, keepdims=True))
+        p = (e * (1.0 / jnp.sum(e, axis=-1, keepdims=True))).astype(BF16)
+        out[:, block(h, 128)] = matmul(p, head(v, v0)).astype(BF16)
+
+    for_each(HEADS, body)
+
+
+def attend_backward_heads(q, q0, k, k0, v, v0, mixed_grad, count, dq, dq0, dk, dk0, dv, dv0):
+    scale = 128 ** (-0.5)
+
+    def body(h):
+        def head(ref, at):
+            return ref[:, pl.ds(pl.multiple_of(at + h * 128, 128), 128)]
+
+        qh, kh, vh, gh = head(q, q0), head(k, k0), head(v, v0), head(mixed_grad, 0)
+        s = matmul_nt(kh, qh) * scale
+        if count is not None:
+            s = jnp.where(lax.broadcasted_iota(jnp.int32, s.shape, 0) < count, s, -1e30)
+        e = jnp.exp(s - jnp.max(s, axis=0, keepdims=True))
+        p = e * (1.0 / jnp.sum(e, axis=0, keepdims=True))
+        dv[:, pl.ds(pl.multiple_of(dv0 + h * 128, 128), 128)] = matmul(p.astype(BF16), gh).astype(BF16)
+        dp = matmul_nt(vh, gh)
+        ds = (p * (dp - jnp.sum(dp * p, axis=0, keepdims=True))).astype(BF16)
+        dk[:, pl.ds(pl.multiple_of(dk0 + h * 128, 128), 128)] = (matmul(ds, qh) * scale).astype(BF16)
+        dq[:, pl.ds(pl.multiple_of(dq0 + h * 128, 128), 128)] = (matmul(kh.T, ds).T * scale).astype(BF16)
+
+    for_each(HEADS, body)
+
+
+class SmallGather:
+    def __init__(self, me, full, send, recv):
+        self.me, self.full, self.send, self.recv = me, full, send, recv
+
+    def copy(self, src, k, r, dev):
+        return remote(src, src, self.send.at[k], self.recv.at[r], dev)
+
+    def sib(self, out=True):
+        me = self.me
+        return self.copy(self.full.at[me.y, me.x, me.z, me.c if out else 1 - me.c], 0, 0, me.dev(c=1 - me.c))
+
+    def zc(self, blk, k, r, to):
+        me = self.me
+        return self.copy(self.full.at[me.y, me.x, blk], k, r, me.dev(z=to))
+
+    def xc(self, out=True):
+        me = self.me
+        return self.copy(self.full.at[me.y, me.x if out else 1 - me.x], 5, 5, me.dev(x=1 - me.x))
+
+    def yc(self, out=True):
+        me = self.me
+        return self.copy(self.full.at[me.y if out else 1 - me.y], 6, 6, me.dev(y=1 - me.y))
+
+    def run(self, s):
+        me = self.me
+        if s == 0:
+            self.sib().start()
+        elif s == 1:
+            self.sib(False).wait_recv()
+            self.zc(me.z, 1, 1 + me.z, me.z1).start()
+            self.zc(me.z, 2, 1 + me.z, me.z2).start()
+
+            @pl.when(~me.is_end)
+            def _():
+                self.zc(me.z, 3, 1 + me.z, me.z3).start()
+
+        elif s == 2:
+
+            @pl.when(~me.is_end)
+            def _():
+                self.zc(me.z3, 4, 1 + me.z3, me.z1).wait_recv()
+                self.zc(me.z3, 4, 1 + me.z3, me.z1).start()
+
+            for z in (me.z1, me.z2):
+                self.zc(z, 1, 1 + z, me.z1).wait_recv()
+
+            @pl.when(me.is_end)
+            def _():
+                self.zc(me.z3, 1, 1 + me.z3, me.z1).wait_recv()
+
+            self.xc().start()
+        elif s == 3:
+            self.xc(False).wait_recv()
+            self.yc().start()
+        elif s == 4:
+            self.yc(False).wait_recv()
+            self.sib().wait_send()
+            self.zc(me.z, 1, 1 + me.z, me.z1).wait_send()
+            self.zc(me.z, 2, 1 + me.z, me.z2).wait_send()
+
+            @pl.when(~me.is_end)
+            def _():
+                self.zc(me.z, 3, 1 + me.z, me.z3).wait_send()
+                self.zc(me.z3, 4, 1 + me.z3, me.z1).wait_send()
+
+            self.xc().wait_send()
+            self.yc().wait_send()
+
+
+class SmallSum:
+    def __init__(self, me, acc, got, send, recv):
+        z_near = jnp.where(me.is_end, me.z1, me.z1)
+        z_far = jnp.where(me.is_end, me.z2, me.z3)
+        self.devs = [me.dev(c=1 - me.c), me.dev(x=1 - me.x), me.dev(y=1 - me.y), me.dev(z=z_near), me.dev(z=z_far)]
+        self.acc, self.got, self.send, self.recv = acc, got, send, recv
+
+    def copy(self, k):
+        return remote(self.acc, self.got.at[k], self.send.at[k], self.recv.at[k], self.devs[k])
+
+    def start(self, k):
+        self.copy(k).start()
+
+    def finish(self, k):
+        c = self.copy(k)
+        c.wait_send()
+        c.wait_recv()
+        self.acc[...] += self.got[k]
+
+
+def mega_kernel(*refs):
+    it = iter(refs)
+    take = lambda n: [next(it) for _ in range(n)]
+    latents, pixels, counts, cotangent, gain_block = take(5)
+    shards = take(8)
+    latents_out, latents_grad, pixels_grad, small_out = take(4)
+    grads_out = take(8)
+    fulls = take(8)
+    (
+        w_buf, wd_buf, part, r1, r2, rz,
+        xt_normed, xt_pix, xt_mixed, xt_nself, xt_smixed, xt_nmlp, xt_act, st_a, st_b,
+        g_out, g_out_in, hid, hid_in, g_branch, g_branch_in, act, packed_in, g_cross, g_cross_in,
+        dq, dq_in, big, dk_in, dv, dv_in,
+        queries, keys, values, packed, after_cross, after_self, resid, pix, tmp, acc,
+        gain_full, gain_vec, gain_acc, small, small_got,
+    ) = take(46)
+    gather_sems, scatter_sems = take(9), take(6)
+    w_sem, wd_sem, in_sem, out_sem, sg_s, sg_r, ss_s, ss_r, xl, xs, xr, gs, gr = take(13)
     me = Place()
     me.barrier()
-    gather = Gather(me, gather_units(shards, fulls), sems)
-    for t in range(gather.ticks(wide)):
-        gather.tick(t, wide)
+
+    cross_units = [(shards[i], fulls[i], 0, 0) for i in (1, 2, 0, 3)]
+    self_units = [(shards[4], fulls[4], 0, k * UNIT_COLS) for k in range(3)] + [(shards[5], fulls[5], 0, 0)]
+    mlp_units = [(shards[6], fulls[6], 0, k * UNIT_COLS) for k in range(4)]
+    mlp_units += [(shards[7], fulls[7], k * UNIT_ROWS, 0) for k in range(4)]
+    gather = Gather(me, cross_units + self_units + mlp_units, gather_sems)
+    scatter_units = [(grads_out[7], k * UNIT_ROWS, 0) for k in range(4)]
+    scatter_units += [(grads_out[6], 0, k * UNIT_COLS) for k in range(4)]
+    scatter_units += [(grads_out[5], 0, 0)] + [(grads_out[4], 0, k * UNIT_COLS) for k in range(3)]
+    scatter_units += [(grads_out[i], 0, 0) for i in (3, 2, 1, 0)]
+    scatter = Scatter(me, scatter_units, (part, r1, r2, rz), scatter_sems)
+    pushed = [0]
+    tick = [0]
+
+    def gather_to(t):
+        while tick[0] <= min(t, gather.ticks(1) - 1):
+            gather.tick(tick[0], 1)
+            tick[0] += 1
+
+    def arrived(u):
+        gather_to(u + Gather.STAGES - 1)
+
+    def settle(last):
+        for s in range(Scatter.STAGES - 1, 0, -1):
+            if 0 <= last - s < len(scatter_units):
+                scatter.stage(s, last - s)
+
+    def load(k, src, dst):
+        return pltpu.make_async_copy(src, dst, in_sem.at[k])
+
+    loads = [load(0, latents.at[0], after_self), load(1, pixels.at[0], pix), load(2, cotangent.at[0], resid)]
+    for c in loads:
+        c.start()
+    own_gain = pltpu.make_async_copy(gain_block, gain_full.at[me.y, me.x, me.z, me.c], in_sem.at[3])
+    own_gain.start()
+    own_gain.wait()
+    gains = SmallGather(me, gain_full, sg_s, sg_r)
+    gains.run(0)
+    gather_to(0)
+    gains.run(1)
+    gather_to(1)
+    gains.run(2)
+    gains.run(3)
+    gather_to(2)
+    gains.run(4)
+    table = jnp.sum(gain_full[...].reshape(32, 8, 128), axis=1).astype(BF16)
+    width = latents.shape[2]
+    lane = lax.broadcasted_iota(jnp.int32, (128, width), 1)
+    place = lax.broadcasted_iota(jnp.int32, (128, width), 0)
+    owner = lax.broadcasted_iota(jnp.int32, (32, width), 0) == (lax.broadcasted_iota(jnp.int32, (32, width), 1) >> 5)
+    for g in range(4):
+        pick = jnp.where(place == (lane & 31) + 32 * g, 1.0, 0.0).astype(BF16)
+        spread = jnp.where(owner, matmul(table, pick), 0.0)
+        gain_vec[g : g + 1, :] = jnp.sum(spread, axis=0, keepdims=True)
+    gain = [gain_vec.at[g : g + 1, :] for g in range(4)]
+    for g in range(4):
+        gain_acc[g] = jnp.zeros_like(gain_acc[g])
+
+    staged = [None, None]
+
+    def hand_over(k, stage, mine, slot, own_dst, far_dst):
+        a = pltpu.make_async_copy(mine, own_dst, xl.at[k])
+        b = remote(stage, far_dst, xs.at[k], xr.at[k], me.dev(c=1 - me.c))
+        a.start()
+        b.start()
+        staged[slot] = (a, b)
+
+    def clear(slot):
+        if staged[slot] is not None:
+            a, b = staged[slot]
+            a.wait()
+            b.wait_send()
+            staged[slot] = None
+
+    turn = [0]
+
+    def transpose_out(k, x, row0, xt, k_rows):
+        slot = turn[0] % 2
+        turn[0] += 1
+        clear(slot)
+
+        def body(j):
+            piece = x[pl.ds(row0, 256), block(j, 256)].T
+            st_b[slot, j // 2, j % 2] = piece.reshape(4, 2, 32, 256)
+
+        for_each(4, body)
+        hand_over(
+            k,
+            st_b.at[slot, :, :, :, 1 - me.c],
+            st_b.at[slot, :, :, :, me.c],
+            slot,
+            xt.at[:, :, :, :, pl.ds(row0, 256)],
+            xt.at[:, :, :, :, pl.ds(k_rows + row0, 256)],
+        )
+
+    def xt_wait(k, xt, row0, k_rows):
+        remote(
+            st_b.at[0, :, :, :, 0],
+            xt.at[:, :, :, :, pl.ds(k_rows + row0, 256)],
+            xs.at[k],
+            xr.at[k],
+            me.dev(c=1 - me.c),
+        ).wait_recv()
+
+    def swap(k, src, dst):
+        return remote(src, dst, gs.at[k], gr.at[k], me.dev(c=1 - me.c))
+
+    w_turn = [0]
+
+    def w_start(full, col):
+        slot = w_turn[0] % 2
+        w_turn[0] += 1
+        c = pltpu.make_async_copy(full.at[:, :, :, :, :, pl.ds(col, UNIT_COLS)], w_buf.at[slot], w_sem.at[slot])
+        c.start()
+        return slot, c
+
+    def w_fetch(full, col):
+        slot, c = w_start(full, col)
+        c.wait()
+        return slot
+
+    def w_cols(slot, j):
+        return w_buf[slot, :, :, :, :, :, block(j, 256)].reshape(width, 256)
+
+    def w_rows(slot, j):
+        return w_buf[slot, j // 2, j % 2].reshape(256, UNIT_COLS)
+
+    def project(x, slot, out):
+        for_each(4, lambda j: out(j, matmul(x[...], w_cols(slot, j))))
+
+    def store(dst, col0=0):
+        def put(j, tile):
+            dst[:, pl.ds(pl.multiple_of(col0 + j * 256, 256), 256)] = tile.astype(dst.dtype)
+
+        return put
+
+    def back(g, col0, slot, dst, first):
+        def body(j):
+            tile = matmul_nt(g[:, pl.ds(col0, UNIT_COLS)], w_rows(slot, j))
+            cols = block(j, 256)
+            if first:
+                dst[:, cols] = tile.astype(dst.dtype)
+            else:
+                dst[:, cols] = dst[:, cols] + tile
+
+        for_each(4, body)
+
+    def weight_grad(xt_at, rows, own, far, col0):
+        u = pushed[0]
+        if u >= PARTIALS:
+            scatter.sent(u - PARTIALS)
+        slot = u % PARTIALS
+
+        def body(j):
+            cols = pl.ds(pl.multiple_of(col0 + j * 256, 256), 256)
+            total = matmul(xt_at(0), own[:, cols]) + matmul(xt_at(rows), far[:, cols])
+            part[slot, :, :, :, :, block(j, 256)] = total.astype(BF16).reshape(2, 2, 4, UNIT_ROWS, 256)
+
+        for_each(4, body)
+        scatter.stage(0, u)
+        pushed[0] += 1
+
+    def xt_of(xt, rows):
+        return lambda at: xt[:, :, :, :, pl.ds(at, rows)].reshape(512, rows)
+
+    loads[0].wait()
+    loads[1].wait()
+    ln_forward(after_self, gain[0], tmp)
+    transpose_out(0, tmp, 0, xt_normed, 256)
+    gather_to(3)
+    ln_forward(pix, gain[1], big)
+    transpose_out(1, big, 0, xt_pix, 512)
+    gather_to(4)
+    transpose_out(2, big, 256, xt_pix, 512)
+    count = counts[0]
+    arrived(0)
+    project(big, w_fetch(fulls[1], 0), store(keys))
+    arrived(1)
+    project(big, w_fetch(fulls[2], 0), store(values))
+    loads[2].wait()
+    for_each(8, lambda i: g_out.__setitem__((block(i, 32), slice(None)), resid[block(i, 32), :].astype(BF16)))
+    swap(0, g_out, g_out_in).start()
+    arrived(2)
+    project(tmp, w_fetch(fulls[0], 0), store(queries))
+    attend_forward_heads(queries, 0, keys, 0, values, 0, tmp, count)
+    arrived(3)
+    transpose_out(3, tmp, 0, xt_mixed, 256)
+
+    def add_to(dst, src):
+        def put(j, tile):
+            dst[:, block(j, 256)] = src[:, block(j, 256)] + tile
+
+        return put
+
+    project(tmp, w_fetch(fulls[3], 0), add_to(after_cross, after_self))
+
+    ln_forward(after_cross, gain[2], tmp)
+    transpose_out(4, tmp, 0, xt_nself, 256)
+    for k in range(3):
+        arrived(4 + k)
+        project(tmp, w_fetch(fulls[4], k * UNIT_COLS), store(packed, k * UNIT_COLS))
+    attend_forward_heads(packed, 0, packed, UNIT_COLS, packed, 2 * UNIT_COLS, tmp, None)
+    arrived(7)
+    transpose_out(5, tmp, 0, xt_smixed, 256)
+    project(tmp, w_fetch(fulls[5], 0), add_to(after_self, after_cross))
+
+    ln_forward(after_self, gain[3], tmp)
+    transpose_out(6, tmp, 0, xt_nmlp, 256)
+    a_staged = [None, None]
+
+    def act_out(k):
+        slot = k % 2
+        if a_staged[slot] is not None:
+            a_staged[slot][0].wait()
+            a_staged[slot][1].wait_send()
+
+        def body(m):
+            st_a[slot, m // 2, m % 2] = act[:, pl.ds(pl.multiple_of(k * UNIT_COLS + m * 128, 128), 128)].T
+
+        for_each(8, body)
+        a = pltpu.make_async_copy(st_a.at[slot, :, me.c], xt_act.at[k // 2, k % 2, :, :, pl.ds(0, 256)], xl.at[7 + k])
+        b = remote(
+            st_a.at[slot, :, 1 - me.c],
+            xt_act.at[k // 2, k % 2, :, :, pl.ds(256, 256)],
+            xs.at[7 + k],
+            xr.at[7 + k],
+            me.dev(c=1 - me.c),
+        )
+        a.start()
+        b.start()
+        a_staged[slot] = (a, b)
+        return a, b
+
+    act_copies = []
+    for k in range(4):
+        arrived(8 + k)
+        slot = w_fetch(fulls[6], k * UNIT_COLS)
+
+        def up(j):
+            x = matmul(tmp[...], w_cols(slot, j))
+            t = jnp.tanh(GELU_A * (x + GELU_B * (x * x * x)))
+            half = 0.5 * (1.0 + t)
+            cols = pl.ds(pl.multiple_of(k * UNIT_COLS + j * 256, 256), 256)
+            act[:, cols] = (x * half).astype(BF16)
+            slope = half + (0.5 * GELU_A) * x * (1.0 - t * t) * (1.0 + (3 * GELU_B) * (x * x))
+            hid[:, cols] = slope.astype(BF16)
+
+        for_each(4, up)
+        act_copies.append(act_out(k))
+    for k in range(2, 4):
+        a_staged[k % 2][0].wait()
+        a_staged[k % 2][1].wait_send()
+    for k in range(4):
+        act_copies[k][1].wait_recv()
+
+    for slot in range(2):
+        clear(slot)
+
+    swap(0, g_out, g_out_in).wait_recv()
+    for k in range(4):
+        def xt_down(at, k=k):
+            return xt_act[:, :, :, pl.ds(k * UNIT_ROWS, UNIT_ROWS), pl.ds(at, 256)].reshape(512, 256)
+
+        weight_grad(xt_down, 256, g_out, g_out_in, 0)
+        arrived(12 + k)
+        settle(k)
+
+    def wd_start(q):
+        c = pltpu.make_async_copy(fulls[7].at[q // 2, q % 2], wd_buf.at[q % 2], wd_sem.at[q % 2])
+        c.start()
+        return c
+
+    wd = [wd_start(0), wd_start(1), None, None]
+    for q in range(4):
+        wd[q].wait()
+
+        def hidden_back(j):
+            w = wd_buf[q % 2, j].reshape(256, width)
+            tile = matmul_nt(g_out[...], w)
+            cols = pl.ds(pl.multiple_of(q * UNIT_COLS + j * 256, 256), 256)
+            hid[:, cols] = (hid[:, cols].astype(F32) * tile).astype(BF16)
+
+        for_each(4, hidden_back)
+        cols = pl.ds(q * UNIT_COLS, UNIT_COLS)
+        swap(1 + q, hid.at[:, cols], hid_in.at[:, cols]).start()
+
+        def down(j):
+            w = wd_buf[q % 2, :, :, :, block(j, 256)].reshape(UNIT_COLS, 256)
+            tile = matmul(act[:, pl.ds(q * UNIT_COLS, UNIT_COLS)], w)
+            dst = block(j, 256)
+            acc[0, :, dst] = (after_self[:, dst] if q == 0 else acc[0, :, dst]) + tile
+
+        for_each(4, down)
+        if q < 2:
+            wd[q + 2] = wd_start(q + 2)
+    xt_wait(6, xt_nmlp, 0, 256)
+    pending = [w_start(fulls[6], 0), None]
+    out_copy = pltpu.make_async_copy(acc.at[0], latents_out.at[0], out_sem.at[0])
+    out_copy.start()
+    small[...] = jnp.zeros_like(small)
+    squares = jnp.zeros((8, width), F32)
+
+    def square(i, total):
+        v = acc[0, block(i, 8), :]
+        return total + v * v
+
+    squares = lax.fori_loop(0, 32, square, squares)
+    mean_square = jnp.sum(jnp.sum(squares, axis=1, keepdims=True), axis=0, keepdims=True) / (latents.shape[1] * width)
+    root_mean = jnp.sqrt(mean_square)
+    small[5:6, :] = jnp.broadcast_to(root_mean, (1, width))
+    for k in range(4):
+        cols = pl.ds(k * UNIT_COLS, UNIT_COLS)
+        swap(1 + k, hid.at[:, cols], hid_in.at[:, cols]).wait_recv()
+        weight_grad(xt_of(xt_nmlp, 256), 256, hid, hid_in, k * UNIT_COLS)
+        slot, c = pending[k % 2]
+        c.wait()
+        if k < 3:
+            pending[(k + 1) % 2] = w_start(fulls[6], (k + 1) * UNIT_COLS)
+        back(hid, k * UNIT_COLS, slot, acc.at[1], k == 0)
+        settle(4 + k)
+    ln_backward(after_self, 0, gain[3], acc.at[1], resid, gain_acc.at[3])
+
+    def round_rows(dst):
+        for_each(8, lambda i: dst.__setitem__((block(i, 32), slice(None)), resid[block(i, 32), :].astype(BF16)))
+
+    so_slot, c_so = w_start(fulls[5], 0)
+    round_rows(g_branch)
+    swap(5, g_branch, g_branch_in).start()
+    c_so.wait()
+    back(g_branch, 0, so_slot, tmp, True)
+    swap(5, g_branch, g_branch_in).wait_recv()
+    xt_wait(5, xt_smixed, 0, 256)
+    weight_grad(xt_of(xt_smixed, 256), 256, g_branch, g_branch_in, 0)
+    settle(8)
+    qkv_w = w_start(fulls[4], 0)
+    attend_backward_heads(
+        packed, 0, packed, UNIT_COLS, packed, 2 * UNIT_COLS, tmp, None, act, 0, act, UNIT_COLS, act, 2 * UNIT_COLS
+    )
+    packed_grad = act.at[:, pl.ds(0, 3 * UNIT_COLS)]
+    swap(6, packed_grad, packed_in).start()
+    swap(6, packed_grad, packed_in).wait_recv()
+    xt_wait(4, xt_nself, 0, 256)
+    out_copy.wait()
+    for k in range(3):
+        weight_grad(xt_of(xt_nself, 256), 256, act, packed_in, k * UNIT_COLS)
+        slot, c = qkv_w
+        c.wait()
+        if k < 2:
+            qkv_w = w_start(fulls[4], (k + 1) * UNIT_COLS)
+        back(act, k * UNIT_COLS, slot, acc.at[0], k == 0)
+        settle(9 + k)
+    wo_slot, c_wo = w_start(fulls[3], 0)
+    ln_backward(after_cross, 0, gain[2], acc.at[0], resid, gain_acc.at[2])
+    again = load(0, latents.at[0], after_self)
+    again.start()
+
+    round_rows(g_cross)
+    swap(7, g_cross, g_cross_in).start()
+    c_wo.wait()
+    back(g_cross, 0, wo_slot, tmp, True)
+    swap(7, g_cross, g_cross_in).wait_recv()
+    xt_wait(3, xt_mixed, 0, 256)
+    weight_grad(xt_of(xt_mixed, 256), 256, g_cross, g_cross_in, 0)
+    settle(12)
+    attend_backward_heads(queries, 0, keys, 0, values, 0, tmp, count, dq, 0, big, 0, dv, 0)
+    given = [swap(8, dv, dv_in), swap(9, big, dk_in), swap(10, dq, dq_in)]
+    for c in given:
+        c.start()
+    w_q = w_start(fulls[0], 0)
+    xt_wait(1, xt_pix, 0, 512)
+    xt_wait(2, xt_pix, 256, 512)
+    given[0].wait_recv()
+    weight_grad(xt_of(xt_pix, 512), 512, dv, dv_in, 0)
+    settle(13)
+    given[1].wait_recv()
+    weight_grad(xt_of(xt_pix, 512), 512, big, dk_in, 0)
+    settle(14)
+    xt_wait(0, xt_normed, 0, 256)
+    given[2].wait_recv()
+    weight_grad(xt_of(xt_normed, 256), 256, dq, dq_in, 0)
+    settle(15)
+    w_q[1].wait()
+    w_k = w_start(fulls[1], 0)
+    back(dq, 0, w_q[0], acc.at[0], True)
+    again.wait()
+    ln_backward(after_self, 0, gain[0], acc.at[0], resid, gain_acc.at[0])
+    grad_copy = pltpu.make_async_copy(resid, latents_grad.at[0], out_sem.at[1])
+    grad_copy.start()
+    settle(16)
+    w_v = w_start(fulls[2], 0)
+    w_k[1].wait()
+    for r in range(2):
+        back(big.at[pl.ds(256 * r, 256)], 0, w_k[0], acc.at[r], True)
+    settle(17)
+    w_v[1].wait()
+    pix_copies = []
+    for r in range(2):
+        back(dv.at[pl.ds(256 * r, 256)], 0, w_v[0], acc.at[r], False)
+        ln_backward(pix, 256 * r, gain[1], acc.at[r], None, gain_acc.at[1])
+        c = pltpu.make_async_copy(acc.at[r], pixels_grad.at[0, pl.ds(256 * r, 256)], out_sem.at[2 + r])
+        c.start()
+        pix_copies.append(c)
+    for g in range(4):
+        small[g : g + 1, :] = jnp.sum(gain_acc[g], axis=0, keepdims=True)
+    small[4:5, :] = small[5:6, :]
+    total = SmallSum(me, small, small_got, ss_s, ss_r)
+    total.start(0)
+    settle(18)
+    total.finish(0)
+    total.start(1)
+    settle(19)
+    for k in range(1, 5):
+        total.finish(k)
+        if k < 4:
+            total.start(k + 1)
+    small[5:6, :] = jnp.broadcast_to(root_mean, (1, width))
+    small_out[...] = small[...]
+
     for u in range(len(gather.units)):
         gather.sent(u)
-
-
-def gather_all(shards, wide=4):
-    outs = [jax.ShapeDtypeStruct((2, 2, 4, 2) + s.shape, s.dtype) for s in shards]
-    return pl.pallas_call(
-        functools.partial(gather_kernel, wide),
+    for u in range(len(scatter_units) - PARTIALS, len(scatter_units)):
+        scatter.sent(u)
+    swap(0, g_out, g_out_in).wait_send()
+    for q in range(4):
+        cols = pl.ds(q * UNIT_COLS, UNIT_COLS)
+        swap(1 + q, hid.at[:, cols], hid_in.at[:, cols]).wait_send()
+    swap(5, g_branch, g_branch_in).wait_send()
+    swap(6, packed_grad, packed_in).wait_send()
+    swap(7, g_cross, g_cross_in).wait_send()
+    for c in given:
+        c.wait_send()
+    grad_copy.wait()
+    for c in pix_copies:
+        c.wait()
+
+
+def mega(latents, pixels, counts, cotangent, gain_block, shards):
+    rows, slots, width = latents.shape[1], pixels.shape[1], latents.shape[2]
+    hidden = shards[6].shape[1]
+    vm = pltpu.VMEM
+    xt = lambda k: vm((2, 2, 4, UNIT_ROWS, k), BF16)
+    wide = lambda n: vm((rows, n), BF16)
+    scratch = [
+        vm((2, 2, 2, 4, 2, UNIT_ROWS, UNIT_COLS), BF16),
+        vm((2, 4, 2, 128, UNIT_COLS), BF16),
+        vm((PARTIALS, 2, 2, 4, UNIT_ROWS, UNIT_COLS), BF16),
+        vm((RING, 2, 4, UNIT_ROWS, UNIT_COLS), BF16),
+        vm((RING, 4, UNIT_ROWS, UNIT_COLS), BF16),
+        vm((RING, 4, 2, UNIT_ROWS, UNIT_COLS), BF16),
+        xt(2 * rows), xt(2 * slots), xt(2 * rows), xt(2 * rows), xt(2 * rows), xt(2 * rows),
+        vm((2, 2, 4, 128, 2 * rows), BF16),
+        vm((2, 4, 2, 128, rows), BF16),
+        vm((2, 2, 2, 4, 2, UNIT_ROWS, 256), BF16),
+        wide(width), wide(width), wide(hidden), wide(hidden), wide(width), wide(width), wide(hidden), wide(3 * width),
+        wide(width), wide(width),
+        wide(width), wide(width), vm((slots, width), BF16), vm((slots, width), BF16), vm((slots, width), BF16), vm((slots, width), BF16),
+        wide(width), vm((slots, width), BF16), vm((slots, width), BF16), wide(3 * width),
+        vm((rows, width), F32), vm((rows, width), F32), vm((rows, width), F32), vm((slots, width), BF16), wide(width), vm((2, rows, width), F32),
+        vm((2, 2, 4, 2, 8, 128), F32), vm((8, width), F32), vm((4, 8, width), F32), vm((8, width), F32), vm((5, 8, width), F32),
+    ]
+    sems = Gather.sems(16) + Scatter.sems(16)
+    sems += [DMA((2,)), DMA((2,)), DMA((4,)), DMA((4,)), DMA((7,)), DMA((7,)), DMA((5,)), DMA((5,))]
+    sems += [DMA((11,))] * 3 + [DMA((11,))] * 2
+    outs = [
+        jax.ShapeDtypeStruct(latents.shape, F32),
+        jax.ShapeDtypeStruct(latents.shape, F32),
+        jax.ShapeDtypeStruct(pixels.shape, F32),
+        jax.ShapeDtypeStruct((8, width), F32),
+    ]
+    outs += [jax.ShapeDtypeStruct(s.shape, F32) for s in shards]
+    outs += [jax.ShapeDtypeStruct((2, 2, 4, 2) + s.shape, s.dtype) for s in shards]
+    hbm, vmem = pl.BlockSpec(memory_space=pl.ANY), pl.BlockSpec(memory_space=pltpu.VMEM)
+    smem = pl.BlockSpec(memory_space=pltpu.SMEM)
+    results = pl.pallas_call(
+        mega_kernel,
         out_shape=outs,
-        in_specs=[pl.BlockSpec(memory_space=pl.ANY)] * 8,
-        out_specs=[pl.BlockSpec(memory_space=pl.ANY)] * 8,
-        scratch_shapes=Gather.sems(16),
-        compiler_params=pltpu.CompilerParams(collective_id=0, has_side_effects=True, vmem_limit_bytes=60 * 2**20),
-    )(*shards)
-
-
-def scatter_kernel(*refs):
-    grads, outs = refs[:8], refs[8:16]
-    part, r1, r2, rz, r0 = refs[16:21]
-    sems, (la, lb, ls, lr) = refs[21:27], refs[27:]
-    me = Place()
-    me.barrier()
-    units = [(outs[7], k * UNIT_ROWS, 0) for k in range(4)]
-    units += [(outs[6], 0, k * UNIT_COLS) for k in range(4)]
-    units += [(outs[4], 0, k * UNIT_COLS) for k in range(3)]
-    units += [(outs[i], 0, 0) for i in (5, 3, 0, 1, 2)]
-    which = [7] * 4 + [6] * 4 + [4] * 3 + [5, 3, 0, 1, 2]
-    sc = Scatter(me, units, (part, r1, r2, rz), sems)
-    n = len(units)
-
-    def mine(u):
-        _, row, col = units[u]
-        src = grads[which[u]].at[:, :, :, me.c, pl.ds(row, UNIT_ROWS), pl.ds(col, UNIT_COLS)]
-        return pltpu.make_async_copy(src, part.at[u], la.at[u])
-
-    def give(u):
-        _, row, col = units[u]
-        src = grads[which[u]].at[:, :, :, 1 - me.c, pl.ds(row, UNIT_ROWS), pl.ds(col, UNIT_COLS)]
-        return remote(src, r0.at[u], ls.at[u], lr.at[u], me.dev(c=1 - me.c))
-
-    for t in range(n + 6):
-        for s in (4, 3, 2, 1, 0, -1, -2):
-            u = t - (s + 2)
-            if not 0 <= u < n:
-                continue
-            if s == -2:
-                mine(u).start()
-                give(u).start()
-            elif s == -1:
-                mine(u).wait()
-                give(u).wait_recv()
-                idx = lambda i: (i // 8, (i // 4) % 2, i % 4)
-                sc.add(16, lambda i: part.at[(u,) + idx(i)], [lambda i: r0.at[(u,) + idx(i)]])
-                give(u).wait_send()
-            else:
-                sc.stage(s, u)
-    for u in range(n):
-        sc.sent(u)
-
-
-def scatter_all(grads):
-    outs = [jax.ShapeDtypeStruct(g.shape[4:], jnp.float32) for g in grads]
-    n = 16
-    return pl.pallas_call(
-        scatter_kernel,
-        out_shape=outs,
-        in_specs=[pl.BlockSpec(memory_space=pl.ANY)] * 8,
-        out_specs=[pl.BlockSpec(memory_space=pltpu.VMEM)] * 8,
-        scratch_shapes=Scatter.scratch(n)
-        + [pltpu.VMEM((n, 2, 2, 4, UNIT_ROWS, UNIT_COLS), jnp.bfloat16)]
-        + Scatter.sems(n)
-        + [DMA((n,))] * 4,
-        compiler_params=pltpu.CompilerParams(collective_id=1, has_side_effects=True, vmem_limit_bytes=62 * 2**20),
-    )(*grads)
-
-
-HEADS = 8
-
-
-EPS = 1e-05
+        in_specs=[hbm, hbm, smem, hbm, hbm] + [hbm] * 8,
+        out_specs=[hbm] * 3 + [vmem] + [vmem] * 8 + [hbm] * 8,
+        scratch_shapes=scratch + sems,
+        compiler_params=pltpu.CompilerParams(collective_id=0, has_side_effects=True, vmem_limit_bytes=63 * 2**20),
+    )(latents, pixels, counts, cotangent, gain_block, *shards)
+    return results[:4], results[4:12]
 
 
 def layer_norm(inputs, gain):
@@ -796,113 +1381,29 @@
     w_up,
     w_down,
 ):
-    groups = latents.shape[0]
-    slots = pixels.shape[1]
-    width = latents.shape[2]
-    local_slot = slot_index % groups
-    chosen = jnp.take(pixels, local_slot, axis=0).astype(jnp.float32)
-    visible_count = jnp.take(counts, local_slot, axis=0)
-    visible = lax.broadcasted_iota(jnp.int32, (groups, slots), 1) < visible_count[:, None]
-    gains = lax.all_gather(jnp.stack([gain_q, gain_kv, gain_self, gain_mlp]), ("dp", "fsdp"), axis=1, tiled=True)
+    gains = jnp.concatenate([gain_q, gain_kv, gain_self, gain_mlp]).astype(jnp.float32)
+    gain_block = jnp.pad(gains[None, :], ((0, 7), (0, 0)))
     shards = (w_query, w_key, w_value, w_out, w_qkv, w_self_out, w_up, w_down)
-    fulls = [f.reshape(-1, f.shape[-1]) for f in gather_all(shards)]
-    cross_all = (gains[0], gains[1], fulls[0], fulls[1], fulls[2], fulls[3])
-    self_all = (gains[2], fulls[4], fulls[5])
-    mlp_all = (gains[3], fulls[6], fulls[7])
-    cross_back, self_back, mlp_back = cross_all, self_all, mlp_all
-    normed = layer_norm(latents, cross_all[0].astype(jnp.float32)).astype(jnp.bfloat16)
-    pix_normed = layer_norm(chosen, cross_all[1].astype(jnp.float32)).astype(jnp.bfloat16)
-    queries = split_heads(project(normed, cross_all[2]).astype(jnp.bfloat16))
-    key_rows = split_heads(project(pix_normed, cross_all[3]).astype(jnp.bfloat16))
-    value_rows = split_heads(project(pix_normed, cross_all[4]).astype(jnp.bfloat16))
-    cross_mixed, cross_total = attend_forward(queries, key_rows, value_rows, visible)
-    cross_flat = merge_heads(cross_mixed)
-    after_cross = latents + project(cross_flat, cross_all[5])
-    normed_self = layer_norm(after_cross, self_all[0].astype(jnp.float32)).astype(jnp.bfloat16)
-    packed = project(normed_self, self_all[1]).astype(jnp.bfloat16)
-    self_queries = split_heads(packed[..., :width])
-    self_keys = split_heads(packed[..., width : 2 * width])
-    self_values = split_heads(packed[..., 2 * width :])
-    self_mixed, self_total = attend_forward(self_queries, self_keys, self_values, None)
-    self_flat = merge_heads(self_mixed)
-    after_self = after_cross + project(self_flat, self_all[2])
-    normed_mlp = layer_norm(after_self, mlp_all[0].astype(jnp.float32)).astype(jnp.bfloat16)
-    hidden = project(normed_mlp, mlp_all[1])
-    activated = jax.nn.gelu(hidden).astype(jnp.bfloat16)
-    latents_out = after_self + project(activated, mlp_all[2])
-    root_mean = jnp.sqrt(jnp.mean(latents_out * latents_out, axis=(1, 2)))
-    out_grad = cotangent.astype(jnp.bfloat16)
-    down_grad = weight_grad(activated, out_grad)
-    act_grad = project_back(out_grad, mlp_back[2])
-    hidden_grad = jax.vjp(jax.nn.gelu, hidden)[1](act_grad)[0].astype(jnp.bfloat16)
-    up_grad = weight_grad(normed_mlp, hidden_grad)
-    mlp_in_grad = project_back(hidden_grad, mlp_back[1])
-    after_self_ln, mlp_gain_grad = jax.vjp(layer_norm, after_self, mlp_back[0].astype(jnp.float32))[
-        1
-    ](mlp_in_grad)
-    after_self_grad = cotangent + after_self_ln
-    self_branch = after_self_grad.astype(jnp.bfloat16)
-    self_out_grad = weight_grad(self_flat, self_branch)
-    self_mixed_grad = split_heads(project_back(self_branch, self_back[2]).astype(jnp.bfloat16))
-    self_q_grad, self_k_grad, self_v_grad = attend_backward(
-        self_queries, self_keys, self_values, None, self_total, self_mixed_grad
-    )
-    packed_grad = jnp.concatenate(
-        [merge_heads(self_q_grad), merge_heads(self_k_grad), merge_heads(self_v_grad)], axis=-1
-    )
-    qkv_grad = weight_grad(normed_self, packed_grad)
-    self_in_grad = project_back(packed_grad, self_back[1])
-    after_cross_ln, self_gain_grad = jax.vjp(
-        layer_norm, after_cross, self_back[0].astype(jnp.float32)
-    )[1](self_in_grad)
-    after_cross_grad = after_self_grad + after_cross_ln
-    cross_branch = after_cross_grad.astype(jnp.bfloat16)
-    out_w_grad = weight_grad(cross_flat, cross_branch)
-    cross_mixed_grad = split_heads(project_back(cross_branch, cross_back[5]).astype(jnp.bfloat16))
-    query_grad, key_grad, value_grad = attend_backward(
-        queries, key_rows, value_rows, visible, cross_total, cross_mixed_grad
-    )
-    query_flat = merge_heads(query_grad)
-    key_flat = merge_heads(key_grad)
-    value_flat = merge_heads(value_grad)
-    query_w_grad = weight_grad(normed, query_flat)
-    key_w_grad = weight_grad(pix_normed, key_flat)
-    value_w_grad = weight_grad(pix_normed, value_flat)
-    normed_grad = project_back(query_flat, cross_back[2])
-    pix_normed_grad = project_back(key_flat, cross_back[3]) + project_back(
-        value_flat, cross_back[4]
-    )
-    latents_ln, query_gain_grad = jax.vjp(layer_norm, latents, cross_back[0].astype(jnp.float32))[
-        1
-    ](normed_grad)
-    latents_grad = after_cross_grad + latents_ln
-    chosen_grad, pixel_gain_grad = jax.vjp(layer_norm, chosen, cross_back[1].astype(jnp.float32))[
-        1
-    ](pix_normed_grad)
-    pixels_grad = jnp.zeros(pixels.shape, jnp.float32).at[local_slot].add(chosen_grad)
-    grads = (query_w_grad, key_w_grad, value_w_grad, out_w_grad, qkv_grad, self_out_grad, up_grad, down_grad)
-    blocks = [g.astype(jnp.bfloat16).reshape(2, 2, 4, 2, -1, g.shape[-1]) for g in grads]
-    g_query, g_key, g_value, g_out, g_qkv, g_self_out, g_up, g_down = scatter_all(blocks)
-    small = jnp.concatenate([query_gain_grad, pixel_gain_grad, self_gain_grad, mlp_gain_grad, root_mean])
-    small = lax.psum(small, ("dp", "fsdp"))
+    (latents_out, latents_grad, pixels_grad, small), grads = mega(latents, pixels, counts, cotangent, gain_block, shards)
     rows = gain_q.shape[0]
-    mine = lax.axis_index(("dp", "fsdp")) * rows
-    gain_grads = [lax.dynamic_slice(small, (k * width + mine,), (rows,)) for k in range(4)]
-    norms = root_mean * (groups * lax.axis_size(("dp", "fsdp"))) / jnp.sum(small[4 * width :])
+    devices = lax.axis_size(("dp", "fsdp"))
+    mine = lax.dynamic_slice(small[:4], (0, lax.axis_index(("dp", "fsdp")) * rows), (4, rows))
+    norms = small[5, :1] * devices / small[4, :1]
+    g_query, g_key, g_value, g_out, g_qkv, g_self_out, g_up, g_down = grads
     return (
         latents_out,
         latents_grad,
         pixels_grad,
-        gain_grads[0],
-        gain_grads[1],
+        mine[0],
+        mine[1],
         g_query,
         g_key,
         g_value,
         g_out,
-        gain_grads[2],
+        mine[2],
         g_qkv,
         g_self_out,
-        gain_grads[3],
+        mine[3],
         g_up,
         g_down,
         norms,

time: 539 us -> 348 us (0.65); the launches traced: 530 us -> 347 us
  matrix products: 91.7 us -> 0 us
  blocking collectives: 81.3 us -> 0 us
  Pallas kernels: 304 us -> 329 us
  local copies, waits for them, and re-layouts: 34 us -> 13.1 us
  other arithmetic: 13.6 us -> 1.37 us
    dot_general x36 -> x0, matrix products: 91.7 us -> none  [the longest x8 30.1 us: weight_grad(): jnp.einsum('gld,gle->de', inputs, grad_rows, preferred_element_type=jnp.f...]
    all_gather x1 -> x0, blocking collectives: 43.3 us -> none  [local_fast(): lax.all_gather(jnp.stack([gain_q, gain_kv, gain_self, gain_mlp]), ('dp',...]
    psum x1 -> x0, blocking collectives: 38 us -> none  [local_fast(): small = lax.psum(small, ('dp', 'fsdp'))]
    pallas_call x2 -> x1, Pallas kernels: 304 us -> 329 us  [mega(): pl.pallas_call(mega_kernel, out_shape=outs, in_specs=[hbm, hbm, smem, hbm...]
    unnamed x131 -> x31, local copies, waits for them, and re-layouts: 24.6 us -> 10.4 us
    another operation x6 -> x0, local copies, waits for them, and re-layouts: 8.24 us -> none
    reduce_sum x12 -> x0, other arithmetic: 7.68 us -> none  [the longest x5 2.76 us: layer_norm(): center = inputs - jnp.mean(inputs, axis=-1, keepdims=True)]
where the time goes in v2:
time: 348 us; the launch traced here: 347 us
  Pallas kernels  329 us (95%)
  local copies, waits for them, and re-layouts  13.1 us (4%)
  between operations  3.83 us (1%)
    pallas_call x1, Pallas kernels, mega(): pl.pallas_call(mega_kernel, out_shape=outs, in_specs=[hbm, hbm, smem, hbm...  329 us
    unnamed x31, local copies, waits for them, and re-layouts  10.4 us

profile of v2, /device:TPU:0, one launch (start us, length us, event | category | flops | bytes accessed | tf_op | source)
XLA Modules:
  0.0 347.2 jit_solution(3798989620720599648)
XLA Ops:
  0.6 1.4 fusion.7.refs_4_
  2.7 328.9 %shard_map.279 = (f32[1,256,1024]{2,1,0:T(8,128)}, f32[1,256,1024]{2,1,0:T(8,128)}, f32[1,512,1024]{2,1,0:T(8,128)}, f32[8,1024]{1,0:T(8,128)}, f32[32,1024]{1,0...) custom-call(f32[1,256,1024]{2,1,0:T(8,128)} %refs_0_.1, ...), custom_call_target="tpu_custom_call" | custom-call | tf_op jit(solution)/shard_map/pallas_call | solution.py:1105
  331.5 0.0 copy-start.1
  331.6 0.8 slice.21
  332.4 0.1 constant_dynamic-slice_fusion
  332.5 0.5 slice_bitcast_fusion
  333.0 1.3 fusion.8
  335.6 0.0 copy-start
  335.6 2.5 copy.44
  338.1 0.0 copy-done.1
  338.1 1.0 copy.45
  339.1 0.0 copy-done
  339.1 0.0 copy-start.6
  339.1 0.0 copy-start.4
  339.1 0.0 copy-start.5
  339.1 1.3 copy.46
  340.4 0.0 copy-done.9
  340.4 0.7 copy.47
  341.1 0.0 copy-done.8
  341.1 0.7 copy.48
  341.7 0.0 copy-done.7
  341.7 0.7 copy.49
  342.4 0.0 copy-done.6
  342.4 0.7 copy.50
  343.1 0.0 copy-done.4
  343.1 0.7 copy.51
  343.8 0.0 copy-done.5
  343.8 0.7 copy.52
  344.5 0.0 copy-done.3
  344.5 0.8 copy.53
  345.3 0.0 copy-done.2
  345.3 0.8 copy.54
  (5 shorter events, 0.0 us)
Async XLA Ops:
  331.5 6.5 %copy-start.1 = (f32[1,256,1024]{2,1,0:T(8,128)S(1)}, f32[1,256,1024]{2,1,0:T(8,128)}, u32[]{:S(2)}) copy-start(f32[1,256,1024]{2,1,0:T(8,128)} %get-tuple-element.63) | copy-start | bytes 3145732
  335.6 3.4 copy-start
  339.1 1.4 copy-start.9
  339.1 2.0 copy-start.8
  339.1 2.7 copy-start.7
  339.1 3.3 copy-start.6
  339.1 4.0 %copy-start.4 = (f32[32,3072]{1,0:T(8,128)S(1)}, f32[32,3072]{1,0:T(8,128)}, u32[]{:S(2)}) copy-start(f32[32,3072]{1,0:T(8,128)} %get-tuple-element.72) | copy-start | bytes 1179652
  339.1 4.7 %copy-start.5 = (f32[32,1024]{1,0:T(8,128)S(1)}, f32[32,1024]{1,0:T(8,128)}, u32[]{:S(2)}) copy-start(f32[32,1024]{1,0:T(8,128)} %get-tuple-element.73) | copy-start | bytes 393220
  340.4 4.0 %copy-start.3 = (f32[32,4096]{1,0:T(8,128)S(1)}, f32[32,4096]{1,0:T(8,128)}, u32[]{:S(2)}) copy-start(f32[32,4096]{1,0:T(8,128)} %get-tuple-element.75) | copy-start | bytes 1572868
  340.4 4.8 %copy-start.2 = (f32[128,1024]{1,0:T(8,128)S(1)}, f32[128,1024]{1,0:T(8,128)}, u32[]{:S(2)}) copy-start(f32[128,1024]{1,0:T(8,128)} %get-tuple-element.76) | copy-start | bytes 1572868

commit v3 on v2

--- a/solution.py
+++ b/solution.py
@@ -12,7 +12,7 @@
 UNIT_COLS = 1024
 UNIT_ROWS = 32
 RING = 4
-PARTIALS = 5
+PARTIALS = 8
 WIDTHS = ((256, 256, 256, 256), (128, 128, 384, 384), (128, 128, 384, 384), (128, 128, 384, 384))
 
 
@@ -148,12 +148,7 @@
         return remote(b, b, self.sib_s.at[u], self.sib_r.at[u], me.dev(c=1 - me.c))
 
     def stage(self, s, u):
-        if s == 0:
-            self.own(u).start()
-        elif s == 1:
-            self.own(u).wait()
-            self.xcopy(u, 2).start()
-            self.ycopy(u, 3).start()
+        if s == 1:
             self.z_a(u, 0)
             self.z_a(u, 1)
         elif s == 2:
@@ -188,6 +183,11 @@
         elif s == 6:
             self.final(u, False).wait_recv()
 
+    def early(self, u):
+        self.own(u).wait()
+        self.xcopy(u, 2).start()
+        self.ycopy(u, 3).start()
+
     def sent(self, u):
         for p in range(4):
             self.z_sent(u, p)
@@ -222,7 +222,7 @@
 
     def first(self, u, p):
         me, s = self.me, slice(None)
-        dst = self.r1.at[u % RING, :, :, :, part_cols(u, p, 0)]
+        dst = self.r1.at[u % PARTIALS, :, :, :, part_cols(u, p, 0)]
         if p in (0, 2):
             return remote(self.pt(u, p, 1 - me.y, s, s), dst, self.s1.at[u, p], self.q1.at[u, p], me.dev(y=1 - me.y))
         return remote(self.pt(u, p, s, 1 - me.x, s), dst, self.s1.at[u, p], self.q1.at[u, p], me.dev(x=1 - me.x))
@@ -247,7 +247,7 @@
             dst = lambda i: self.pt(u, p, me.y, i // 4, i % 4)
         else:
             dst = lambda i: self.pt(u, p, i // 4, me.x, i % 4)
-        self.add(8, dst, [lambda i: self.r1.at[u % RING, i // 4, i % 4, :, part_cols(u, p, 0)]])
+        self.add(8, dst, [lambda i: self.r1.at[u % PARTIALS, i // 4, i % 4, :, part_cols(u, p, 0)]])
 
     def second(self, u, p):
         me, s = self.me, slice(None)
@@ -483,8 +483,10 @@
     for_each(incoming.shape[0] // 32, body)
 
 
-def attend_forward_heads(q, q0, k, k0, v, v0, out, count):
-    def body(h):
+def attend_forward_heads(first, heads, q, q0, k, k0, v, v0, out, count):
+    def body(i):
+        h = first + i
+
         def head(ref, at):
             return ref[:, pl.ds(pl.multiple_of(at + h * 128, 128), 128)]
 
@@ -495,13 +497,15 @@
         p = (e * (1.0 / jnp.sum(e, axis=-1, keepdims=True))).astype(BF16)
         out[:, block(h, 128)] = matmul(p, head(v, v0)).astype(BF16)
 
-    for_each(HEADS, body)
-
-
-def attend_backward_heads(q, q0, k, k0, v, v0, mixed_grad, count, dq, dq0, dk, dk0, dv, dv0):
+    for_each(heads, body)
+
+
+def attend_backward_heads(first, heads, q, q0, k, k0, v, v0, mixed_grad, count, dq, dq0, dk, dk0, dv, dv0):
     scale = 128 ** (-0.5)
 
-    def body(h):
+    def body(i):
+        h = first + i
+
         def head(ref, at):
             return ref[:, pl.ds(pl.multiple_of(at + h * 128, 128), 128)]
 
@@ -517,7 +521,7 @@
         dk[:, pl.ds(pl.multiple_of(dk0 + h * 128, 128), 128)] = (matmul(ds, qh) * scale).astype(BF16)
         dq[:, pl.ds(pl.multiple_of(dq0 + h * 128, 128), 128)] = (matmul(kh.T, ds).T * scale).astype(BF16)
 
-    for_each(HEADS, body)
+    for_each(heads, body)
 
 
 class SmallGather:
@@ -643,22 +647,57 @@
     pushed = [0]
     tick = [0]
 
-    def gather_to(t):
-        while tick[0] <= min(t, gather.ticks(1) - 1):
-            gather.tick(tick[0], 1)
-            tick[0] += 1
-
-    def arrived(u):
-        gather_to(u + Gather.STAGES - 1)
-
-    def settle(last):
+    clock = [0.0]
+    settled = [-1]
+    ready = []
+
+    def tick_ready(t):
+        return 13 + 3.7 * min(t, 6) + 7.35 * max(0, t - 6)
+
+    def settle_ready(k):
+        return ready[k] if k < len(ready) else ready[-1] + 4.0 * (k - len(ready) + 1)
+
+    def next_tick():
+        clock[0] = max(clock[0], tick_ready(tick[0])) + 0.5
+        gather.tick(tick[0], 1)
+        tick[0] += 1
+
+    def next_settle():
+        settled[0] += 1
+        last = settled[0]
+        clock[0] = max(clock[0], settle_ready(last)) + 1.0
         for s in range(Scatter.STAGES - 1, 0, -1):
             if 0 <= last - s < len(scatter_units):
                 scatter.stage(s, last - s)
 
+    def spend(us):
+        clock[0] += us
+        while True:
+            k = settled[0] + 1
+            if tick[0] < gather.ticks(1) and tick_ready(tick[0]) <= clock[0]:
+                next_tick()
+            elif pushed[0] and k <= pushed[0] and k < len(scatter_units) + 4 and settle_ready(k) <= clock[0]:
+                next_settle()
+            else:
+                break
+
+    def arrived(u):
+        while tick[0] < gather.ticks(1) and tick[0] <= u + Gather.STAGES - 1:
+            next_tick()
+
+    def gather_to(t):
+        while tick[0] <= t:
+            next_tick()
+
+    def settle_to(last):
+        while settled[0] < last:
+            next_settle()
+
     def load(k, src, dst):
         return pltpu.make_async_copy(src, dst, in_sem.at[k])
 
+    for u in range(len(gather.units)):
+        gather.own(u).start()
     loads = [load(0, latents.at[0], after_self), load(1, pixels.at[0], pix), load(2, cotangent.at[0], resid)]
     for c in loads:
         c.start()
@@ -667,12 +706,15 @@
     own_gain.wait()
     gains = SmallGather(me, gain_full, sg_s, sg_r)
     gains.run(0)
-    gather_to(0)
+    gather.early(0)
+    gather_to(1)
+    for u in range(1, len(gather.units)):
+        gather.early(u)
     gains.run(1)
-    gather_to(1)
+    gather_to(2)
     gains.run(2)
+    gather_to(3)
     gains.run(3)
-    gather_to(2)
     gains.run(4)
     table = jnp.sum(gain_full[...].reshape(32, 8, 128), axis=1).astype(BF16)
     width = latents.shape[2]
@@ -778,6 +820,7 @@
 
     def weight_grad(xt_at, rows, own, far, col0):
         u = pushed[0]
+        settle_to(u - 3)
         if u >= PARTIALS:
             scatter.sent(u - PARTIALS)
         slot = u % PARTIALS
@@ -790,6 +833,10 @@
         for_each(4, body)
         scatter.stage(0, u)
         pushed[0] += 1
+        clock[0] += 1.7 if rows > 256 else 1.2
+        gap = 7.35 if tick[0] >= gather.ticks(1) else 14.7
+        ready.append(max(clock[0] + 9, (ready[-1] if ready else 0) + gap))
+        spend(0)
 
     def xt_of(xt, rows):
         return lambda at: xt[:, :, :, :, pl.ds(at, rows)].reshape(512, rows)
@@ -798,22 +845,27 @@
     loads[1].wait()
     ln_forward(after_self, gain[0], tmp)
     transpose_out(0, tmp, 0, xt_normed, 256)
-    gather_to(3)
+    spend(2)
     ln_forward(pix, gain[1], big)
     transpose_out(1, big, 0, xt_pix, 512)
-    gather_to(4)
+    spend(3.3)
     transpose_out(2, big, 256, xt_pix, 512)
     count = counts[0]
-    arrived(0)
-    project(big, w_fetch(fulls[1], 0), store(keys))
-    arrived(1)
-    project(big, w_fetch(fulls[2], 0), store(values))
     loads[2].wait()
     for_each(8, lambda i: g_out.__setitem__((block(i, 32), slice(None)), resid[block(i, 32), :].astype(BF16)))
     swap(0, g_out, g_out_in).start()
+    arrived(0)
+    project(big, w_fetch(fulls[1], 0), store(keys))
+    spend(3.3)
+    arrived(1)
+    project(big, w_fetch(fulls[2], 0), store(values))
+    spend(3.3)
     arrived(2)
     project(tmp, w_fetch(fulls[0], 0), store(queries))
-    attend_forward_heads(queries, 0, keys, 0, values, 0, tmp, count)
+    spend(2.7)
+    for half in range(2):
+        attend_forward_heads(4 * half, 4, queries, 0, keys, 0, values, 0, tmp, count)
+        spend(2.3)
     arrived(3)
     transpose_out(3, tmp, 0, xt_mixed, 256)
 
@@ -824,19 +876,26 @@
         return put
 
     project(tmp, w_fetch(fulls[3], 0), add_to(after_cross, after_self))
+    spend(3)
 
     ln_forward(after_cross, gain[2], tmp)
     transpose_out(4, tmp, 0, xt_nself, 256)
+    spend(1.8)
     for k in range(3):
         arrived(4 + k)
         project(tmp, w_fetch(fulls[4], k * UNIT_COLS), store(packed, k * UNIT_COLS))
-    attend_forward_heads(packed, 0, packed, UNIT_COLS, packed, 2 * UNIT_COLS, tmp, None)
+        spend(2.7)
+    for half in range(2):
+        attend_forward_heads(4 * half, 4, packed, 0, packed, UNIT_COLS, packed, 2 * UNIT_COLS, tmp, None)
+        spend(2.2)
     arrived(7)
     transpose_out(5, tmp, 0, xt_smixed, 256)
     project(tmp, w_fetch(fulls[5], 0), add_to(after_self, after_cross))
+    spend(3)
 
     ln_forward(after_self, gain[3], tmp)
     transpose_out(6, tmp, 0, xt_nmlp, 256)
+    spend(1.8)
     a_staged = [None, None]
 
     def act_out(k):
@@ -878,35 +937,46 @@
 
         for_each(4, up)
         act_copies.append(act_out(k))
+        spend(3.2)
     for k in range(2, 4):
         a_staged[k % 2][0].wait()
         a_staged[k % 2][1].wait_send()
     for k in range(4):
         act_copies[k][1].wait_recv()
-
     for slot in range(2):
         clear(slot)
+    spend(2)
 
     swap(0, g_out, g_out_in).wait_recv()
-    for k in range(4):
-        def xt_down(at, k=k):
+
+    def down_grad(k):
+        def xt_down(at):
             return xt_act[:, :, :, pl.ds(k * UNIT_ROWS, UNIT_ROWS), pl.ds(at, 256)].reshape(512, 256)
 
         weight_grad(xt_down, 256, g_out, g_out_in, 0)
-        arrived(12 + k)
-        settle(k)
+
+    down_grad(0)
+    arrived(13)
+    down_grad(1)
+    arrived(15)
+
+    wd_turn = [0]
 
     def wd_start(q):
-        c = pltpu.make_async_copy(fulls[7].at[q // 2, q % 2], wd_buf.at[q % 2], wd_sem.at[q % 2])
+        slot = wd_turn[0] % 2
+        wd_turn[0] += 1
+        c = pltpu.make_async_copy(fulls[7].at[q // 2, q % 2], wd_buf.at[slot], wd_sem.at[slot])
         c.start()
-        return c
-
+        return slot, c
+
+    pending = w_start(fulls[6], 0)
     wd = [wd_start(0), wd_start(1), None, None]
     for q in range(4):
-        wd[q].wait()
+        slot, c = wd[q]
+        c.wait()
 
         def hidden_back(j):
-            w = wd_buf[q % 2, j].reshape(256, width)
+            w = wd_buf[slot, j].reshape(256, width)
             tile = matmul_nt(g_out[...], w)
             cols = pl.ds(pl.multiple_of(q * UNIT_COLS + j * 256, 256), 256)
             hid[:, cols] = (hid[:, cols].astype(F32) * tile).astype(BF16)
@@ -914,136 +984,153 @@
         for_each(4, hidden_back)
         cols = pl.ds(q * UNIT_COLS, UNIT_COLS)
         swap(1 + q, hid.at[:, cols], hid_in.at[:, cols]).start()
-
-        def down(j):
-            w = wd_buf[q % 2, :, :, :, block(j, 256)].reshape(UNIT_COLS, 256)
-            tile = matmul(act[:, pl.ds(q * UNIT_COLS, UNIT_COLS)], w)
-            dst = block(j, 256)
-            acc[0, :, dst] = (after_self[:, dst] if q == 0 else acc[0, :, dst]) + tile
-
-        for_each(4, down)
+        spend(1.5)
         if q < 2:
             wd[q + 2] = wd_start(q + 2)
+            down_grad(2 + q)
     xt_wait(6, xt_nmlp, 0, 256)
-    pending = [w_start(fulls[6], 0), None]
-    out_copy = pltpu.make_async_copy(acc.at[0], latents_out.at[0], out_sem.at[0])
-    out_copy.start()
-    small[...] = jnp.zeros_like(small)
-    squares = jnp.zeros((8, width), F32)
-
-    def square(i, total):
-        v = acc[0, block(i, 8), :]
-        return total + v * v
-
-    squares = lax.fori_loop(0, 32, square, squares)
-    mean_square = jnp.sum(jnp.sum(squares, axis=1, keepdims=True), axis=0, keepdims=True) / (latents.shape[1] * width)
-    root_mean = jnp.sqrt(mean_square)
-    small[5:6, :] = jnp.broadcast_to(root_mean, (1, width))
+    wd = [wd_start(0), wd_start(1), None, None]
     for k in range(4):
+        slot, c = pending
+        c.wait()
+        if k < 3:
+            pending = w_start(fulls[6], (k + 1) * UNIT_COLS)
+        back(hid, k * UNIT_COLS, slot, acc.at[1], k == 0)
+        spend(1.4)
         cols = pl.ds(k * UNIT_COLS, UNIT_COLS)
         swap(1 + k, hid.at[:, cols], hid_in.at[:, cols]).wait_recv()
         weight_grad(xt_of(xt_nmlp, 256), 256, hid, hid_in, k * UNIT_COLS)
-        slot, c = pending[k % 2]
-        c.wait()
-        if k < 3:
-            pending[(k + 1) % 2] = w_start(fulls[6], (k + 1) * UNIT_COLS)
-        back(hid, k * UNIT_COLS, slot, acc.at[1], k == 0)
-        settle(4 + k)
+    so_slot, c_so = w_start(fulls[5], 0)
     ln_backward(after_self, 0, gain[3], acc.at[1], resid, gain_acc.at[3])
+    spend(2.3)
 
     def round_rows(dst):
         for_each(8, lambda i: dst.__setitem__((block(i, 32), slice(None)), resid[block(i, 32), :].astype(BF16)))
 
-    so_slot, c_so = w_start(fulls[5], 0)
     round_rows(g_branch)
     swap(5, g_branch, g_branch_in).start()
     c_so.wait()
+    qkv_w = w_start(fulls[4], 0)
     back(g_branch, 0, so_slot, tmp, True)
+    spend(1.8)
     swap(5, g_branch, g_branch_in).wait_recv()
     xt_wait(5, xt_smixed, 0, 256)
     weight_grad(xt_of(xt_smixed, 256), 256, g_branch, g_branch_in, 0)
-    settle(8)
-    qkv_w = w_start(fulls[4], 0)
-    attend_backward_heads(
-        packed, 0, packed, UNIT_COLS, packed, 2 * UNIT_COLS, tmp, None, act, 0, act, UNIT_COLS, act, 2 * UNIT_COLS
-    )
-    packed_grad = act.at[:, pl.ds(0, 3 * UNIT_COLS)]
+    for q in range(4):
+        cols = pl.ds(q * UNIT_COLS, UNIT_COLS)
+        swap(1 + q, hid.at[:, cols], hid_in.at[:, cols]).wait_send()
+    for half in range(2):
+        attend_backward_heads(
+            4 * half, 4, packed, 0, packed, UNIT_COLS, packed, 2 * UNIT_COLS, tmp, None,
+            hid, 0, hid, UNIT_COLS, hid, 2 * UNIT_COLS,
+        )
+        spend(3.4)
+    packed_grad = hid.at[:, pl.ds(0, 3 * UNIT_COLS)]
     swap(6, packed_grad, packed_in).start()
-    swap(6, packed_grad, packed_in).wait_recv()
-    xt_wait(4, xt_nself, 0, 256)
-    out_copy.wait()
     for k in range(3):
-        weight_grad(xt_of(xt_nself, 256), 256, act, packed_in, k * UNIT_COLS)
         slot, c = qkv_w
         c.wait()
         if k < 2:
             qkv_w = w_start(fulls[4], (k + 1) * UNIT_COLS)
-        back(act, k * UNIT_COLS, slot, acc.at[0], k == 0)
-        settle(9 + k)
+        back(hid, k * UNIT_COLS, slot, acc.at[0], k == 0)
+        spend(1.3)
+        if k == 0:
+            swap(6, packed_grad, packed_in).wait_recv()
+            xt_wait(4, xt_nself, 0, 256)
+        weight_grad(xt_of(xt_nself, 256), 256, hid, packed_in, k * UNIT_COLS)
     wo_slot, c_wo = w_start(fulls[3], 0)
     ln_backward(after_cross, 0, gain[2], acc.at[0], resid, gain_acc.at[2])
-    again = load(0, latents.at[0], after_self)
-    again.start()
+    spend(2.3)
 
     round_rows(g_cross)
     swap(7, g_cross, g_cross_in).start()
     c_wo.wait()
     back(g_cross, 0, wo_slot, tmp, True)
+    spend(1.8)
     swap(7, g_cross, g_cross_in).wait_recv()
     xt_wait(3, xt_mixed, 0, 256)
     weight_grad(xt_of(xt_mixed, 256), 256, g_cross, g_cross_in, 0)
-    settle(12)
-    attend_backward_heads(queries, 0, keys, 0, values, 0, tmp, count, dq, 0, big, 0, dv, 0)
+
+    for q in range(4):
+        slot, c = wd[q]
+        c.wait()
+
+        def down(j):
+            w = wd_buf[slot, :, :, :, block(j, 256)].reshape(UNIT_COLS, 256)
+            tile = matmul(act[:, pl.ds(q * UNIT_COLS, UNIT_COLS)], w)
+            dst = block(j, 256)
+            acc[0, :, dst] = (after_self[:, dst] if q == 0 else acc[0, :, dst]) + tile
+
+        for_each(4, down)
+        if q < 2:
+            wd[q + 2] = wd_start(q + 2)
+        spend(1.3)
+    again = load(0, latents.at[0], after_self)
+    again.start()
+    out_copy = pltpu.make_async_copy(acc.at[0], latents_out.at[0], out_sem.at[0])
+    out_copy.start()
+    small[...] = jnp.zeros_like(small)
+
+    def square(i, total):
+        v = acc[0, block(i, 8), :]
+        return total + v * v
+
+    squares = lax.fori_loop(0, 32, square, jnp.zeros((8, width), F32))
+    mean_square = jnp.sum(jnp.sum(squares, axis=1, keepdims=True), axis=0, keepdims=True) / (latents.shape[1] * width)
+    root_mean = jnp.sqrt(mean_square)
+    small[4:5, :] = jnp.broadcast_to(root_mean, (1, width))
+    spend(1)
+
+    for half in range(2):
+        attend_backward_heads(4 * half, 4, queries, 0, keys, 0, values, 0, tmp, count, dq, 0, big, 0, dv, 0)
+        spend(3.2)
     given = [swap(8, dv, dv_in), swap(9, big, dk_in), swap(10, dq, dq_in)]
     for c in given:
         c.start()
-    w_q = w_start(fulls[0], 0)
+    w_v = w_start(fulls[2], 0)
+    w_k = w_start(fulls[1], 0)
     xt_wait(1, xt_pix, 0, 512)
     xt_wait(2, xt_pix, 256, 512)
     given[0].wait_recv()
     weight_grad(xt_of(xt_pix, 512), 512, dv, dv_in, 0)
-    settle(13)
     given[1].wait_recv()
     weight_grad(xt_of(xt_pix, 512), 512, big, dk_in, 0)
-    settle(14)
     xt_wait(0, xt_normed, 0, 256)
     given[2].wait_recv()
     weight_grad(xt_of(xt_normed, 256), 256, dq, dq_in, 0)
-    settle(15)
-    w_q[1].wait()
-    w_k = w_start(fulls[1], 0)
-    back(dq, 0, w_q[0], acc.at[0], True)
-    again.wait()
-    ln_backward(after_self, 0, gain[0], acc.at[0], resid, gain_acc.at[0])
-    grad_copy = pltpu.make_async_copy(resid, latents_grad.at[0], out_sem.at[1])
-    grad_copy.start()
-    settle(16)
-    w_v = w_start(fulls[2], 0)
+    out_copy.wait()
+    w_v[1].wait()
+    for r in range(2):
+        back(dv.at[pl.ds(256 * r, 256)], 0, w_v[0], acc.at[r], True)
+        spend(1.3)
+    w_q = w_start(fulls[0], 0)
     w_k[1].wait()
-    for r in range(2):
-        back(big.at[pl.ds(256 * r, 256)], 0, w_k[0], acc.at[r], True)
-    settle(17)
-    w_v[1].wait()
     pix_copies = []
     for r in range(2):
-        back(dv.at[pl.ds(256 * r, 256)], 0, w_v[0], acc.at[r], False)
+        back(big.at[pl.ds(256 * r, 256)], 0, w_k[0], acc.at[r], False)
+        spend(1.3)
         ln_backward(pix, 256 * r, gain[1], acc.at[r], None, gain_acc.at[1])
         c = pltpu.make_async_copy(acc.at[r], pixels_grad.at[0, pl.ds(256 * r, 256)], out_sem.at[2 + r])
         c.start()
         pix_copies.append(c)
+        spend(2.3)
+    w_q[1].wait()
+    back(dq, 0, w_q[0], after_cross, True)
+    spend(1.3)
+    again.wait()
+    ln_backward(after_self, 0, gain[0], after_cross, resid, gain_acc.at[0])
+    grad_copy = pltpu.make_async_copy(resid, latents_grad.at[0], out_sem.at[1])
+    grad_copy.start()
+    spend(2.3)
     for g in range(4):
         small[g : g + 1, :] = jnp.sum(gain_acc[g], axis=0, keepdims=True)
-    small[4:5, :] = small[5:6, :]
     total = SmallSum(me, small, small_got, ss_s, ss_r)
-    total.start(0)
-    settle(18)
-    total.finish(0)
-    total.start(1)
-    settle(19)
-    for k in range(1, 5):
+    for k in range(5):
+        total.start(k)
+        if settled[0] < len(scatter_units) + 3:
+            next_settle()
         total.finish(k)
-        if k < 4:
-            total.start(k + 1)
+    settle_to(len(scatter_units) + 3)
     small[5:6, :] = jnp.broadcast_to(root_mean, (1, width))
     small_out[...] = small[...]
 
@@ -1052,9 +1139,6 @@
     for u in range(len(scatter_units) - PARTIALS, len(scatter_units)):
         scatter.sent(u)
     swap(0, g_out, g_out_in).wait_send()
-    for q in range(4):
-        cols = pl.ds(q * UNIT_COLS, UNIT_COLS)
-        swap(1 + q, hid.at[:, cols], hid_in.at[:, cols]).wait_send()
     swap(5, g_branch, g_branch_in).wait_send()
     swap(6, packed_grad, packed_in).wait_send()
     swap(7, g_cross, g_cross_in).wait_send()
@@ -1075,7 +1159,7 @@
         vm((2, 2, 2, 4, 2, UNIT_ROWS, UNIT_COLS), BF16),
         vm((2, 4, 2, 128, UNIT_COLS), BF16),
         vm((PARTIALS, 2, 2, 4, UNIT_ROWS, UNIT_COLS), BF16),
-        vm((RING, 2, 4, UNIT_ROWS, UNIT_COLS), BF16),
+        vm((PARTIALS, 2, 4, UNIT_ROWS, UNIT_COLS), BF16),
         vm((RING, 4, UNIT_ROWS, UNIT_COLS), BF16),
         vm((RING, 4, 2, UNIT_ROWS, UNIT_COLS), BF16),
         xt(2 * rows), xt(2 * slots), xt(2 * rows), xt(2 * rows), xt(2 * rows), xt(2 * rows),
@@ -1105,7 +1189,7 @@
     results = pl.pallas_call(
         mega_kernel,
         out_shape=outs,
-        in_specs=[hbm, hbm, smem, hbm, hbm] + [hbm] * 8,
+        in_specs=[hbm, hbm, smem, hbm, hbm] + [vmem] * 8,
         out_specs=[hbm] * 3 + [vmem] + [vmem] * 8 + [hbm] * 8,
         scratch_shapes=scratch + sems,
         compiler_params=pltpu.CompilerParams(collective_id=0, has_side_effects=True, vmem_limit_bytes=63 * 2**20),
@@ -1385,6 +1469,7 @@
     gain_block = jnp.pad(gains[None, :], ((0, 7), (0, 0)))
     shards = (w_query, w_key, w_value, w_out, w_qkv, w_self_out, w_up, w_down)
     (latents_out, latents_grad, pixels_grad, small), grads = mega(latents, pixels, counts, cotangent, gain_block, shards)
+    latents_out, latents_grad, pixels_grad, *grads = hand_out([latents_out, latents_grad, pixels_grad] + list(grads))
     rows = gain_q.shape[0]
     devices = lax.axis_size(("dp", "fsdp"))
     mine = lax.dynamic_slice(small[:4], (0, lax.axis_index(("dp", "fsdp")) * rows), (4, rows))
@@ -1410,6 +1495,31 @@
     )
 
 
+def hand_out(arrays):
+    n = len(arrays)
+
+    def kernel(*refs):
+        sems = refs[3 * n]
+        fetch = [pltpu.make_async_copy(refs[k], refs[2 * n + k], sems.at[0, k]) for k in range(n)]
+        put = [pltpu.make_async_copy(refs[2 * n + k], refs[n + k], sems.at[1, k]) for k in range(n)]
+        for c in fetch:
+            c.start()
+        for k in range(n):
+            fetch[k].wait()
+            put[k].start()
+        for c in put:
+            c.wait()
+
+    return pl.pallas_call(
+        kernel,
+        out_shape=[jax.ShapeDtypeStruct(a.shape, a.dtype) for a in arrays],
+        in_specs=[pl.BlockSpec(memory_space=pl.ANY)] * n,
+        out_specs=[pl.BlockSpec(memory_space=pl.ANY)] * n,
+        scratch_shapes=[pltpu.VMEM(a.shape, a.dtype) for a in arrays] + [DMA((2, n))],
+        compiler_params=pltpu.CompilerParams(vmem_limit_bytes=63 * 2**20),
+    )(*arrays)
+
+
 def fits(mesh):
     return mesh.shape["dp"] == 4 and mesh.shape["fsdp"] == 8
 

time: 348 us -> 331 us (0.951)
  local copies, waits for them, and re-layouts: 13.1 us -> 1.14 us
  Pallas kernels: 329 us -> 324 us
    pallas_call x1, Pallas kernels: 329 us -> 318 us  [mega(): pl.pallas_call(mega_kernel, out_shape=outs, in_specs=[hbm, hbm, smem, hbm...]
    unnamed x31 -> x2, local copies, waits for them, and re-layouts: 10.4 us -> 0.01 us
    pallas_call x0 -> x1, Pallas kernels: none -> 5.35 us  [hand_out(): pl.pallas_call(kernel, out_shape=[jax.ShapeDtypeStruct(a.shape, a.dtype)...]
where the time goes in v3:
time: 331 us; the launch traced here: 330 us
  Pallas kernels  324 us (98%)
  between operations  3.78 us (1%)
    pallas_call x1, Pallas kernels, mega(): pl.pallas_call(mega_kernel, out_shape=outs, in_specs=[hbm, hbm, smem, hbm...  318 us

profile of v3, /device:TPU:0, one launch (start us, length us, event | category | flops | bytes accessed | tf_op | source)
XLA Modules:
  0.0 329.9 jit_solution(2877228432345470207)
XLA Ops:
  0.6 1.4 fusion.7.refs_4_
  2.7 318.3 %shard_map.279 = (f32[1,256,1024]{2,1,0:T(8,128)}, f32[1,256,1024]{2,1,0:T(8,128)}, f32[1,512,1024]{2,1,0:T(8,128)}, f32[8,1024]{1,0:T(8,128)}, f32[32,1024]{1,0...) custom-call(f32[1,256,1024]{2,1,0:T(8,128)} %refs_0_.1, ...), custom_call_target="tpu_custom_call" | custom-call | tf_op jit(solution)/shard_map/pallas_call | solution.py:1189
  321.0 0.0 copy-start
  321.0 5.3 %shard_map.280 = (f32[1,256,1024]{2,1,0:T(8,128)}, f32[1,256,1024]{2,1,0:T(8,128)}, f32[1,512,1024]{2,1,0:T(8,128)}, f32[32,1024]{1,0:T(8,128)}, f32[32,1024]{1,...) custom-call(f32[1,256,1024]{2,1,0:T(8,128)} %get-tuple-element.39.re, ...), custom_call_target="tpu_custom_call" | custom-call | tf_op jit(solution)/shard_map/pallas_call | solution.py:1513
  326.3 0.0 copy-done
  326.3 0.1 constant_dynamic-slice_fusion
  326.4 0.5 slice_bitcast_fusion
  327.0 0.5 fusion.8
  (1 shorter events, 0.0 us)
Async XLA Ops:
  321.0 5.4 %copy-start = (f32[8,1024]{1,0:T(8,128)S(1)}, f32[8,1024]{1,0:T(8,128)}, u32[]{:S(2)}) copy-start(f32[8,1024]{1,0:T(8,128)} %get-tuple-element.53) | copy-start | bytes 98308

commit v4 on v3

--- a/solution.py
+++ b/solution.py
@@ -13,7 +13,9 @@
 UNIT_ROWS = 32
 RING = 4
 PARTIALS = 8
-WIDTHS = ((256, 256, 256, 256), (128, 128, 384, 384), (128, 128, 384, 384), (128, 128, 384, 384))
+SCATTER_WIDTHS = ((256, 256, 256, 256),) * RING
+GATHER_WIDTHS = ((256, 256, 256, 256),)
+WHOLE = (0, 0, UNIT_COLS, 0)
 
 
 class Place:
@@ -54,9 +56,13 @@
     )
 
 
-def part_cols(u, p, base):
-    widths = WIDTHS[u % RING]
+def columns(widths, p, base):
     return pl.ds(base + sum(widths[:p]), widths[p])
+
+
+class Unit:
+    def __init__(self, kind, shard, full, row=0, col=0, rows=UNIT_ROWS):
+        self.kind, self.shard, self.full, self.row, self.col, self.rows = kind, shard, full, row, col, rows
 
 
 class Gather:
@@ -65,19 +71,37 @@
     def __init__(self, me, units, sems):
         self.me, self.units = me, units
         self.loc, self.sib_s, self.sib_r, self.zs, self.zr, self.xs, self.xr, self.ys, self.yr = sems
+        self.widths, plain = [], 0
+        for unit in units:
+            self.widths.append(GATHER_WIDTHS[plain % len(GATHER_WIDTHS)] if unit.kind == "all" else WHOLE)
+            plain += unit.kind == "all"
 
     @staticmethod
     def sems(n):
         return [DMA((n,))] * 3 + [DMA((n, 4, 4))] * 2 + [DMA((n, 4))] * 4
 
     def at(self, u, y, x, z, c, p=None):
-        _, full, row, col = self.units[u]
-        cols = pl.ds(col, UNIT_COLS) if p is None else part_cols(u, p, col)
-        return full.at[y, x, z, c, pl.ds(row, UNIT_ROWS), cols]
+        unit = self.units[u]
+        cols = pl.ds(unit.col, UNIT_COLS) if p is None else columns(self.widths[u], p, unit.col)
+        rows = pl.ds(unit.row, unit.rows)
+        if unit.kind == "down":
+            return unit.full.at[y, z, c, rows, cols]
+        return unit.full.at[y, x, z, c, rows, cols]
+
+    def parts(self, u, *which):
+        return [p for p in which if self.widths[u][p]]
+
+    def half(self, u, x):
+        unit = self.units[u]
+        col = pl.multiple_of(2 * unit.col + x * UNIT_COLS, UNIT_COLS)
+        return unit.shard.at[pl.ds(unit.row, unit.rows), pl.ds(col, UNIT_COLS)]
 
     def own(self, u):
-        me, (shard, _, row, col) = self.me, self.units[u]
-        src = shard.at[pl.ds(row, UNIT_ROWS), pl.ds(col, UNIT_COLS)]
+        me, unit = self.me, self.units[u]
+        if unit.kind == "up":
+            src = self.half(u, me.x)
+        else:
+            src = unit.shard.at[pl.ds(unit.row, unit.rows), pl.ds(unit.col, UNIT_COLS)]
         return pltpu.make_async_copy(src, self.at(u, me.y, me.x, me.z, me.c), self.loc.at[u])
 
     def zblk(self, u, p, z):
@@ -135,6 +159,8 @@
     def xcopy(self, u, p, out=True):
         me, s = self.me, slice(None)
         b = self.at(u, me.y if p != 3 and p != 1 else s, me.x if out else 1 - me.x, me.z if p == 2 else s, me.c, p)
+        if self.units[u].kind == "up" and out:
+            return remote(self.half(u, 1 - me.x), b, self.xs.at[u, p], self.xr.at[u, p], me.dev(x=1 - me.x))
         return remote(b, b, self.xs.at[u, p], self.xr.at[u, p], me.dev(x=1 - me.x))
 
     def ycopy(self, u, p, out=True):
@@ -148,50 +174,48 @@
         return remote(b, b, self.sib_s.at[u], self.sib_r.at[u], me.dev(c=1 - me.c))
 
     def stage(self, s, u):
+        kind = self.units[u].kind
         if s == 1:
-            self.z_a(u, 0)
-            self.z_a(u, 1)
+            for p in self.parts(u, 0, 1):
+                self.z_a(u, p)
         elif s == 2:
-            self.z_b(u, 0)
-            self.z_b(u, 1)
-            self.xcopy(u, 2, False).wait_recv()
-            self.z_a(u, 2)
-            self.ycopy(u, 3, False).wait_recv()
-            self.z_a(u, 3)
+            for p in self.parts(u, 0, 1):
+                self.z_b(u, p)
+            for p in self.parts(u, 2, 3):
+                if kind != "down":
+                    (self.xcopy if p == 2 else self.ycopy)(u, p, False).wait_recv()
+                self.z_a(u, p)
         elif s == 3:
-            self.z_wait(u, 0)
-            self.xcopy(u, 0).start()
-            self.z_wait(u, 1)
-            self.ycopy(u, 1).start()
-            self.z_b(u, 2)
-            self.z_b(u, 3)
+            for p in self.parts(u, 0, 1):
+                self.z_wait(u, p)
+                (self.xcopy if p == 0 else self.ycopy)(u, p).start()
+            for p in self.parts(u, 2, 3):
+                self.z_b(u, p)
         elif s == 4:
-            self.z_wait(u, 2)
-            self.ycopy(u, 2).start()
-            self.z_wait(u, 3)
-            self.xcopy(u, 3).start()
-            self.xcopy(u, 0, False).wait_recv()
-            self.ycopy(u, 0).start()
-            self.ycopy(u, 1, False).wait_recv()
-            self.xcopy(u, 1).start()
+            for p in self.parts(u, 2, 3):
+                self.z_wait(u, p)
+                (self.ycopy if p == 2 else self.xcopy)(u, p).start()
+            for p in self.parts(u, 0, 1):
+                (self.xcopy if p == 0 else self.ycopy)(u, p, False).wait_recv()
+                (self.ycopy if p == 0 else self.xcopy)(u, p).start()
         elif s == 5:
-            self.ycopy(u, 2, False).wait_recv()
-            self.xcopy(u, 3, False).wait_recv()
-            self.ycopy(u, 0, False).wait_recv()
-            self.xcopy(u, 1, False).wait_recv()
+            for p in self.parts(u, 2, 3, 0, 1):
+                (self.ycopy if p in (0, 2) else self.xcopy)(u, p, False).wait_recv()
             self.final(u).start()
         elif s == 6:
             self.final(u, False).wait_recv()
 
     def early(self, u):
         self.own(u).wait()
-        self.xcopy(u, 2).start()
-        self.ycopy(u, 3).start()
+        for p in self.parts(u, 2, 3):
+            if self.units[u].kind != "down":
+                (self.xcopy if p == 2 else self.ycopy)(u, p).start()
 
     def sent(self, u):
-        for p in range(4):
+        for p in self.parts(u, 0, 1, 2, 3):
             self.z_sent(u, p)
-            self.xcopy(u, p).wait_send()
+            if self.units[u].kind != "down":
+                self.xcopy(u, p).wait_send()
             self.ycopy(u, p).wait_send()
         self.final(u).wait_send()
 
@@ -217,12 +241,27 @@
     def sems(n):
         return [DMA((n, 4))] * 4 + [DMA((n, 4, 4))] * 2
 
+    def kind(self, u):
+        return self.units[u][0]
+
+    def widths(self, u):
+        return SCATTER_WIDTHS[u % RING] if self.kind(u) == "all" else WHOLE
+
+    def cols(self, u, p):
+        return columns(self.widths(u), p, 0)
+
+    def parts(self, u, *which):
+        return [p for p in which if self.widths(u)[p]]
+
+    def slot2(self, u):
+        return u % RING if self.kind(u) == "all" else RING + u % 2
+
     def pt(self, u, p, y, x, z):
-        return self.part.at[u % PARTIALS, y, x, z, :, part_cols(u, p, 0)]
+        return self.part.at[u % PARTIALS, y, x, z, :, self.cols(u, p)]
 
     def first(self, u, p):
         me, s = self.me, slice(None)
-        dst = self.r1.at[u % PARTIALS, :, :, :, part_cols(u, p, 0)]
+        dst = self.r1.at[u % PARTIALS, :, :, :, self.cols(u, p)]
         if p in (0, 2):
             return remote(self.pt(u, p, 1 - me.y, s, s), dst, self.s1.at[u, p], self.q1.at[u, p], me.dev(y=1 - me.y))
         return remote(self.pt(u, p, s, 1 - me.x, s), dst, self.s1.at[u, p], self.q1.at[u, p], me.dev(x=1 - me.x))
@@ -247,13 +286,13 @@
             dst = lambda i: self.pt(u, p, me.y, i // 4, i % 4)
         else:
             dst = lambda i: self.pt(u, p, i // 4, me.x, i % 4)
-        self.add(8, dst, [lambda i: self.r1.at[u % PARTIALS, i // 4, i % 4, :, part_cols(u, p, 0)]])
+        self.add(8, dst, [lambda i: self.r1.at[u % PARTIALS, i // 4, i % 4, :, self.cols(u, p)]])
 
     def second(self, u, p):
         me, s = self.me, slice(None)
-        cols = part_cols(u, p, 0)
+        cols = self.cols(u, p)
         z = s if p < 2 else me.z
-        dst = self.r2.at[u % RING, :, :, cols] if p < 2 else self.r2.at[u % RING, 0, :, cols]
+        dst = self.r2.at[self.slot2(u), :, :, cols] if p < 2 else self.r2.at[self.slot2(u), 0, :, cols]
         if p in (0, 2):
             return remote(self.pt(u, p, me.y, 1 - me.x, z), dst, self.s2.at[u, p], self.q2.at[u, p], me.dev(x=1 - me.x))
         return remote(self.pt(u, p, 1 - me.y, me.x, z), dst, self.s2.at[u, p], self.q2.at[u, p], me.dev(y=1 - me.y))
@@ -264,7 +303,7 @@
         self.add(
             4,
             lambda i: self.pt(u, p, me.y, me.x, i),
-            [lambda i: self.r2.at[u % RING, i, :, part_cols(u, p, 0)]],
+            [lambda i: self.r2.at[self.slot2(u), i, :, self.cols(u, p)]],
         )
 
     def zblk(self, u, p, z):
@@ -272,7 +311,7 @@
         return self.pt(u, p, me.y if p != 3 else s, me.x if p != 2 else s, z)
 
     def zslot(self, u, p, slot):
-        cols = part_cols(u, p, 0)
+        cols = self.cols(u, p)
         return self.rz.at[u % RING, slot, 0, :, cols] if p < 2 else self.rz.at[u % RING, slot, :, :, cols]
 
     def zcopy(self, u, p, which, block, slot, z_to):
@@ -321,7 +360,7 @@
             self.z_gone(u, p).start()
 
     def z_add(self, u, p, block, slots):
-        cols = part_cols(u, p, 0)
+        cols = self.cols(u, p)
         me = self.me
         if p < 2:
             dst, count = (lambda i: self.pt(u, p, me.y, me.x, block)), 1
@@ -341,11 +380,11 @@
             self.zget(u, p, 2).wait_recv()
 
     def out(self, u, p):
-        out, row, col = self.units[u]
-        return out.at[pl.ds(row, UNIT_ROWS), part_cols(u, p, col)]
+        _, out, row, col = self.units[u]
+        return out.at[pl.ds(row, UNIT_ROWS), columns(self.widths(u), p, col)]
 
     def finish_z(self, u, p):
-        me, cols = self.me, part_cols(u, p, 0)
+        me, cols = self.me, self.cols(u, p)
         self.z_in(u, p)
         f32 = lambda ref: ref[...].astype(jnp.float32)
         total = f32(self.pt(u, p, me.y, me.x, me.z)) + f32(self.rz.at[u % RING, 0, 0, :, cols]) + f32(self.rz.at[u % RING, 1, 0, :, cols])
@@ -358,6 +397,28 @@
         def _():
             self.out(u, p)[...] = total + f32(self.rz.at[u % RING, 2, 0, :, cols])
 
+    def finish_down(self, u):
+        me = self.me
+        _, out, row, col = self.units[u]
+        self.z_in(u, 2)
+        f32 = lambda ref: ref[...].astype(jnp.float32)
+        for r in range(2):
+            dst = out.at[pl.ds(row + r * UNIT_ROWS, UNIT_ROWS), pl.ds(col, UNIT_COLS)]
+            dst[...] = f32(self.pt(u, 2, me.y, r, me.z)) + f32(self.rz.at[u % RING, 0, r]) + f32(self.rz.at[u % RING, 1, r])
+
+            @pl.when(~me.is_end)
+            def _():
+                dst[...] = dst[...] + f32(self.rz.at[u % RING, 2, r])
+
+    def finish_up(self, u):
+        me = self.me
+        _, out, row, col = self.units[u]
+        self.second(u, 2).wait_recv()
+        rows = pl.ds(row, UNIT_ROWS)
+        for x, ref in ((me.x, self.pt(u, 2, me.y, me.x, me.z)), (1 - me.x, self.r2.at[self.slot2(u), 0])):
+            cols = pl.ds(pl.multiple_of(2 * col + x * UNIT_COLS, UNIT_COLS), UNIT_COLS)
+            out[rows, cols] = ref[...].astype(jnp.float32)
+
     def pass_z(self, u, p):
         me = self.me
         self.z_in(u, p)
@@ -373,44 +434,52 @@
         self.second(u, p).start()
 
     def finish_last(self, u, p):
-        me, cols = self.me, part_cols(u, p, 0)
+        me, cols = self.me, self.cols(u, p)
         self.second(u, p).wait_recv()
-        total = self.pt(u, p, me.y, me.x, me.z)[...].astype(jnp.float32) + self.r2.at[u % RING, 0, :, cols][...].astype(jnp.float32)
+        total = self.pt(u, p, me.y, me.x, me.z)[...].astype(jnp.float32) + self.r2.at[self.slot2(u), 0, :, cols][...].astype(jnp.float32)
         self.out(u, p)[...] = total
 
     def stage(self, s, u):
+        kind = self.kind(u)
         if s == 0:
-            for p in (2, 3, 0, 1):
+            for p in self.parts(u, 2, 3, 0, 1):
                 self.first(u, p).start()
         elif s == 1:
-            for p in (2, 3):
+            for p in self.parts(u, 2, 3):
                 self.first_in(u, p)
                 self.z_a(u, p)
-            for p in (0, 1):
+            for p in self.parts(u, 0, 1):
                 self.first_in(u, p)
                 self.second(u, p).start()
         elif s == 2:
-            for p in (2, 3):
+            for p in self.parts(u, 2, 3):
                 self.z_b(u, p)
-            for p in (0, 1):
+            for p in self.parts(u, 0, 1):
                 self.second_in(u, p)
                 self.z_a(u, p)
         elif s == 3:
-            for p in (2, 3):
-                self.pass_z(u, p)
-            for p in (0, 1):
+            if kind == "down":
+                self.finish_down(u)
+            else:
+                for p in self.parts(u, 2, 3):
+                    self.pass_z(u, p)
+            for p in self.parts(u, 0, 1):
                 self.z_b(u, p)
         elif s == 4:
-            for p in (0, 1):
-                self.finish_z(u, p)
-            for p in (2, 3):
-                self.finish_last(u, p)
+            if kind == "up":
+                self.finish_up(u)
+            elif kind == "all":
+                for p in (0, 1):
+                    self.finish_z(u, p)
+                for p in (2, 3):
+                    self.finish_last(u, p)
 
     def sent(self, u):
         me = self.me
-        for p in range(4):
+        for p in self.parts(u, 0, 1, 2, 3):
             self.first(u, p).wait_send()
-            self.second(u, p).wait_send()
+            if self.kind(u) != "down":
+                self.second(u, p).wait_send()
 
             @pl.when(me.is_end)
             def _():
@@ -567,6 +636,7 @@
                 self.zc(me.z3, 4, 1 + me.z3, me.z1).wait_recv()
                 self.zc(me.z3, 4, 1 + me.z3, me.z1).start()
 
+        elif s == 3:
             for z in (me.z1, me.z2):
                 self.zc(z, 1, 1 + z, me.z1).wait_recv()
 
@@ -575,10 +645,10 @@
                 self.zc(me.z3, 1, 1 + me.z3, me.z1).wait_recv()
 
             self.xc().start()
-        elif s == 3:
+        elif s == 4:
             self.xc(False).wait_recv()
             self.yc().start()
-        elif s == 4:
+        elif s == 5:
             self.yc(False).wait_recv()
             self.sib().wait_send()
             self.zc(me.z, 1, 1 + me.z, me.z1).wait_send()
@@ -624,25 +694,28 @@
     (
         w_buf, wd_buf, part, r1, r2, rz,
         xt_normed, xt_pix, xt_mixed, xt_nself, xt_smixed, xt_nmlp, xt_act, st_a, st_b,
-        g_out, g_out_in, hid, hid_in, g_branch, g_branch_in, act, packed_in, g_cross, g_cross_in,
+        g_out, g_out_in, hid, hid_in, g_branch, g_branch_in, act, packed_in,
         dq, dq_in, big, dk_in, dv, dv_in,
         queries, keys, values, packed, after_cross, after_self, resid, pix, tmp, acc,
         gain_full, gain_vec, gain_acc, small, small_got,
-    ) = take(46)
+    ) = take(44)
     gather_sems, scatter_sems = take(9), take(6)
-    w_sem, wd_sem, in_sem, out_sem, sg_s, sg_r, ss_s, ss_r, xl, xs, xr, gs, gr = take(13)
+    w_sem, wd_sem, in_sem, out_sem, sg_s, sg_r, ss_s, ss_r, xl, xs, xr, gs, gr, across_s, across_r = take(15)
     me = Place()
-    me.barrier()
-
-    cross_units = [(shards[i], fulls[i], 0, 0) for i in (1, 2, 0, 3)]
-    self_units = [(shards[4], fulls[4], 0, k * UNIT_COLS) for k in range(3)] + [(shards[5], fulls[5], 0, 0)]
-    mlp_units = [(shards[6], fulls[6], 0, k * UNIT_COLS) for k in range(4)]
-    mlp_units += [(shards[7], fulls[7], k * UNIT_ROWS, 0) for k in range(4)]
-    gather = Gather(me, cross_units + self_units + mlp_units, gather_sems)
-    scatter_units = [(grads_out[7], k * UNIT_ROWS, 0) for k in range(4)]
-    scatter_units += [(grads_out[6], 0, k * UNIT_COLS) for k in range(4)]
-    scatter_units += [(grads_out[5], 0, 0)] + [(grads_out[4], 0, k * UNIT_COLS) for k in range(3)]
-    scatter_units += [(grads_out[i], 0, 0) for i in (3, 2, 1, 0)]
+
+    plain = lambda i, k: Unit("all", shards[i], fulls[i], 0, k * UNIT_COLS)
+    up_unit = lambda k: Unit("up", shards[6], fulls[6], 0, k * UNIT_COLS)
+    down_unit = lambda k: Unit("down", shards[7], fulls[7], 2 * k * UNIT_ROWS, 0, 2 * UNIT_ROWS)
+    order = ["key", "value", "query", "out", "qkv0", "qkv1", "qkv2", "self", "up0", "up1", "down0", "down1"]
+    made = {"query": plain(0, 0), "key": plain(1, 0), "value": plain(2, 0), "out": plain(3, 0), "self": plain(5, 0)}
+    made.update({f"qkv{k}": plain(4, k) for k in range(3)})
+    made.update({f"up{k}": up_unit(k) for k in range(2)})
+    made.update({f"down{k}": down_unit(k) for k in range(2)})
+    gather = Gather(me, [made[name] for name in order], gather_sems)
+    scatter_units = [("down", grads_out[7], 2 * k * UNIT_ROWS, 0) for k in range(2)]
+    scatter_units += [("up", grads_out[6], 0, k * UNIT_COLS) for k in range(2)]
+    scatter_units += [("all", grads_out[5], 0, 0)] + [("all", grads_out[4], 0, k * UNIT_COLS) for k in range(3)]
+    scatter_units += [("all", grads_out[i], 0, 0) for i in (3, 2, 1, 0)]
     scatter = Scatter(me, scatter_units, (part, r1, r2, rz), scatter_sems)
     pushed = [0]
     tick = [0]
@@ -652,7 +725,7 @@
     ready = []
 
     def tick_ready(t):
-        return 13 + 3.7 * min(t, 6) + 7.35 * max(0, t - 6)
+        return 17 + 3.7 * min(t, 6) + 8.4 * min(max(0, t - 6), 8) + 11.5 * max(0, t - 14)
 
     def settle_ready(k):
         return ready[k] if k < len(ready) else ready[-1] + 4.0 * (k - len(ready) + 1)
@@ -681,7 +754,8 @@
             else:
                 break
 
-    def arrived(u):
+    def arrived(name):
+        u = order.index(name)
         while tick[0] < gather.ticks(1) and tick[0] <= u + Gather.STAGES - 1:
             next_tick()
 
@@ -696,26 +770,33 @@
     def load(k, src, dst):
         return pltpu.make_async_copy(src, dst, in_sem.at[k])
 
+    def across(k, src, dst):
+        return remote(src, dst, across_s.at[k], across_r.at[k], me.dev(x=1 - me.x))
+
+    mine, theirs = pl.ds(0, 256), pl.ds(256, 256)
+    loads = [load(0, latents.at[0], after_self), load(1, pixels.at[0], pix), load(2, cotangent.at[0], resid)]
+    own_gain = load(3, gain_block, gain_full.at[me.y, me.x, me.z, me.c])
+    own_gain.start()
+    loads[2].start()
     for u in range(len(gather.units)):
         gather.own(u).start()
-    loads = [load(0, latents.at[0], after_self), load(1, pixels.at[0], pix), load(2, cotangent.at[0], resid)]
-    for c in loads:
-        c.start()
-    own_gain = pltpu.make_async_copy(gain_block, gain_full.at[me.y, me.x, me.z, me.c], in_sem.at[3])
-    own_gain.start()
+    loads[0].start()
+    loads[1].start()
+    loads[2].wait()
+    for_each(8, lambda i: g_out.__setitem__((block(i, 32), slice(None)), resid[block(i, 32), :].astype(BF16)))
     own_gain.wait()
     gains = SmallGather(me, gain_full, sg_s, sg_r)
+    me.barrier()
     gains.run(0)
     gather.early(0)
     gather_to(1)
     for u in range(1, len(gather.units)):
         gather.early(u)
+    across(0, g_out.at[mine], g_out.at[theirs]).start()
     gains.run(1)
-    gather_to(2)
-    gains.run(2)
-    gather_to(3)
-    gains.run(3)
-    gains.run(4)
+    for s in range(2, 6):
+        gather_to(s)
+        gains.run(s)
     table = jnp.sum(gain_full[...].reshape(32, 8, 128), axis=1).astype(BF16)
     width = latents.shape[2]
     lane = lax.broadcasted_iota(jnp.int32, (128, width), 1)
@@ -818,25 +899,29 @@
 
         for_each(4, body)
 
-    def weight_grad(xt_at, rows, own, far, col0):
+    def partial_sums(us, body):
         u = pushed[0]
         settle_to(u - 3)
         if u >= PARTIALS:
             scatter.sent(u - PARTIALS)
-        slot = u % PARTIALS
-
-        def body(j):
-            cols = pl.ds(pl.multiple_of(col0 + j * 256, 256), 256)
-            total = matmul(xt_at(0), own[:, cols]) + matmul(xt_at(rows), far[:, cols])
-            part[slot, :, :, :, :, block(j, 256)] = total.astype(BF16).reshape(2, 2, 4, UNIT_ROWS, 256)
-
-        for_each(4, body)
+        body(u % PARTIALS)
         scatter.stage(0, u)
         pushed[0] += 1
-        clock[0] += 1.7 if rows > 256 else 1.2
-        gap = 7.35 if tick[0] >= gather.ticks(1) else 14.7
-        ready.append(max(clock[0] + 9, (ready[-1] if ready else 0) + gap))
+        clock[0] += us
+        lag, gap = (18, 10) if scatter.kind(u) == "all" else (24, 12)
+        ready.append(max(clock[0] + lag, (ready[-1] if ready else 0) + gap))
         spend(0)
+
+    def weight_grad(xt_at, rows, own, far, col0):
+        def fill(slot):
+            def body(j):
+                cols = pl.ds(pl.multiple_of(col0 + j * 256, 256), 256)
+                total = matmul(xt_at(0), own[:, cols]) + matmul(xt_at(rows), far[:, cols])
+                part[slot, :, :, :, :, block(j, 256)] = total.astype(BF16).reshape(2, 2, 4, UNIT_ROWS, 256)
+
+            for_each(4, body)
+
+        partial_sums(1.7 if rows > 256 else 1.2, fill)
 
     def xt_of(xt, rows):
         return lambda at: xt[:, :, :, :, pl.ds(at, rows)].reshape(512, rows)
@@ -851,22 +936,19 @@
     spend(3.3)
     transpose_out(2, big, 256, xt_pix, 512)
     count = counts[0]
-    loads[2].wait()
-    for_each(8, lambda i: g_out.__setitem__((block(i, 32), slice(None)), resid[block(i, 32), :].astype(BF16)))
-    swap(0, g_out, g_out_in).start()
-    arrived(0)
+    arrived("key")
     project(big, w_fetch(fulls[1], 0), store(keys))
     spend(3.3)
-    arrived(1)
+    arrived("value")
     project(big, w_fetch(fulls[2], 0), store(values))
     spend(3.3)
-    arrived(2)
+    arrived("query")
     project(tmp, w_fetch(fulls[0], 0), store(queries))
     spend(2.7)
     for half in range(2):
         attend_forward_heads(4 * half, 4, queries, 0, keys, 0, values, 0, tmp, count)
         spend(2.3)
-    arrived(3)
+    arrived("out")
     transpose_out(3, tmp, 0, xt_mixed, 256)
 
     def add_to(dst, src):
@@ -882,67 +964,82 @@
     transpose_out(4, tmp, 0, xt_nself, 256)
     spend(1.8)
     for k in range(3):
-        arrived(4 + k)
+        arrived(f"qkv{k}")
         project(tmp, w_fetch(fulls[4], k * UNIT_COLS), store(packed, k * UNIT_COLS))
         spend(2.7)
     for half in range(2):
         attend_forward_heads(4 * half, 4, packed, 0, packed, UNIT_COLS, packed, 2 * UNIT_COLS, tmp, None)
         spend(2.2)
-    arrived(7)
+    arrived("self")
     transpose_out(5, tmp, 0, xt_smixed, 256)
     project(tmp, w_fetch(fulls[5], 0), add_to(after_self, after_cross))
     spend(3)
 
-    ln_forward(after_self, gain[3], tmp)
-    transpose_out(6, tmp, 0, xt_nmlp, 256)
+    across(0, g_out.at[mine], g_out.at[theirs]).wait_recv()
+    swap(0, g_out, g_out_in).start()
+    ln_forward(after_self, gain[3], big.at[mine])
+    across(1, big.at[mine], big.at[theirs]).start()
+    transpose_out(6, big, 0, xt_nmlp, 512)
     spend(1.8)
+
+    def up_rows(slot, k, rows):
+        def up(j):
+            x = matmul(big[rows, :], w_cols(slot, j))
+            t = jnp.tanh(GELU_A * (x + GELU_B * (x * x * x)))
+            half = 0.5 * (1.0 + t)
+            cols = pl.ds(pl.multiple_of(k * UNIT_COLS + j * 256, 256), 256)
+            act[rows, cols] = (x * half).astype(BF16)
+            slope = half + (0.5 * GELU_A) * x * (1.0 - t * t) * (1.0 + (3 * GELU_B) * (x * x))
+            hid[rows, cols] = slope.astype(BF16)
+
+        for_each(4, up)
+
     a_staged = [None, None]
-
-    def act_out(k):
-        slot = k % 2
-        if a_staged[slot] is not None:
-            a_staged[slot][0].wait()
-            a_staged[slot][1].wait_send()
+    act_copies = []
+
+    def act_out(k, row0):
+        n = len(act_copies)
+        slot = n % 2
+        if n >= 2:
+            act_copies[n - 2][0].wait()
+            act_copies[n - 2][1].wait_send()
 
         def body(m):
-            st_a[slot, m // 2, m % 2] = act[:, pl.ds(pl.multiple_of(k * UNIT_COLS + m * 128, 128), 128)].T
+            st_a[slot, m // 2, m % 2] = act[pl.ds(row0, 256), pl.ds(pl.multiple_of(k * UNIT_COLS + m * 128, 128), 128)].T
 
         for_each(8, body)
-        a = pltpu.make_async_copy(st_a.at[slot, :, me.c], xt_act.at[k // 2, k % 2, :, :, pl.ds(0, 256)], xl.at[7 + k])
+        a = pltpu.make_async_copy(st_a.at[slot, :, me.c], xt_act.at[k, :, :, pl.ds(row0, 256)], xl.at[8 + n])
         b = remote(
             st_a.at[slot, :, 1 - me.c],
-            xt_act.at[k // 2, k % 2, :, :, pl.ds(256, 256)],
-            xs.at[7 + k],
-            xr.at[7 + k],
+            xt_act.at[k, :, :, pl.ds(512 + row0, 256)],
+            xs.at[8 + n],
+            xr.at[8 + n],
             me.dev(c=1 - me.c),
         )
         a.start()
         b.start()
-        a_staged[slot] = (a, b)
-        return a, b
-
-    act_copies = []
-    for k in range(4):
-        arrived(8 + k)
-        slot = w_fetch(fulls[6], k * UNIT_COLS)
-
-        def up(j):
-            x = matmul(tmp[...], w_cols(slot, j))
-            t = jnp.tanh(GELU_A * (x + GELU_B * (x * x * x)))
-            half = 0.5 * (1.0 + t)
-            cols = pl.ds(pl.multiple_of(k * UNIT_COLS + j * 256, 256), 256)
-            act[:, cols] = (x * half).astype(BF16)
-            slope = half + (0.5 * GELU_A) * x * (1.0 - t * t) * (1.0 + (3 * GELU_B) * (x * x))
-            hid[:, cols] = slope.astype(BF16)
-
-        for_each(4, up)
-        act_copies.append(act_out(k))
-        spend(3.2)
-    for k in range(2, 4):
-        a_staged[k % 2][0].wait()
-        a_staged[k % 2][1].wait_send()
-    for k in range(4):
-        act_copies[k][1].wait_recv()
+        act_copies.append((a, b))
+
+    up_slots = []
+    for k in range(2):
+        arrived(f"up{k}")
+        up_slots.append(w_fetch(fulls[6], k * UNIT_COLS))
+        up_rows(up_slots[k], k, mine)
+        spend(2.8)
+        act_out(k, 0)
+        spend(0.5)
+    across(1, big.at[mine], big.at[theirs]).wait_recv()
+    for k in range(2):
+        up_rows(up_slots[k], k, theirs)
+        spend(1.3)
+        act_out(k, 256)
+        spend(0.5)
+    transpose_out(7, big, 256, xt_nmlp, 512)
+    for a, b in act_copies[2:]:
+        a.wait()
+        b.wait_send()
+    for _, b in act_copies:
+        b.wait_recv()
     for slot in range(2):
         clear(slot)
     spend(2)
@@ -950,28 +1047,33 @@
     swap(0, g_out, g_out_in).wait_recv()
 
     def down_grad(k):
-        def xt_down(at):
-            return xt_act[:, :, :, pl.ds(k * UNIT_ROWS, UNIT_ROWS), pl.ds(at, 256)].reshape(512, 256)
-
-        weight_grad(xt_down, 256, g_out, g_out_in, 0)
+        def fill(slot):
+            def body(i):
+                r, cols = i // 4, block(i % 4, 256)
+                rows = pl.ds(pl.multiple_of((2 * k + r) * UNIT_ROWS, UNIT_ROWS), UNIT_ROWS)
+                near = xt_act[:, :, rows, pl.ds(0, 512)].reshape(256, 512)
+                far = xt_act[:, :, rows, pl.ds(512, 512)].reshape(256, 512)
+                total = matmul(near, g_out[:, cols]) + matmul(far, g_out_in[:, cols])
+                part[slot, :, r, :, :, cols] = total.astype(BF16).reshape(2, 4, UNIT_ROWS, 256)
+
+            for_each(8, body)
+
+        partial_sums(2, fill)
 
     down_grad(0)
-    arrived(13)
-    down_grad(1)
-    arrived(15)
+    arrived("down1")
 
     wd_turn = [0]
 
     def wd_start(q):
         slot = wd_turn[0] % 2
         wd_turn[0] += 1
-        c = pltpu.make_async_copy(fulls[7].at[q // 2, q % 2], wd_buf.at[slot], wd_sem.at[slot])
+        c = pltpu.make_async_copy(fulls[7].at[q], wd_buf.at[slot], wd_sem.at[slot])
         c.start()
         return slot, c
 
-    pending = w_start(fulls[6], 0)
-    wd = [wd_start(0), wd_start(1), None, None]
-    for q in range(4):
+    wd = [wd_start(0), wd_start(1)]
+    for q in range(2):
         slot, c = wd[q]
         c.wait()
 
@@ -984,22 +1086,30 @@
         for_each(4, hidden_back)
         cols = pl.ds(q * UNIT_COLS, UNIT_COLS)
         swap(1 + q, hid.at[:, cols], hid_in.at[:, cols]).start()
-        spend(1.5)
-        if q < 2:
-            wd[q + 2] = wd_start(q + 2)
-            down_grad(2 + q)
-    xt_wait(6, xt_nmlp, 0, 256)
-    wd = [wd_start(0), wd_start(1), None, None]
-    for k in range(4):
-        slot, c = pending
-        c.wait()
-        if k < 3:
-            pending = w_start(fulls[6], (k + 1) * UNIT_COLS)
-        back(hid, k * UNIT_COLS, slot, acc.at[1], k == 0)
-        spend(1.4)
+        spend(2)
+    for k in range(2):
+        back(hid.at[theirs], k * UNIT_COLS, up_slots[k], acc.at[0], k == 0)
+        spend(1.3)
+    across(1, big.at[mine], big.at[theirs]).wait_send()
+    for_each(8, lambda i: big.__setitem__((block(i, 32), slice(None)), acc[0, block(i, 32), :].astype(BF16)))
+    across(2, big.at[mine], tmp).start()
+    down_grad(1)
+    for k in range(2):
+        back(hid.at[mine], k * UNIT_COLS, up_slots[k], acc.at[1], k == 0)
+        spend(1.3)
+    xt_wait(6, xt_nmlp, 0, 512)
+    xt_wait(7, xt_nmlp, 256, 512)
+    for k in range(2):
         cols = pl.ds(k * UNIT_COLS, UNIT_COLS)
         swap(1 + k, hid.at[:, cols], hid_in.at[:, cols]).wait_recv()
-        weight_grad(xt_of(xt_nmlp, 256), 256, hid, hid_in, k * UNIT_COLS)
+        weight_grad(xt_of(xt_nmlp, 512), 512, hid, hid_in, k * UNIT_COLS)
+    across(2, big.at[mine], tmp).wait_recv()
+
+    def add_theirs(i):
+        rows = block(i, 32)
+        acc[1, rows, :] = acc[1, rows, :] + tmp[rows, :].astype(F32)
+
+    for_each(8, add_theirs)
     so_slot, c_so = w_start(fulls[5], 0)
     ln_backward(after_self, 0, gain[3], acc.at[1], resid, gain_acc.at[3])
     spend(2.3)
@@ -1008,79 +1118,53 @@
         for_each(8, lambda i: dst.__setitem__((block(i, 32), slice(None)), resid[block(i, 32), :].astype(BF16)))
 
     round_rows(g_branch)
-    swap(5, g_branch, g_branch_in).start()
+    swap(3, g_branch, g_branch_in).start()
     c_so.wait()
     qkv_w = w_start(fulls[4], 0)
     back(g_branch, 0, so_slot, tmp, True)
     spend(1.8)
-    swap(5, g_branch, g_branch_in).wait_recv()
+    swap(3, g_branch, g_branch_in).wait_recv()
     xt_wait(5, xt_smixed, 0, 256)
     weight_grad(xt_of(xt_smixed, 256), 256, g_branch, g_branch_in, 0)
-    for q in range(4):
+    for q in range(2):
         cols = pl.ds(q * UNIT_COLS, UNIT_COLS)
         swap(1 + q, hid.at[:, cols], hid_in.at[:, cols]).wait_send()
+    corner = [hid.at[mine, pl.ds(0, UNIT_COLS)], hid.at[mine, pl.ds(UNIT_COLS, UNIT_COLS)], hid.at[theirs, pl.ds(0, UNIT_COLS)]]
     for half in range(2):
         attend_backward_heads(
             4 * half, 4, packed, 0, packed, UNIT_COLS, packed, 2 * UNIT_COLS, tmp, None,
-            hid, 0, hid, UNIT_COLS, hid, 2 * UNIT_COLS,
+            corner[0], 0, corner[1], 0, corner[2], 0,
         )
         spend(3.4)
-    packed_grad = hid.at[:, pl.ds(0, 3 * UNIT_COLS)]
-    swap(6, packed_grad, packed_in).start()
+    packed_swaps = [swap(4 + k, corner[k], packed_in.at[k]) for k in range(3)]
+    for c in packed_swaps:
+        c.start()
     for k in range(3):
         slot, c = qkv_w
         c.wait()
         if k < 2:
             qkv_w = w_start(fulls[4], (k + 1) * UNIT_COLS)
-        back(hid, k * UNIT_COLS, slot, acc.at[0], k == 0)
+        back(corner[k], 0, slot, acc.at[0], k == 0)
         spend(1.3)
+        packed_swaps[k].wait_recv()
         if k == 0:
-            swap(6, packed_grad, packed_in).wait_recv()
             xt_wait(4, xt_nself, 0, 256)
-        weight_grad(xt_of(xt_nself, 256), 256, hid, packed_in, k * UNIT_COLS)
+        weight_grad(xt_of(xt_nself, 256), 256, corner[k], packed_in.at[k], 0)
     wo_slot, c_wo = w_start(fulls[3], 0)
     ln_backward(after_cross, 0, gain[2], acc.at[0], resid, gain_acc.at[2])
     spend(2.3)
 
-    round_rows(g_cross)
-    swap(7, g_cross, g_cross_in).start()
+    swap(3, g_branch, g_branch_in).wait_send()
+    round_rows(g_branch)
+    swap(7, g_branch, g_branch_in).start()
     c_wo.wait()
-    back(g_cross, 0, wo_slot, tmp, True)
+    back(g_branch, 0, wo_slot, tmp, True)
     spend(1.8)
-    swap(7, g_cross, g_cross_in).wait_recv()
+    swap(7, g_branch, g_branch_in).wait_recv()
     xt_wait(3, xt_mixed, 0, 256)
-    weight_grad(xt_of(xt_mixed, 256), 256, g_cross, g_cross_in, 0)
-
-    for q in range(4):
-        slot, c = wd[q]
-        c.wait()
-
-        def down(j):
-            w = wd_buf[slot, :, :, :, block(j, 256)].reshape(UNIT_COLS, 256)
-            tile = matmul(act[:, pl.ds(q * UNIT_COLS, UNIT_COLS)], w)
-            dst = block(j, 256)
-            acc[0, :, dst] = (after_self[:, dst] if q == 0 else acc[0, :, dst]) + tile
-
-        for_each(4, down)
-        if q < 2:
-            wd[q + 2] = wd_start(q + 2)
-        spend(1.3)
-    again = load(0, latents.at[0], after_self)
-    again.start()
-    out_copy = pltpu.make_async_copy(acc.at[0], latents_out.at[0], out_sem.at[0])
-    out_copy.start()
-    small[...] = jnp.zeros_like(small)
-
-    def square(i, total):
-        v = acc[0, block(i, 8), :]
-        return total + v * v
-
-    squares = lax.fori_loop(0, 32, square, jnp.zeros((8, width), F32))
-    mean_square = jnp.sum(jnp.sum(squares, axis=1, keepdims=True), axis=0, keepdims=True) / (latents.shape[1] * width)
-    root_mean = jnp.sqrt(mean_square)
-    small[4:5, :] = jnp.broadcast_to(root_mean, (1, width))
-    spend(1)
-
+    weight_grad(xt_of(xt_mixed, 256), 256, g_branch, g_branch_in, 0)
+
+    across(2, big.at[mine], tmp).wait_send()
     for half in range(2):
         attend_backward_heads(4 * half, 4, queries, 0, keys, 0, values, 0, tmp, count, dq, 0, big, 0, dv, 0)
         spend(3.2)
@@ -1098,7 +1182,24 @@
     xt_wait(0, xt_normed, 0, 256)
     given[2].wait_recv()
     weight_grad(xt_of(xt_normed, 256), 256, dq, dq_in, 0)
-    out_copy.wait()
+    def down(rows, slot, q, dst, base):
+        def body(j):
+            w = wd_buf[slot, :, :, :, block(j, 256)].reshape(UNIT_COLS, 256)
+            tile = matmul(act[rows, pl.ds(q * UNIT_COLS, UNIT_COLS)], w)
+            cols = block(j, 256)
+            if base is None:
+                dst[:, cols] = tile
+            else:
+                dst[:, cols] = base[:, cols] + tile
+
+        for_each(4, body)
+        spend(1.3)
+
+    outer = hid.at[theirs, pl.ds(UNIT_COLS, UNIT_COLS)]
+    down(theirs, wd[0][0], 0, after_cross, None)
+    down(theirs, wd[1][0], 1, after_cross, after_cross)
+    for_each(8, lambda i: tmp.__setitem__((block(i, 32), slice(None)), after_cross[block(i, 32), :].astype(BF16)))
+    across(3, tmp, outer).start()
     w_v[1].wait()
     for r in range(2):
         back(dv.at[pl.ds(256 * r, 256)], 0, w_v[0], acc.at[r], True)
@@ -1114,11 +1215,33 @@
         c.start()
         pix_copies.append(c)
         spend(2.3)
+    down(mine, wd[0][0], 0, after_cross, after_self)
+    down(mine, wd[1][0], 1, after_cross, after_cross)
+    again = load(0, latents.at[0], after_self)
+    again.start()
+    across(3, tmp, outer).wait_recv()
+    small[...] = jnp.zeros_like(small)
+
+    def add_output(i, total):
+        rows = block(i, 32)
+        v = after_cross[rows, :] + outer[rows, :].astype(F32)
+        after_cross[rows, :] = v
+        v = v * v
+        return total + v[0:8] + v[8:16] + v[16:24] + v[24:32]
+
+    squares = lax.fori_loop(0, 8, add_output, jnp.zeros((8, width), F32))
+    out_copy = pltpu.make_async_copy(after_cross, latents_out.at[0], out_sem.at[0])
+    out_copy.start()
+    mean_square = jnp.sum(jnp.sum(squares, axis=1, keepdims=True), axis=0, keepdims=True) / (latents.shape[1] * width)
+    root_mean = jnp.sqrt(mean_square)
+    small[4:5, :] = jnp.broadcast_to(root_mean, (1, width))
+    spend(1)
+    pix_copies[0].wait()
     w_q[1].wait()
-    back(dq, 0, w_q[0], after_cross, True)
+    back(dq, 0, w_q[0], acc.at[0], True)
     spend(1.3)
     again.wait()
-    ln_backward(after_self, 0, gain[0], after_cross, resid, gain_acc.at[0])
+    ln_backward(after_self, 0, gain[0], acc.at[0], resid, gain_acc.at[0])
     grad_copy = pltpu.make_async_copy(resid, latents_grad.at[0], out_sem.at[1])
     grad_copy.start()
     spend(2.3)
@@ -1139,14 +1262,16 @@
     for u in range(len(scatter_units) - PARTIALS, len(scatter_units)):
         scatter.sent(u)
     swap(0, g_out, g_out_in).wait_send()
-    swap(5, g_branch, g_branch_in).wait_send()
-    swap(6, packed_grad, packed_in).wait_send()
-    swap(7, g_cross, g_cross_in).wait_send()
+    across(0, g_out.at[mine], g_out.at[theirs]).wait_send()
+    for c in packed_swaps:
+        c.wait_send()
+    swap(7, g_branch, g_branch_in).wait_send()
     for c in given:
         c.wait_send()
     grad_copy.wait()
-    for c in pix_copies:
-        c.wait()
+    pix_copies[1].wait()
+    out_copy.wait()
+    across(3, tmp, outer).wait_send()
 
 
 def mega(latents, pixels, counts, cotangent, gain_block, shards):
@@ -1160,22 +1285,22 @@
         vm((2, 4, 2, 128, UNIT_COLS), BF16),
         vm((PARTIALS, 2, 2, 4, UNIT_ROWS, UNIT_COLS), BF16),
         vm((PARTIALS, 2, 4, UNIT_ROWS, UNIT_COLS), BF16),
-        vm((RING, 4, UNIT_ROWS, UNIT_COLS), BF16),
+        vm((RING + 2, 4, UNIT_ROWS, UNIT_COLS), BF16),
         vm((RING, 4, 2, UNIT_ROWS, UNIT_COLS), BF16),
-        xt(2 * rows), xt(2 * slots), xt(2 * rows), xt(2 * rows), xt(2 * rows), xt(2 * rows),
-        vm((2, 2, 4, 128, 2 * rows), BF16),
+        xt(2 * rows), xt(2 * slots), xt(2 * rows), xt(2 * rows), xt(2 * rows), xt(4 * rows),
+        vm((2, 4, 128, 4 * rows), BF16),
         vm((2, 4, 2, 128, rows), BF16),
         vm((2, 2, 2, 4, 2, UNIT_ROWS, 256), BF16),
-        wide(width), wide(width), wide(hidden), wide(hidden), wide(width), wide(width), wide(hidden), wide(3 * width),
-        wide(width), wide(width),
+        vm((2 * rows, width), BF16), vm((2 * rows, width), BF16), vm((2 * rows, hidden // 2), BF16), vm((2 * rows, hidden // 2), BF16),
+        wide(width), wide(width), vm((2 * rows, hidden // 2), BF16), vm((3, rows, width), BF16),
         wide(width), wide(width), vm((slots, width), BF16), vm((slots, width), BF16), vm((slots, width), BF16), vm((slots, width), BF16),
         wide(width), vm((slots, width), BF16), vm((slots, width), BF16), wide(3 * width),
         vm((rows, width), F32), vm((rows, width), F32), vm((rows, width), F32), vm((slots, width), BF16), wide(width), vm((2, rows, width), F32),
         vm((2, 2, 4, 2, 8, 128), F32), vm((8, width), F32), vm((4, 8, width), F32), vm((8, width), F32), vm((5, 8, width), F32),
     ]
-    sems = Gather.sems(16) + Scatter.sems(16)
+    sems = Gather.sems(12) + Scatter.sems(12)
     sems += [DMA((2,)), DMA((2,)), DMA((4,)), DMA((4,)), DMA((7,)), DMA((7,)), DMA((5,)), DMA((5,))]
-    sems += [DMA((11,))] * 3 + [DMA((11,))] * 2
+    sems += [DMA((12,))] * 3 + [DMA((11,))] * 2 + [DMA((4,))] * 2
     outs = [
         jax.ShapeDtypeStruct(latents.shape, F32),
         jax.ShapeDtypeStruct(latents.shape, F32),
@@ -1183,7 +1308,9 @@
         jax.ShapeDtypeStruct((8, width), F32),
     ]
     outs += [jax.ShapeDtypeStruct(s.shape, F32) for s in shards]
-    outs += [jax.ShapeDtypeStruct((2, 2, 4, 2) + s.shape, s.dtype) for s in shards]
+    outs += [jax.ShapeDtypeStruct((2, 2, 4, 2) + s.shape, s.dtype) for s in shards[:6]]
+    outs.append(jax.ShapeDtypeStruct((2, 2, 4, 2, shards[6].shape[0], hidden // 2), BF16))
+    outs.append(jax.ShapeDtypeStruct((2, 4, 2) + shards[7].shape, BF16))
     hbm, vmem = pl.BlockSpec(memory_space=pl.ANY), pl.BlockSpec(memory_space=pltpu.VMEM)
     smem = pl.BlockSpec(memory_space=pltpu.SMEM)
     results = pl.pallas_call(

time: 331 us -> 302 us (0.912)
  Pallas kernels: 324 us -> 295 us
    pallas_call x1, Pallas kernels: 318 us -> 290 us  [mega(): pl.pallas_call(mega_kernel, out_shape=outs, in_specs=[hbm, hbm, smem, hbm...]
where the time goes in v4:
time: 302 us; the launch traced here: 301 us
  Pallas kernels  295 us (98%)
  between operations  3.78 us (1%)
    pallas_call x1, Pallas kernels, mega(): pl.pallas_call(mega_kernel, out_shape=outs, in_specs=[hbm, hbm, smem, hbm...  290 us

profile of v4, /device:TPU:0, one launch (start us, length us, event | category | flops | bytes accessed | tf_op | source)
XLA Modules:
  0.0 301.2 jit_solution(2870608055896803761)
XLA Ops:
  0.6 1.4 fusion.7.refs_4_
  2.7 289.6 %shard_map.279 = (f32[1,256,1024]{2,1,0:T(8,128)}, f32[1,256,1024]{2,1,0:T(8,128)}, f32[1,512,1024]{2,1,0:T(8,128)}, f32[8,1024]{1,0:T(8,128)}, f32[32,1024]{1,0...) custom-call(f32[1,256,1024]{2,1,0:T(8,128)} %refs_0_.1, ...), custom_call_target="tpu_custom_call" | custom-call | tf_op jit(solution)/shard_map/pallas_call | solution.py:1316
  292.3 0.0 copy-start
  292.3 5.3 %shard_map.280 = (f32[1,256,1024]{2,1,0:T(8,128)}, f32[1,256,1024]{2,1,0:T(8,128)}, f32[1,512,1024]{2,1,0:T(8,128)}, f32[32,1024]{1,0:T(8,128)}, f32[32,1024]{1,...) custom-call(f32[1,256,1024]{2,1,0:T(8,128)} %get-tuple-element.39.re, ...), custom_call_target="tpu_custom_call" | custom-call | tf_op jit(solution)/shard_map/pallas_call | solution.py:1640
  297.6 0.0 copy-done
  297.7 0.1 constant_dynamic-slice_fusion
  297.7 0.5 slice_bitcast_fusion
  298.3 0.5 fusion.8
  (1 shorter events, 0.0 us)
Async XLA Ops:
  292.3 5.4 %copy-start = (f32[8,1024]{1,0:T(8,128)S(1)}, f32[8,1024]{1,0:T(8,128)}, u32[]{:S(2)}) copy-start(f32[8,1024]{1,0:T(8,128)} %get-tuple-element.53) | copy-start | bytes 98308

commit v5 on v4

--- a/solution.py
+++ b/solution.py
@@ -792,7 +792,6 @@
     gather_to(1)
     for u in range(1, len(gather.units)):
         gather.early(u)
-    across(0, g_out.at[mine], g_out.at[theirs]).start()
     gains.run(1)
     for s in range(2, 6):
         gather_to(s)
@@ -908,7 +907,7 @@
         scatter.stage(0, u)
         pushed[0] += 1
         clock[0] += us
-        lag, gap = (18, 10) if scatter.kind(u) == "all" else (24, 12)
+        lag, gap = (14, 9) if scatter.kind(u) == "all" else (20, 11.5)
         ready.append(max(clock[0] + lag, (ready[-1] if ready else 0) + gap))
         spend(0)
 
@@ -975,10 +974,9 @@
     project(tmp, w_fetch(fulls[5], 0), add_to(after_self, after_cross))
     spend(3)
 
-    across(0, g_out.at[mine], g_out.at[theirs]).wait_recv()
-    swap(0, g_out, g_out_in).start()
     ln_forward(after_self, gain[3], big.at[mine])
     across(1, big.at[mine], big.at[theirs]).start()
+    across(0, g_out.at[mine], g_out.at[theirs]).start()
     transpose_out(6, big, 0, xt_nmlp, 512)
     spend(1.8)
 
@@ -1034,6 +1032,8 @@
         spend(1.3)
         act_out(k, 256)
         spend(0.5)
+    across(0, g_out.at[mine], g_out.at[theirs]).wait_recv()
+    swap(0, g_out, g_out_in).start()
     transpose_out(7, big, 256, xt_nmlp, 512)
     for a, b in act_copies[2:]:
         a.wait()

time: 302 us -> 297 us (0.983)
  Pallas kernels: 295 us -> 290 us
    pallas_call x1, Pallas kernels: 290 us -> 284 us  [mega(): pl.pallas_call(mega_kernel, out_shape=outs, in_specs=[hbm, hbm, smem, hbm...]
where the time goes in v5:
time: 297 us; the launch traced here: 296 us
  Pallas kernels  290 us (98%)
  between operations  3.78 us (1%)
    pallas_call x1, Pallas kernels, mega(): pl.pallas_call(mega_kernel, out_shape=outs, in_specs=[hbm, hbm, smem, hbm...  284 us

profile of v5, /device:TPU:0, one launch (start us, length us, event | category | flops | bytes accessed | tf_op | source)
XLA Modules:
  0.0 296.0 jit_solution(8284846740242189118)
XLA Ops:
  0.6 1.4 fusion.7.refs_4_
  2.7 284.4 %shard_map.279 = (f32[1,256,1024]{2,1,0:T(8,128)}, f32[1,256,1024]{2,1,0:T(8,128)}, f32[1,512,1024]{2,1,0:T(8,128)}, f32[8,1024]{1,0:T(8,128)}, f32[32,1024]{1,0...) custom-call(f32[1,256,1024]{2,1,0:T(8,128)} %refs_0_.1, ...), custom_call_target="tpu_custom_call" | custom-call | tf_op jit(solution)/shard_map/pallas_call | solution.py:1316
  287.1 0.0 copy-start
  287.1 5.3 %shard_map.280 = (f32[1,256,1024]{2,1,0:T(8,128)}, f32[1,256,1024]{2,1,0:T(8,128)}, f32[1,512,1024]{2,1,0:T(8,128)}, f32[32,1024]{1,0:T(8,128)}, f32[32,1024]{1,...) custom-call(f32[1,256,1024]{2,1,0:T(8,128)} %get-tuple-element.39.re, ...), custom_call_target="tpu_custom_call" | custom-call | tf_op jit(solution)/shard_map/pallas_call | solution.py:1640
  292.4 0.0 copy-done
  292.5 0.1 constant_dynamic-slice_fusion
  292.5 0.5 slice_bitcast_fusion
  293.1 0.5 fusion.8
  (1 shorter events, 0.0 us)
Async XLA Ops:
  287.1 5.4 %copy-start = (f32[8,1024]{1,0:T(8,128)S(1)}, f32[8,1024]{1,0:T(8,128)}, u32[]{:S(2)}) copy-start(f32[8,1024]{1,0:T(8,128)} %get-tuple-element.53) | copy-start | bytes 98308

commit v6 on v5

--- a/solution.py
+++ b/solution.py
@@ -1087,12 +1087,23 @@
         cols = pl.ds(q * UNIT_COLS, UNIT_COLS)
         swap(1 + q, hid.at[:, cols], hid_in.at[:, cols]).start()
         spend(2)
-    for k in range(2):
-        back(hid.at[theirs], k * UNIT_COLS, up_slots[k], acc.at[0], k == 0)
+    across(1, big.at[mine], big.at[theirs]).wait_send()
+    sides = [pl.ds(0, UNIT_COLS // 2), pl.ds(UNIT_COLS // 2, UNIT_COLS // 2)]
+    sums = [across(k, big.at[mine, cols], tmp.at[:, cols]) for k, cols in zip((2, 4), sides)]
+
+    def sums_for(side):
+        def body(i):
+            j = 2 * side + i
+            tile = matmul_nt(hid[theirs, pl.ds(0, UNIT_COLS)], w_rows(up_slots[0], j))
+            tile = tile + matmul_nt(hid[theirs, pl.ds(UNIT_COLS, UNIT_COLS)], w_rows(up_slots[1], j))
+            big[mine, block(j, 256)] = tile.astype(BF16)
+
+        for_each(2, body)
+        sums[side].start()
         spend(1.3)
-    across(1, big.at[mine], big.at[theirs]).wait_send()
-    for_each(8, lambda i: big.__setitem__((block(i, 32), slice(None)), acc[0, block(i, 32), :].astype(BF16)))
-    across(2, big.at[mine], tmp).start()
+
+    sums_for(0)
+    sums_for(1)
     down_grad(1)
     for k in range(2):
         back(hid.at[mine], k * UNIT_COLS, up_slots[k], acc.at[1], k == 0)
@@ -1103,7 +1114,8 @@
         cols = pl.ds(k * UNIT_COLS, UNIT_COLS)
         swap(1 + k, hid.at[:, cols], hid_in.at[:, cols]).wait_recv()
         weight_grad(xt_of(xt_nmlp, 512), 512, hid, hid_in, k * UNIT_COLS)
-    across(2, big.at[mine], tmp).wait_recv()
+    for c in sums:
+        c.wait_recv()
 
     def add_theirs(i):
         rows = block(i, 32)
@@ -1164,7 +1176,8 @@
     xt_wait(3, xt_mixed, 0, 256)
     weight_grad(xt_of(xt_mixed, 256), 256, g_branch, g_branch_in, 0)
 
-    across(2, big.at[mine], tmp).wait_send()
+    for c in sums:
+        c.wait_send()
     for half in range(2):
         attend_backward_heads(4 * half, 4, queries, 0, keys, 0, values, 0, tmp, count, dq, 0, big, 0, dv, 0)
         spend(3.2)
@@ -1300,7 +1313,7 @@
     ]
     sems = Gather.sems(12) + Scatter.sems(12)
     sems += [DMA((2,)), DMA((2,)), DMA((4,)), DMA((4,)), DMA((7,)), DMA((7,)), DMA((5,)), DMA((5,))]
-    sems += [DMA((12,))] * 3 + [DMA((11,))] * 2 + [DMA((4,))] * 2
+    sems += [DMA((12,))] * 3 + [DMA((11,))] * 2 + [DMA((5,))] * 2
     outs = [
         jax.ShapeDtypeStruct(latents.shape, F32),
         jax.ShapeDtypeStruct(latents.shape, F32),

time: 297 us -> 295 us (level)
  no operation moved by 1% of the time
where the time goes in v6:
time: 295 us; the launch traced here: 294 us
  Pallas kernels  288 us (98%)
  between operations  3.78 us (1%)
    pallas_call x1, Pallas kernels, mega(): pl.pallas_call(mega_kernel, out_shape=outs, in_specs=[hbm, hbm, smem, hbm...  283 us

profile of v6, /device:TPU:0, one launch (start us, length us, event | category | flops | bytes accessed | tf_op | source)
XLA Modules:
  0.0 294.2 jit_solution(10214618002912476327)
XLA Ops:
  0.6 1.4 fusion.7.refs_4_
  2.7 282.5 %shard_map.279 = (f32[1,256,1024]{2,1,0:T(8,128)}, f32[1,256,1024]{2,1,0:T(8,128)}, f32[1,512,1024]{2,1,0:T(8,128)}, f32[8,1024]{1,0:T(8,128)}, f32[32,1024]{1,0...) custom-call(f32[1,256,1024]{2,1,0:T(8,128)} %refs_0_.1, ...), custom_call_target="tpu_custom_call" | custom-call | tf_op jit(solution)/shard_map/pallas_call | solution.py:1329
  285.2 0.0 copy-start
  285.2 5.3 %shard_map.280 = (f32[1,256,1024]{2,1,0:T(8,128)}, f32[1,256,1024]{2,1,0:T(8,128)}, f32[1,512,1024]{2,1,0:T(8,128)}, f32[32,1024]{1,0:T(8,128)}, f32[32,1024]{1,...) custom-call(f32[1,256,1024]{2,1,0:T(8,128)} %get-tuple-element.39.re, ...), custom_call_target="tpu_custom_call" | custom-call | tf_op jit(solution)/shard_map/pallas_call | solution.py:1653
  290.6 0.0 copy-done
  290.6 0.1 constant_dynamic-slice_fusion
  290.7 0.5 slice_bitcast_fusion
  291.2 0.5 fusion.8
  (1 shorter events, 0.0 us)
Async XLA Ops:
  285.2 5.4 %copy-start = (f32[8,1024]{1,0:T(8,128)S(1)}, f32[8,1024]{1,0:T(8,128)}, u32[]{:S(2)}) copy-start(f32[8,1024]{1,0:T(8,128)} %get-tuple-element.53) | copy-start | bytes 98308
